TPU v7x, 128 devices: a whole 4x4x4 slice. The times are simulated.
128 devices in a mesh: gx: 8 (over z, core), gy: 16 (over y, x).
Axes of the slice: x: 4, y: 4, z: 4, core: 2. Of those that a mesh axis runs over, the one named last changes fastest.
Arguments:
- right_side: float32 [3, 2, 16, 128, 1024], P(None, None, None, 'gy', 'gx'), may hold values from -14 to 14
- materials: int32 [16, 128, 1024], P(None, 'gy', 'gx'), may hold values from 0 to 7
- sigma_diag: float32 [3, 8], replicated, may hold values from 0.1 to 10
- sigma_off: float32 [3, 8], replicated, may hold values from -0.45 to 0.45
Outputs:
- solution: float32 [3, 2, 16, 128, 1024], P(None, None, None, 'gy', 'gx')
- hessenberg: float32 [3, 2], replicated
All inputs are finite; a program needn't handle non-finite values.
Results may differ from a plain program's by a relative error of at most 0.0001.
Values sent between devices are 32-bit elements; how exact they have to be, the bound alone decides.
No kernel may reach another device: no remote copies, remote signals or barrier semaphores. Data moves between devices by JAX's collectives and lax.ppermute only.
A program may use at most 128 MiB of HBM per device.

v0:
```python
import jax
import jax.numpy as jnp
from jax import lax
from jax.sharding import PartitionSpec as P

ITERS = 2


omega_shift = 2.0
edge_center = 4.0
node_center = 6.0
nodal_shift = 4.0
edge_first = 0.7
edge_second = 0.6
node_first = 0.8
node_second = 0.5
epsilon = 1e-06


def with_halo(value, sides, width):
    for axis, dim in sides:
        size, length = (lax.axis_size(axis), value.shape[dim])
        up = [(i, (i + 1) % size) for i in range(size)]
        down = [(j, i) for i, j in up]
        last = lax.slice_in_dim(value, length - width, length, axis=dim)
        first = lax.slice_in_dim(value, 0, width, axis=dim)
        before = lax.ppermute(last, axis, up)
        after = lax.ppermute(first, axis, down)
        value = jnp.concatenate([before, value, after], axis=dim)
    return value


def forward_depth(values):
    zero_layer = jnp.zeros_like(values[..., :1, :, :])
    return jnp.concatenate([values[..., 1:, :, :], zero_layer], axis=-3) - values


def backward_depth(values):
    zero_layer = jnp.zeros_like(values[..., :1, :, :])
    return jnp.concatenate([zero_layer, values[..., :-1, :, :]], axis=-3) - values


def lead_east(values):
    return values[..., :-1, 1:] - values[..., :-1, :-1]


def lead_north(values):
    return values[..., 1:, :-1] - values[..., :-1, :-1]


def trail_east(values):
    return values[..., 1:, :-1] - values[..., 1:, 1:]


def trail_north(values):
    return values[..., :-1, 1:] - values[..., 1:, 1:]


def trim_high(values):
    return values[..., :-1, :-1]


def trim_low(values):
    return values[..., 1:, 1:]


def interior(values):
    return values[..., 1:-1, 1:-1]


def edge_halo(values):
    return with_halo(values, (("gx", 4), ("gy", 3)), 1)


def node_halo(values):
    return with_halo(values, (("gx", 3), ("gy", 2)), 1)


def norm_of(values):
    return jnp.sqrt(lax.psum(jnp.sum(values * values), ("gx", "gy")) + epsilon)


def tensor_table(sigma_diag, sigma_off):
    along_east = sigma_diag[0]
    along_north = sigma_diag[1]
    along_depth = sigma_diag[2]
    return jnp.stack(
        [
            along_east,
            along_north,
            along_depth,
            sigma_off[0] * jnp.sqrt(along_east * along_north),
            sigma_off[1] * jnp.sqrt(along_east * along_depth),
            sigma_off[2] * jnp.sqrt(along_north * along_depth),
        ]
    )


def tensor_apply(tensor, values):
    along_one = values[0]
    along_two = values[1]
    along_three = values[2]
    return jnp.stack(
        [
            tensor[0][None] * along_one
            + tensor[3][None] * along_two
            + tensor[4][None] * along_three,
            tensor[3][None] * along_one
            + tensor[1][None] * along_two
            + tensor[5][None] * along_three,
            tensor[4][None] * along_one
            + tensor[5][None] * along_two
            + tensor[2][None] * along_three,
        ]
    )


def rotate_quarter(values):
    return jnp.stack([-values[:, 1], values[:, 0]], axis=1)


def curl_curl_wide(padded):
    edge_east = padded[0]
    edge_north = padded[1]
    edge_depth = padded[2]
    flux_east = lead_north(edge_depth) - forward_depth(trim_high(edge_north))
    flux_north = forward_depth(trim_high(edge_east)) - lead_east(edge_depth)
    flux_depth = lead_east(edge_north) - lead_north(edge_east)
    return jnp.stack(
        [
            trail_north(flux_depth) - backward_depth(trim_low(flux_north)),
            backward_depth(trim_low(flux_east)) - trail_east(flux_depth),
            trail_east(flux_north) - trail_north(flux_east),
        ]
    )


def apply_operator(values, tensor):
    return curl_curl_wide(edge_halo(values)) + omega_shift * rotate_quarter(
        tensor_apply(tensor, values)
    )


def edge_inverse(residual, tensor):
    shift_part = omega_shift * tensor[0:3][:, None]
    denominator = edge_center * edge_center + shift_part * shift_part
    real_part = (edge_center * residual[:, 0:1] + shift_part * residual[:, 1:2]) / denominator
    imag_part = (edge_center * residual[:, 1:2] - shift_part * residual[:, 0:1]) / denominator
    return jnp.concatenate([real_part, imag_part], axis=1)


def node_inverse(nodal_source, tensor):
    shift_part = nodal_shift * (tensor[0] + tensor[1] + tensor[2])
    denominator = node_center * node_center + shift_part * shift_part
    real_part = (node_center * nodal_source[0] + shift_part * nodal_source[1]) / denominator
    imag_part = (node_center * nodal_source[1] - shift_part * nodal_source[0]) / denominator
    return jnp.stack([real_part, imag_part])


def divergence_wide(padded):
    return (
        trail_east(trim_high(padded[0]))
        + trail_north(trim_high(padded[1]))
        + backward_depth(interior(padded[2]))
    )


def gradient_wide(padded):
    return jnp.stack(
        [trim_low(lead_east(padded)), trim_low(lead_north(padded)), forward_depth(interior(padded))]
    )


def nodal_operator_wide(padded, wide_tensor):
    slopes = jnp.stack([lead_east(padded), lead_north(padded), forward_depth(trim_high(padded))])
    fluxes = slopes + omega_shift * rotate_quarter(tensor_apply(wide_tensor, slopes))
    return trail_east(fluxes[0]) + trail_north(fluxes[1]) + backward_depth(trim_low(fluxes[2]))


def precondition(vector, edge_tensor, wide_tensor):
    first_pass = edge_first * edge_inverse(vector, edge_tensor)
    remainder = vector - apply_operator(first_pass, edge_tensor)
    correction = edge_inverse(remainder, edge_tensor)
    smoothed = first_pass + edge_second * correction
    leftover = remainder - edge_second * apply_operator(correction, edge_tensor)
    nodal_source = divergence_wide(edge_halo(leftover))
    coarse = node_first * node_inverse(nodal_source, edge_tensor)
    coarse = coarse + node_second * node_inverse(
        nodal_source - nodal_operator_wide(node_halo(coarse), wide_tensor), edge_tensor
    )
    lifted = gradient_wide(node_halo(coarse))
    return (smoothed + lifted, leftover, lifted)


def least_squares(hessenberg, initial_norm):
    gram_matrix = jnp.dot(hessenberg.T, hessenberg, precision=lax.Precision.HIGHEST)
    target = initial_norm * hessenberg[0]
    factor = jnp.linalg.cholesky(gram_matrix)
    extent = hessenberg.shape[1]
    middle = []
    for position in range(extent):
        partial_value = target[position]
        for earlier in range(position):
            partial_value = partial_value - factor[position, earlier] * middle[earlier]
        middle.append(partial_value / factor[position, position])
    weights = list(middle)
    for position in range(extent - 1, -1, -1):
        partial_value = middle[position]
        for later_index in range(position + 1, extent):
            partial_value = partial_value - factor[later_index, position] * weights[later_index]
        weights[position] = partial_value / factor[position, position]
    return weights


def expand_tensor(material_grid, material_table):
    cell_tensor = jnp.zeros((6,) + material_grid.shape, jnp.float32)
    for material in range(material_table.shape[1]):
        cell_tensor = jnp.where(
            (material_grid == material)[None],
            material_table[:, material][:, None, None, None],
            cell_tensor,
        )
    return cell_tensor


def on_device(right_side, materials, sigma_diag, sigma_off):
    material_table = tensor_table(sigma_diag, sigma_off)
    material_grid = with_halo(materials, (("gx", 2), ("gy", 1)), 1)
    cell_tensor = expand_tensor(material_grid, material_table)
    wide_tensor = 0.25 * (
        cell_tensor[..., :-1, :-1]
        + cell_tensor[..., :-1, 1:]
        + cell_tensor[..., 1:, :-1]
        + cell_tensor[..., 1:, 1:]
    )
    edge_tensor = trim_low(wide_tensor)
    initial_norm = norm_of(right_side)
    krylov = [right_side / initial_norm]
    updates = []
    hessenberg = jnp.zeros((ITERS + 1, ITERS), jnp.float32)
    for column in range(ITERS):
        vector = krylov[column]
        update, leftover, lifted = precondition(vector, edge_tensor, wide_tensor)
        applied = apply_operator(update, edge_tensor)
        updates.append(update)
        for earlier in range(column + 1):
            factor_value = lax.psum(jnp.sum(krylov[earlier] * applied), ("gx", "gy"))
            applied = applied - factor_value * krylov[earlier]
            hessenberg = hessenberg.at[earlier, column].set(factor_value)
        height = norm_of(applied)
        hessenberg = hessenberg.at[column + 1, column].set(height)
        if column + 1 < ITERS:
            krylov.append(applied / height)
    weights = least_squares(hessenberg, initial_norm)
    solution = weights[0] * updates[0]
    column = 1
    solution = solution + weights[column] * updates[column]
    return (solution, hessenberg)


def solution(mesh):
    return jax.shard_map(
        on_device,
        mesh=mesh,
        in_specs=(P(None, None, None, "gy", "gx"), P(None, "gy", "gx"), P(), P()),
        out_specs=(P(None, None, None, "gy", "gx"), P()),
        check_vma=False,
    )
```

profile of v0, /device:TPU:1, one launch (start us, length us, event | category | flops | bytes accessed | tf_op | source)
XLA Modules:
  0.0 648.8 jit_solution(4276677305458766648)
XLA Ops:
  1.6 1.4 collective-permute-start.1
  3.8 1.6 collective-permute-start
  5.4 68.6 %psum.42 = f32[]{:T(128)} all-reduce(f32[]{:T(128)} %multiply_reduce_fusion.5), channel_id=1, replica_groups=mesh['gx'=8,'gy'=16] {'gx','gy'}, use_global_device_ids=true, to_apply=%region_1.2 | all-reduce | flops 1 | bytes 8 | tf_op jit(solution)/shard_map/psum | solution.py:80
  75.5 2.4 collective-permute-start.3
  78.8 5.0 collective-permute-done.2
  85.7 2.1 collective-permute-start.5
  87.9 5.2 collective-permute-done.5
  93.4 1.5 collective-permute-start.6
  94.9 2.0 collective-permute-done.7
  96.8 3.4 collective-permute-done.6
  102.1 4.2 collective-permute-start.9
  106.4 4.5 collective-permute-done.9
  111.3 1.5 collective-permute-start.10
  112.8 2.0 collective-permute-done.11
  114.7 3.4 collective-permute-done.10
  119.8 4.9 collective-permute-start.13
  124.7 4.5 collective-permute-done.13
  129.7 1.5 collective-permute-start.14
  131.2 2.0 collective-permute-done.15
  133.2 3.4 collective-permute-done.14
  137.7 4.9 collective-permute-start.17
  144.8 5.0 collective-permute-start.19
  152.4 4.8 collective-permute-start.21
  157.2 1.4 collective-permute-done.21
  159.4 5.3 collective-permute-start.23
  167.4 4.6 collective-permute-start.25
  172.0 4.5 collective-permute-done.25
  176.8 4.9 collective-permute-start.27
  181.8 1.6 collective-permute-done.27
  183.4 5.1 collective-permute-done.26
  190.6 66.6 %psum.43 = f32[]{:T(128)} all-reduce(f32[]{:T(128)} %multiply_reduce_fusion.4), channel_id=1, replica_groups=mesh['gx'=8,'gy'=16] {'gx','gy'}, use_global_device_ids=true, to_apply=%region_3.4 | all-reduce | flops 1 | bytes 8 | tf_op jit(solution)/shard_map/psum | solution.py:247
  257.1 1.4 multiply_reduce_fusion.3
  258.6 62.5 %psum.44 = f32[]{:T(128)} all-reduce(f32[]{:T(128)} %multiply_reduce_fusion.3), channel_id=1, replica_groups=mesh['gx'=8,'gy'=16] {'gx','gy'}, use_global_device_ids=true, to_apply=%region_5.6 | all-reduce | flops 1 | bytes 8 | tf_op jit(solution)/shard_map/psum | solution.py:80
  324.9 5.7 collective-permute-done.29
  330.8 2.3 collective-permute-start.31
  333.2 1.6 collective-permute-done.31
  334.8 5.1 collective-permute-done.30
  342.6 3.7 collective-permute-start.33
  346.4 4.9 collective-permute-done.33
  351.5 1.6 collective-permute-start.34
  353.2 1.8 collective-permute-done.35
  355.0 3.6 collective-permute-done.34
  361.0 4.7 collective-permute-start.37
  365.7 4.5 collective-permute-done.37
  370.6 1.5 collective-permute-start.38
  372.1 2.0 collective-permute-done.39
  374.1 3.4 collective-permute-done.38
  379.0 4.9 collective-permute-start.41
  383.9 1.4 collective-permute-done.41
  386.0 4.8 collective-permute-start.43
  394.6 4.8 collective-permute-start.45
  399.4 1.4 collective-permute-done.45
  401.6 4.8 collective-permute-start.47
  409.2 4.8 collective-permute-start.49
  414.1 4.5 collective-permute-done.49
  418.9 4.9 collective-permute-start.51
  423.8 1.6 collective-permute-done.51
  425.4 5.1 collective-permute-done.50
  433.3 66.6 %psum.45 = f32[]{:T(128)} all-reduce(f32[]{:T(128)} %multiply_reduce_fusion.2), channel_id=1, replica_groups=mesh['gx'=8,'gy'=16] {'gx','gy'}, use_global_device_ids=true, to_apply=%region_7.8 | all-reduce | flops 1 | bytes 8 | tf_op jit(solution)/shard_map/psum | solution.py:247
  499.9 2.1 multiply_reduce_fusion.1
  502.7 62.8 %psum.46 = f32[]{:T(128)} all-reduce(f32[]{:T(128)} %multiply_reduce_fusion.1), channel_id=1, replica_groups=mesh['gx'=8,'gy'=16] {'gx','gy'}, use_global_device_ids=true, to_apply=%region_9.10 | all-reduce | flops 1 | bytes 8 | tf_op jit(solution)/shard_map/psum | solution.py:247
  565.6 3.7 multiply_reduce_fusion
  569.4 64.1 %psum.47 = f32[]{:T(128)} all-reduce(f32[]{:T(128)} %multiply_reduce_fusion), channel_id=1, replica_groups=mesh['gx'=8,'gy'=16] {'gx','gy'}, use_global_device_ids=true, to_apply=%region_11.12 | all-reduce | flops 1 | bytes 8 | tf_op jit(solution)/shard_map/psum | solution.py:80
  634.2 1.9 scatter.20
  (296 shorter events, 50.0 us)
Async XLA Ops:
  1.6 73.8 %collective-permute-start.1 = (s32[16,8,1]{2,0,1:T(8,128)S(1)}, s32[16,8,1]{2,0,1:T(8,128)S(1)}, u32[]{:S(2)}, u32[]{:S(2)}) collective-permute-start(s32[16,8,1]{2,0,1:T(8,128)S(1)} %get-tuple-element.277), channel_id=1, source_target_pairs={{16,0},{32,16},{48,32},{64,48},{80,64},{96,80},{112,96},{0,112},{1... | collective-permute-start | bytes 1544 | tf_op jit(solution)/shard_map/ppermute | solution.py:28
  3.8 71.7 %collective-permute-start = (s32[16,8,1]{2,0,1:T(8,128)S(1)}, s32[16,8,1]{2,0,1:T(8,128)S(1)}, u32[]{:S(2)}, u32[]{:S(2)}) collective-permute-start(s32[16,8,1]{2,0,1:T(8,128)S(1)} %get-tuple-element.276), channel_id=1, source_target_pairs={{0,16},{16,32},{32,48},{48,64},{64,80},{80,96},{96,112},{112,0},{1... | collective-permute-start | bytes 1544 | tf_op jit(solution)/shard_map/ppermute | solution.py:27
  75.5 3.3 collective-permute-start.3
  77.9 5.9 collective-permute-start.2
  85.4 81.0 %copy-start.1 = (f32[3,1,16,8,128]{4,2,3,1,0:T(8,128)}, f32[3,1,16,8,128]{4,2,3,1,0:T(8,128)S(1)}, u32[]{:S(2)}) copy-start(f32[3,1,16,8,128]{4,2,3,1,0:T(8,128)S(1)} %get-tuple-element.90) | copy-start | bytes 589828
  85.4 81.0 %copy-start.3 = (f32[3,1,16,8,128]{4,2,3,1,0:T(8,128)}, f32[3,1,16,8,128]{4,2,3,1,0:T(8,128)S(1)}, u32[]{:S(2)}) copy-start(f32[3,1,16,8,128]{4,2,3,1,0:T(8,128)S(1)} %get-tuple-element.91) | copy-start | bytes 589828
  85.7 7.5 %collective-permute-start.5 = (f32[3,2,16,8,1]{4,2,3,1,0:T(8,128)S(1)}, f32[3,2,16,8,1]{4,2,3,1,0:T(8,128)S(1)}, u32[]{:S(2)}, u32[]{:S(2)}) collective-permute-start(f32[3,2,16,8,1]{4,2,3,1,0:T(8,128)S(1)} %get-tuple-element.206), channel_id=1, source_target_pairs={{16,0},{32,16},{48,32},{64,48},{80,64},{96,80},{112,96},{0,112},{1... | collective-permute-start | bytes 9224 | tf_op jit(solution)/shard_map/ppermute | solution.py:28
  87.8 5.4 collective-permute-start.4
  93.3 3.5 collective-permute-start.7
  93.4 6.9 %collective-permute-start.6 = (f32[3,2,16,1,130]{4,2,3,1,0:T(8,128)S(1)}, f32[3,2,16,1,130]{4,2,3,1,0:T(8,128)S(1)}, u32[]{:S(2)}, u32[]{:S(2)}) collective-permute-start(f32[3,2,16,1,130]{4,2,3,1,0:T(8,128)S(1)} %get-tuple-element.106), channel_id=1, source_target_pairs={{0,1},{1,2},{2,3},{3,4},{4,5},{5,6},{6,7},{7,8},{8,9},{9,10},{10,1... | collective-permute-start | bytes 149768 | tf_op jit(solution)/shard_map/ppermute | solution.py:27
  102.1 8.8 %collective-permute-start.9 = (f32[3,2,16,8,1]{4,2,3,1,0:T(8,128)S(1)}, f32[3,2,16,8,1]{4,2,3,1,0:T(8,128)S(1)}, u32[]{:S(2)}, u32[]{:S(2)}) collective-permute-start(f32[3,2,16,8,1]{4,2,3,1,0:T(8,128)S(1)} %get-tuple-element.202), channel_id=1, source_target_pairs={{16,0},{32,16},{48,32},{64,48},{80,64},{96,80},{112,96},{0,112},{1... | collective-permute-start | bytes 9224 | tf_op jit(solution)/shard_map/ppermute | solution.py:28
  106.3 4.7 collective-permute-start.8
  111.2 3.5 collective-permute-start.11
  111.3 6.9 %collective-permute-start.10 = (f32[3,2,16,1,130]{4,2,3,1,0:T(8,128)S(1)}, f32[3,2,16,1,130]{4,2,3,1,0:T(8,128)S(1)}, u32[]{:S(2)}, u32[]{:S(2)}) collective-permute-start(f32[3,2,16,1,130]{4,2,3,1,0:T(8,128)S(1)} %get-tuple-element.104), channel_id=1, source_target_pairs={{0,1},{1,2},{2,3},{3,4},{4,5},{5,6},{6,7},{7,8},{8,9},{9,10},{10,1... | collective-permute-start | bytes 149768 | tf_op jit(solution)/shard_map/ppermute | solution.py:27
  119.8 9.4 %collective-permute-start.13 = (f32[3,2,16,8,1]{4,2,3,1,0:T(8,128)S(1)}, f32[3,2,16,8,1]{4,2,3,1,0:T(8,128)S(1)}, u32[]{:S(2)}, u32[]{:S(2)}) collective-permute-start(f32[3,2,16,8,1]{4,2,3,1,0:T(8,128)S(1)} %get-tuple-element.198), channel_id=1, source_target_pairs={{16,0},{32,16},{48,32},{64,48},{80,64},{96,80},{112,96},{0,112},{1... | collective-permute-start | bytes 9224 | tf_op jit(solution)/shard_map/ppermute | solution.py:28
  124.7 4.7 collective-permute-start.12
  129.6 3.5 collective-permute-start.15
  129.7 6.9 %collective-permute-start.14 = (f32[3,2,16,1,130]{4,2,3,1,0:T(8,128)S(1)}, f32[3,2,16,1,130]{4,2,3,1,0:T(8,128)S(1)}, u32[]{:S(2)}, u32[]{:S(2)}) collective-permute-start(f32[3,2,16,1,130]{4,2,3,1,0:T(8,128)S(1)} %get-tuple-element.102), channel_id=1, source_target_pairs={{0,1},{1,2},{2,3},{3,4},{4,5},{5,6},{6,7},{7,8},{8,9},{9,10},{10,1... | collective-permute-start | bytes 149768 | tf_op jit(solution)/shard_map/ppermute | solution.py:27
  137.5 14.7 %copy-start.10 = (f32[1,16,8,128]{3,1,2,0:T(8,128)}, f32[1,16,8,128]{3,1,2,0:T(8,128)S(1)}, u32[]{:S(2)}) copy-start(f32[1,16,8,128]{3,1,2,0:T(8,128)S(1)} %get-tuple-element.83) | copy-start | bytes 196612
  137.7 6.3 collective-permute-start.17
  142.5 2.0 collective-permute-start.16
  144.6 6.2 collective-permute-start.18
  144.7 6.5 copy-start.12
  144.8 6.5 copy-start.14
  144.8 6.2 collective-permute-start.19
  152.4 6.3 collective-permute-start.21
  157.2 2.0 collective-permute-start.20
  159.3 6.6 %collective-permute-start.22 = (f32[2,16,1,130]{3,1,2,0:T(8,128)S(1)}, f32[2,16,1,130]{3,1,2,0:T(8,128)S(1)}, u32[]{:S(2)}, u32[]{:S(2)}) collective-permute-start(f32[2,16,1,130]{3,1,2,0:T(8,128)S(1)} %get-tuple-element.193), channel_id=1, source_target_pairs={{0,1},{1,2},{2,3},{3,4},{4,5},{5,6},{6,7},{7,8},{8,9},{9,10},{10,1... | collective-permute-start | bytes 49928 | tf_op jit(solution)/shard_map/ppermute | solution.py:27
  159.4 6.8 %collective-permute-start.23 = (f32[2,16,1,130]{3,1,2,0:T(8,128)S(1)}, f32[2,16,1,130]{3,1,2,0:T(8,128)S(1)}, u32[]{:S(2)}, u32[]{:S(2)}) collective-permute-start(f32[2,16,1,130]{3,1,2,0:T(8,128)S(1)} %get-tuple-element.194), channel_id=1, source_target_pairs={{1,0},{2,1},{3,2},{4,3},{5,4},{6,5},{7,6},{8,7},{9,8},{10,9},{11,1... | collective-permute-start | bytes 49928 | tf_op jit(solution)/shard_map/ppermute | solution.py:28
  167.4 9.1 %collective-permute-start.25 = (f32[3,2,16,8,1]{4,2,3,1,0:T(8,128)S(1)}, f32[3,2,16,8,1]{4,2,3,1,0:T(8,128)S(1)}, u32[]{:S(2)}, u32[]{:S(2)}) collective-permute-start(f32[3,2,16,8,1]{4,2,3,1,0:T(8,128)S(1)} %get-tuple-element.190), channel_id=1, source_target_pairs={{16,0},{32,16},{48,32},{64,48},{80,64},{96,80},{112,96},{0,112},{1... | collective-permute-start | bytes 9224 | tf_op jit(solution)/shard_map/ppermute | solution.py:28
  172.0 4.7 collective-permute-start.24
  176.8 6.5 %collective-permute-start.27 = (f32[3,2,16,1,130]{4,2,3,1,0:T(8,128)S(1)}, f32[3,2,16,1,130]{4,2,3,1,0:T(8,128)S(1)}, u32[]{:S(2)}, u32[]{:S(2)}) collective-permute-start(f32[3,2,16,1,130]{4,2,3,1,0:T(8,128)S(1)} %get-tuple-element.101), channel_id=1, source_target_pairs={{1,0},{2,1},{3,2},{4,3},{5,4},{6,5},{7,6},{8,7},{9,8},{10,9},{11,1... | collective-permute-start | bytes 149768 | tf_op jit(solution)/shard_map/ppermute | solution.py:28
  181.7 6.8 %collective-permute-start.26 = (f32[3,2,16,1,130]{4,2,3,1,0:T(8,128)S(1)}, f32[3,2,16,1,130]{4,2,3,1,0:T(8,128)S(1)}, u32[]{:S(2)}, u32[]{:S(2)}) collective-permute-start(f32[3,2,16,1,130]{4,2,3,1,0:T(8,128)S(1)} %get-tuple-element.100), channel_id=1, source_target_pairs={{0,1},{1,2},{2,3},{3,4},{4,5},{5,6},{6,7},{7,8},{8,9},{9,10},{10,1... | collective-permute-start | bytes 149768 | tf_op jit(solution)/shard_map/ppermute | solution.py:27
  322.8 85.4 %copy-start.5 = (f32[3,1,16,8,128]{4,2,3,0,1:T(8,128)}, f32[3,1,16,8,128]{4,2,3,0,1:T(8,128)S(1)}, u32[]{:S(2)}) copy-start(f32[3,1,16,8,128]{4,2,3,0,1:T(8,128)S(1)} %get-tuple-element.86) | copy-start | bytes 589828
  322.8 85.4 %copy-start.7 = (f32[3,1,16,8,128]{4,2,3,0,1:T(8,128)}, f32[3,1,16,8,128]{4,2,3,0,1:T(8,128)S(1)}, u32[]{:S(2)}) copy-start(f32[3,1,16,8,128]{4,2,3,0,1:T(8,128)S(1)} %get-tuple-element.87) | copy-start | bytes 589828
  323.1 7.5 %collective-permute-start.29 = (f32[3,2,16,8,1]{4,2,3,1,0:T(8,128)S(1)}, f32[3,2,16,8,1]{4,2,3,1,0:T(8,128)S(1)}, u32[]{:S(2)}, u32[]{:S(2)}) collective-permute-start(f32[3,2,16,8,1]{4,2,3,1,0:T(8,128)S(1)} %get-tuple-element.188), channel_id=1, source_target_pairs={{16,0},{32,16},{48,32},{64,48},{80,64},{96,80},{112,96},{0,112},{1... | collective-permute-start | bytes 9224 | tf_op jit(solution)/shard_map/ppermute | solution.py:28
  323.7 6.9 %collective-permute-start.28 = (f32[3,2,16,8,1]{4,2,3,1,0:T(8,128)S(1)}, f32[3,2,16,8,1]{4,2,3,1,0:T(8,128)S(1)}, u32[]{:S(2)}, u32[]{:S(2)}) collective-permute-start(f32[3,2,16,8,1]{4,2,3,1,0:T(8,128)S(1)} %get-tuple-element.187), channel_id=1, source_target_pairs={{0,16},{16,32},{32,48},{48,64},{64,80},{80,96},{96,112},{112,0},{1... | collective-permute-start | bytes 9224 | tf_op jit(solution)/shard_map/ppermute | solution.py:27
  330.8 4.0 collective-permute-start.31
  333.1 6.8 %collective-permute-start.30 = (f32[3,2,16,1,130]{4,2,3,1,0:T(8,128)S(1)}, f32[3,2,16,1,130]{4,2,3,1,0:T(8,128)S(1)}, u32[]{:S(2)}, u32[]{:S(2)}) collective-permute-start(f32[3,2,16,1,130]{4,2,3,1,0:T(8,128)S(1)} %get-tuple-element.98), channel_id=1, source_target_pairs={{0,1},{1,2},{2,3},{3,4},{4,5},{5,6},{6,7},{7,8},{8,9},{9,10},{10,1... | collective-permute-start | bytes 149768 | tf_op jit(solution)/shard_map/ppermute | solution.py:27
  342.6 8.7 %collective-permute-start.33 = (f32[3,2,16,8,1]{4,2,3,1,0:T(8,128)S(1)}, f32[3,2,16,8,1]{4,2,3,1,0:T(8,128)S(1)}, u32[]{:S(2)}, u32[]{:S(2)}) collective-permute-start(f32[3,2,16,8,1]{4,2,3,1,0:T(8,128)S(1)} %get-tuple-element.184), channel_id=1, source_target_pairs={{16,0},{32,16},{48,32},{64,48},{80,64},{96,80},{112,96},{0,112},{1... | collective-permute-start | bytes 9224 | tf_op jit(solution)/shard_map/ppermute | solution.py:28
  346.3 4.9 collective-permute-start.32
  351.4 3.5 collective-permute-start.35
  351.5 7.1 %collective-permute-start.34 = (f32[3,2,16,1,130]{4,2,3,1,0:T(8,128)S(1)}, f32[3,2,16,1,130]{4,2,3,1,0:T(8,128)S(1)}, u32[]{:S(2)}, u32[]{:S(2)}) collective-permute-start(f32[3,2,16,1,130]{4,2,3,1,0:T(8,128)S(1)} %get-tuple-element.96), channel_id=1, source_target_pairs={{0,1},{1,2},{2,3},{3,4},{4,5},{5,6},{6,7},{7,8},{8,9},{9,10},{10,1... | collective-permute-start | bytes 149768 | tf_op jit(solution)/shard_map/ppermute | solution.py:27
  361.0 9.2 %collective-permute-start.37 = (f32[3,2,16,8,1]{4,2,3,1,0:T(8,128)S(1)}, f32[3,2,16,8,1]{4,2,3,1,0:T(8,128)S(1)}, u32[]{:S(2)}, u32[]{:S(2)}) collective-permute-start(f32[3,2,16,8,1]{4,2,3,1,0:T(8,128)S(1)} %get-tuple-element.180), channel_id=1, source_target_pairs={{16,0},{32,16},{48,32},{64,48},{80,64},{96,80},{112,96},{0,112},{1... | collective-permute-start | bytes 9224 | tf_op jit(solution)/shard_map/ppermute | solution.py:28
  365.6 4.7 collective-permute-start.36
  370.5 3.5 collective-permute-start.39
  370.6 6.9 %collective-permute-start.38 = (f32[3,2,16,1,130]{4,2,3,1,0:T(8,128)S(1)}, f32[3,2,16,1,130]{4,2,3,1,0:T(8,128)S(1)}, u32[]{:S(2)}, u32[]{:S(2)}) collective-permute-start(f32[3,2,16,1,130]{4,2,3,1,0:T(8,128)S(1)} %get-tuple-element.94), channel_id=1, source_target_pairs={{0,1},{1,2},{2,3},{3,4},{4,5},{5,6},{6,7},{7,8},{8,9},{9,10},{10,1... | collective-permute-start | bytes 149768 | tf_op jit(solution)/shard_map/ppermute | solution.py:27
  379.0 6.3 collective-permute-start.41
  383.9 2.0 collective-permute-start.40
  385.9 6.2 collective-permute-start.42
  386.0 6.3 collective-permute-start.43
  394.6 6.3 collective-permute-start.45
  399.4 2.0 collective-permute-start.44
  401.5 6.2 collective-permute-start.46
  401.6 6.4 collective-permute-start.47
  409.2 9.4 %collective-permute-start.49 = (f32[3,2,16,8,1]{4,2,3,1,0:T(8,128)S(1)}, f32[3,2,16,8,1]{4,2,3,1,0:T(8,128)S(1)}, u32[]{:S(2)}, u32[]{:S(2)}) collective-permute-start(f32[3,2,16,8,1]{4,2,3,1,0:T(8,128)S(1)} %get-tuple-element.172), channel_id=1, source_target_pairs={{16,0},{32,16},{48,32},{64,48},{80,64},{96,80},{112,96},{0,112},{1... | collective-permute-start | bytes 9224 | tf_op jit(solution)/shard_map/ppermute | solution.py:28
  414.0 4.7 collective-permute-start.48
  418.9 6.5 %collective-permute-start.51 = (f32[3,2,16,1,130]{4,2,3,1,0:T(8,128)S(1)}, f32[3,2,16,1,130]{4,2,3,1,0:T(8,128)S(1)}, u32[]{:S(2)}, u32[]{:S(2)}) collective-permute-start(f32[3,2,16,1,130]{4,2,3,1,0:T(8,128)S(1)} %get-tuple-element.93), channel_id=1, source_target_pairs={{1,0},{2,1},{3,2},{4,3},{5,4},{6,5},{7,6},{8,7},{9,8},{10,9},{11,1... | collective-permute-start | bytes 149768 | tf_op jit(solution)/shard_map/ppermute | solution.py:28
  423.8 6.8 %collective-permute-start.50 = (f32[3,2,16,1,130]{4,2,3,1,0:T(8,128)S(1)}, f32[3,2,16,1,130]{4,2,3,1,0:T(8,128)S(1)}, u32[]{:S(2)}, u32[]{:S(2)}) collective-permute-start(f32[3,2,16,1,130]{4,2,3,1,0:T(8,128)S(1)} %get-tuple-element.92), channel_id=1, source_target_pairs={{0,1},{1,2},{2,3},{3,4},{4,5},{5,6},{6,7},{7,8},{8,9},{9,10},{10,1... | collective-permute-start | bytes 149768 | tf_op jit(solution)/shard_map/ppermute | solution.py:27
  431.9 68.0 %copy-start.9 = (f32[1,2,16,8,128]{4,2,3,1,0:T(8,128)}, f32[1,2,16,8,128]{4,2,3,1,0:T(8,128)S(1)}, u32[]{:S(2)}) copy-start(f32[1,2,16,8,128]{4,2,3,1,0:T(8,128)S(1)} %get-tuple-element.227) | copy-start | bytes 393220
  565.5 80.6 %copy-start.2 = (f32[3,1,16,8,128]{4,2,3,1,0:T(8,128)S(1)}, f32[3,1,16,8,128]{4,2,3,1,0:T(8,128)}, u32[]{:S(2)}) copy-start(f32[3,1,16,8,128]{4,2,3,1,0:T(8,128)} %copy-done.1) | copy-start | bytes 589828
  565.5 80.6 %copy-start.4 = (f32[3,1,16,8,128]{4,2,3,1,0:T(8,128)S(1)}, f32[3,1,16,8,128]{4,2,3,1,0:T(8,128)}, u32[]{:S(2)}) copy-start(f32[3,1,16,8,128]{4,2,3,1,0:T(8,128)} %copy-done.3) | copy-start | bytes 589828
  565.6 80.6 %copy-start.6 = (f32[3,1,16,8,128]{4,2,3,0,1:T(8,128)S(1)}, f32[3,1,16,8,128]{4,2,3,0,1:T(8,128)}, u32[]{:S(2)}) copy-start(f32[3,1,16,8,128]{4,2,3,0,1:T(8,128)} %copy-done.5) | copy-start | bytes 589828
  565.6 80.6 %copy-start.8 = (f32[3,1,16,8,128]{4,2,3,0,1:T(8,128)S(1)}, f32[3,1,16,8,128]{4,2,3,0,1:T(8,128)}, u32[]{:S(2)}) copy-start(f32[3,1,16,8,128]{4,2,3,0,1:T(8,128)} %copy-done.7) | copy-start | bytes 589828
  (17 other events, 26.4 us)
where the time goes:
time: 658 us; the launch traced here: 649 us
  blocking collectives  391 us (59%)
  waiting for transfers between devices  105 us (16%)
  starting transfers between devices  95.9 us (15%)
  other arithmetic  30.5 us (5%)
  local copies, waits for them, and re-layouts  16.3 us (2%)
  between operations  10.1 us (2%)
    psum x3, blocking collectives, on_device(): factor_value = lax.psum(jnp.sum(krylov[earlier] * applied), ('gx', 'gy'))  196 us
    psum x3, blocking collectives, norm_of(): return jnp.sqrt(lax.psum(jnp.sum(values * values), ('gx', 'gy')) + epsilon)  195 us
    ppermute x26, starting transfers between devices, with_halo(): after = lax.ppermute(first, axis, down)  85.3 us
    ppermute x26, waiting for transfers between devices, with_halo(): after = lax.ppermute(first, axis, down)  59.1 us
    ppermute x26, waiting for transfers between devices, with_halo(): before = lax.ppermute(last, axis, up)  45.6 us
  transfers between devices with their start and end apart: 52, of which 43 were waited for; matrix products, arithmetic and copies ran while one was open for 0% of the time, Pallas kernels for 0%

commit v1 on v0

v1 whole, which is shorter than its diff:
```python
import jax
import jax.numpy as jnp
from jax import lax
from jax.experimental import pallas as pl
from jax.experimental.pallas import tpu as pltpu
from jax.sharding import PartitionSpec as P

epsilon = 1e-06
LANES = 128
SUBS = 8
REACH = 4
HALO = 2 * REACH
ROWS = SUBS + 2 * HALO
STRIP = 16
VMEM_LIMIT = 56 * 2**20


class Field:
    def __init__(self, parts):
        self.parts = tuple(parts)

    def zip(self, other, op):
        if isinstance(other, Field):
            return Field(op(a, b) for a, b in zip(self.parts, other.parts))
        return Field(op(a, other) for a in self.parts)

    def __add__(self, other):
        return self.zip(other, lambda a, b: a + b)

    def __sub__(self, other):
        return self.zip(other, lambda a, b: a - b)

    def __mul__(self, other):
        return self.zip(other, lambda a, b: a * b)

    __rmul__ = __mul__

    def __rtruediv__(self, top):
        return Field(top / a for a in self.parts)


class Shifts:
    def __init__(self):
        lane = lax.broadcasted_iota(jnp.int32, (SUBS, LANES), 1)
        sub = lax.broadcasted_iota(jnp.int32, (SUBS, LANES), 0)
        self.first_lane = lane == 0
        self.last_lane = lane == LANES - 1
        self.first_sub = sub == 0
        self.last_sub = sub == SUBS - 1

    def east(self, field):
        r = [pltpu.roll(t, LANES - 1, 1) for t in field.parts]
        return Field(jnp.where(self.last_lane, r[k ^ 1], r[k]) for k in range(4))

    def west(self, field):
        r = [pltpu.roll(t, 1, 1) for t in field.parts]
        return Field(jnp.where(self.first_lane, r[k ^ 1], r[k]) for k in range(4))

    def above(self, field):
        r = [pltpu.roll(t, SUBS - 1, 0) for t in field.parts]
        low = [jnp.where(self.last_sub, r[2 + k], r[k]) for k in range(2)]
        return Field(low + [jnp.where(self.last_sub, 0.0, r[2 + k]) for k in range(2)])

    def below(self, field):
        r = [pltpu.roll(t, 1, 0) for t in field.parts]
        low = [jnp.where(self.first_sub, 0.0, r[k]) for k in range(2)]
        return Field(low + [jnp.where(self.first_sub, r[k], r[2 + k]) for k in range(2)])


def get(ref, row, c):
    return Field(ref[row, c, k] for k in range(4))


def put(ref, row, c, field):
    for k in range(4):
        ref[row, c, k] = field.parts[k]


def loop(start, stop, body):
    lax.fori_loop(start, stop, lambda i, c: (body(i), c)[1], 0)


def pack_kernel(rhs_ref, mat_ref, out_ref):
    for y in range(SUBS):
        for z in range(2):
            rows = pl.ds(z * 64 + y, SUBS, stride=SUBS)
            for c in range(6):
                out_ref[y, c, z] = rhs_ref[c, rows, :]
            out_ref[y, 6, z] = mat_ref[rows, :].astype(jnp.float32)


def strip_kernel(low_ref, own_ref, high_ref, last_ref, left_ref, right_ref):
    lane = lax.broadcasted_iota(jnp.int32, (SUBS, LANES), 1)
    for group, ref in enumerate((low_ref, own_ref, high_ref)):

        def channel(c, ref=ref, group=group):
            for z in range(2):
                left = ref[0, c, z]
                right = pltpu.roll(left, STRIP, 1)
                for r in range(1, SUBS):
                    tile = ref[r, c, z]
                    here = (lane >= STRIP * r) & (lane < STRIP * (r + 1))
                    left = jnp.where(here, pltpu.roll(tile, STRIP * r, 1), left)
                    right = jnp.where(here, pltpu.roll(tile, (STRIP * (r + 1)) % LANES, 1), right)
                left_ref[group * 7 + c, z] = left
                right_ref[group * 7 + c, z] = right

        loop(0, 7, channel)
    for z in range(2):
        left_ref[21, z] = last_ref[z]
        right_ref[21, z] = pltpu.roll(last_ref[z], STRIP, 1)


def iterate(sh, v, out, u, s2, coef, z1, t1, p, node, flux, a, b):
    def fluxes(e, above_row):
        bx = (above_row[1] - e[2]) - (sh.above(e[1]) - e[1])
        by = (sh.above(e[0]) - e[0]) - (sh.east(e[2]) - e[2])
        bz = (sh.east(e[1]) - e[1]) - (above_row[0] - e[0])
        return bx, by, bz

    def curl(row, e, e_next):
        result = []
        for part in range(2):
            here = [e[2 * c + part] for c in range(3)]
            bx, by, bz = fluxes(here, (e_next[part], e_next[4 + part]))
            pbx, pbz = get(flux, row, 2 * part), get(flux, row, 2 * part + 1)
            put(flux, row + 1, 2 * part, bx)
            put(flux, row + 1, 2 * part + 1, bz)
            result.append(
                (
                    (pbz - bz) - (sh.below(by) - by),
                    (sh.below(bx) - bx) - (sh.west(bz) - bz),
                    (sh.west(by) - by) - (pbx - bx),
                )
            )
        return [result[k % 2][k // 2] for k in range(6)]

    def tensor(row, e):
        s = [get(s2, row, c) for c in range(6)]
        return [
            s[0] * e[0] + s[3] * e[1] + s[4] * e[2],
            s[3] * e[0] + s[1] * e[1] + s[5] * e[2],
            s[4] * e[0] + s[5] * e[1] + s[2] * e[2],
        ]

    def operator(row, e, e_next):
        k = curl(row, e, e_next)
        si = tensor(row, e[1::2])
        sr = tensor(row, e[0::2])
        return [k[j] - si[j // 2] if j % 2 == 0 else k[j] + sr[j // 2] for j in range(6)]

    def jacobi(row, e, scale):
        result = []
        for c in range(3):
            alpha, beta = get(coef, row, c), get(coef, row, 3 + c)
            result.append(scale * (alpha * e[2 * c] + beta * e[2 * c + 1]))
            result.append(scale * (alpha * e[2 * c + 1] - beta * e[2 * c]))
        return result

    def nodal(row, q, scale):
        alpha, beta = get(coef, row, 6), get(coef, row, 7)
        return [scale * (alpha * q[0] + beta * q[1]), scale * (alpha * q[1] - beta * q[0])]

    def load(ref, row, n=6):
        return [get(ref, row, c) for c in range(n)]

    def store(ref, row, values, base=0):
        for c, value in enumerate(values):
            put(ref, row, base + c, value)

    store(z1, a, jacobi(a, load(v, a), 0.7))

    def first(y):
        ahead = jacobi(y + 1, load(v, y + 1), 0.7)
        store(z1, y + 1, ahead)
        applied = operator(y, load(z1, y), ahead)
        rest = [r - w for r, w in zip(load(v, y), applied)]
        store(t1, y, rest)
        store(p, y, jacobi(y, rest, 0.6))

    loop(a, b - 1, first)

    def second(y):
        applied = operator(y, load(p, y), load(p, y + 1))
        rest = [r - w for r, w in zip(load(t1, y), applied)]
        source = []
        for part in range(2):
            x, n, d = rest[part], rest[2 + part], rest[4 + part]
            before = get(node, y, 6 + part)
            put(node, y + 1, 6 + part, n)
            source.append(((sh.west(x) - x) + (before - n)) + (sh.below(d) - d))
        store(node, y, source)
        store(node, y, nodal(y, source, 0.8), 2)

    loop(a + 1, b - 2, second)

    def third(y):
        w = [get(node, y, 2 + part) for part in range(2)]
        slopes = []
        for part in range(2):
            ahead = get(node, y + 1, 2 + part)
            slopes.append((sh.east(w[part]) - w[part], ahead - w[part], sh.above(w[part]) - w[part]))
        si = tensor(y, slopes[1])
        sr = tensor(y, slopes[0])
        rest = []
        for part in range(2):
            if part == 0:
                x, n, d = [g - s for g, s in zip(slopes[0], si)]
            else:
                x, n, d = [g + s for g, s in zip(slopes[1], sr)]
            before = get(node, y, 6 + part)
            put(node, y + 1, 6 + part, n)
            applied = ((sh.west(x) - x) + (before - n)) + (sh.below(d) - d)
            rest.append(get(node, y, part) - applied)
        fix = nodal(y, rest, 0.5)
        store(node, y, [w[part] + fix[part] for part in range(2)], 4)

    loop(a + 2, b - 3, third)

    def lift(y):
        w = [get(node, y, 4 + part) for part in range(2)]
        result = []
        for c in range(3):
            for part in range(2):
                k = 2 * c + part
                if c == 0:
                    slope = sh.east(w[part]) - w[part]
                elif c == 1:
                    slope = get(node, y + 1, 4 + part) - w[part]
                else:
                    slope = sh.above(w[part]) - w[part]
                result.append((get(z1, y, k) + get(p, y, k)) + slope)
        store(u, y, result)
        return result

    lift(a + 3)

    def fourth(y):
        ahead = lift(y + 1)
        store(out, y, operator(y, load(u, y), ahead))

    loop(a + 3, b - 4, fourth)


def two_sum(a, b):
    s = a + b
    t = s - a
    return s, (a - (s - t)) + (b - t)


def main_kernel(
    low_ref, own_ref, high_ref, last_ref, left_ref, right_ref, table_ref,
    a0_ref, a1_ref, sums_ref,
    v, c0, c1, u0, u1, mat, pair, s2, coef, z1, t1, p, node, flux,
):
    sh = Shifts()
    lane = lax.broadcasted_iota(jnp.int32, (SUBS, LANES), 1)
    near = lane < LANES // 2

    def halo(strip, z, r):
        east = pltpu.roll(right_ref[strip, z], lax.rem(LANES - STRIP * r, LANES), 1)
        west = pltpu.roll(left_ref[strip, z], lax.rem(2 * LANES - STRIP - STRIP * r, LANES), 1)
        return jnp.where(near, east, west)

    for group, ref in enumerate((low_ref, own_ref, high_ref)):

        def unpack(r, ref=ref, group=group):
            y = group * SUBS + r
            for z in range(2):
                for c in range(6):
                    v[y, c, 2 * z] = ref[r, c, z]
                    v[y, c, 2 * z + 1] = halo(group * 7 + c, z, r)
                mat[y, 2 * z] = ref[r, 6, z]
                mat[y, 2 * z + 1] = halo(group * 7 + 6, z, r)

        loop(0, SUBS, unpack)
    for z in range(2):
        mat[ROWS, 2 * z] = last_ref[z]
        mat[ROWS, 2 * z + 1] = halo(21, z, 0)

    def pairs(y):
        ids = [mat[y, k].astype(jnp.int32) for k in range(4)]
        for c in range(6):
            cell = Field(jnp.take_along_axis(table_ref[c], i, axis=1) for i in ids)
            put(pair, y, c, cell + sh.east(cell))

    loop(0, ROWS + 1, pairs)

    def tensors(y):
        s = [get(pair, y, c) + get(pair, y + 1, c) for c in range(6)]
        for c in range(6):
            put(s2, y, c, s[c])
        for c in range(3):
            inverse = 1.0 / (s[c] * s[c] + 16.0)
            put(coef, y, c, 4.0 * inverse)
            put(coef, y, 3 + c, s[c] * inverse)
        shift = 2.0 * ((s[0] + s[1]) + s[2])
        inverse = 1.0 / (shift * shift + 36.0)
        put(coef, y, 6, 6.0 * inverse)
        put(coef, y, 7, shift * inverse)

    loop(0, ROWS, tensors)

    iterate(sh, v, c0, u0, s2, coef, z1, t1, p, node, flux, 0, ROWS)
    iterate(sh, c0, c1, u1, s2, coef, z1, t1, p, node, flux, REACH, ROWS - REACH)

    def dots(r, sums):
        y = HALO + r
        sums = list(sums)
        for c in range(6):
            for z in range(2):
                a0_ref[r, c, z] = u0[y, c, 2 * z]
                a1_ref[r, c, z] = u1[y, c, 2 * z]
                f, g, h = v[y, c, 2 * z], c0[y, c, 2 * z], c1[y, c, 2 * z]
                for k, term in enumerate((f * f, f * g, g * g, f * h, g * h, h * h)):
                    sums[k] = sums[k] + term
        return tuple(sums)

    zero = jnp.zeros((SUBS, LANES), jnp.float32)
    sums = lax.fori_loop(0, SUBS, dots, (zero,) * 6)
    row = zero
    for k, total in enumerate(sums):
        rest = zero
        for axis, size in ((0, SUBS), (1, LANES)):
            step = size // 2
            while step:
                total, error = two_sum(total, pltpu.roll(total, step, axis))
                rest = rest + pltpu.roll(rest, step, axis) + error
                step //= 2
        row = jnp.where(lane == k, total, row)
        row = jnp.where(lane == 6 + k, rest, row)
    for k in range(16):
        sums_ref[pl.ds(k * SUBS, SUBS), :] = row


def two_product(a, b):
    def split(x):
        t = 4097.0 * x
        high = t - (t - x)
        return high, x - high

    p = a * b
    ah, al = split(a)
    bh, bl = split(b)
    return p, ((ah * bh - p) + ah * bl + al * bh) + al * bl


def quick(s, e):
    t = s + e
    return t, e - (t - s)


def plus(x, y):
    s, e = two_sum(x[0], y[0])
    return quick(s, e + (x[1] + y[1]))


def minus(x, y):
    return plus(x, (-y[0], -y[1]))


def times(x, y):
    p, e = two_product(x[0], y[0])
    return quick(p, e + (x[0] * y[1] + x[1] * y[0]))


def scaled(x, factor):
    p, e = two_product(x[0], jnp.full_like(x[0], factor))
    return quick(p, e + x[1] * factor)


def over(x, y):
    q = x[0] / y[0]
    r = minus(x, times(y, (q, jnp.zeros_like(q))))
    return quick(q, (r[0] + r[1]) / y[0])


def final_kernel(sums_ref, a0_ref, a1_ref, out_ref, hess_ref):
    lane = lax.broadcasted_iota(jnp.int32, (SUBS, LANES), 1)
    sub = lax.broadcasted_iota(jnp.int32, (SUBS, LANES), 0)
    total = sums_ref[pl.ds(0, SUBS), :]
    rest = jnp.zeros_like(total)
    for k in range(1, 16):
        total, error = two_sum(total, sums_ref[pl.ds(k * SUBS, SUBS), :])
        rest = rest + error
    for step in (4, 2, 1):
        total, error = two_sum(total, pltpu.roll(total, step, 0))
        rest = rest + pltpu.roll(rest, step, 0) + error
    rest = rest + pltpu.roll(total, LANES - 6, 1)

    def pick(values, k):
        one = jnp.sum(jnp.where(lane == k, values, 0.0), axis=1, keepdims=True)
        return jnp.broadcast_to(one, (SUBS, LANES))

    bb, bc, cc, bd, cd, dd = [quick(pick(total, k), pick(rest, k)) for k in range(6)]
    eps = (jnp.full((SUBS, LANES), epsilon, jnp.float32), jnp.zeros((SUBS, LANES), jnp.float32))
    beta2 = plus(bb, eps)
    h00 = over(bc, beta2)
    norm1 = minus(minus(cc, times(h00, bc)), times(eps, times(h00, h00)))
    norm1 = (jnp.maximum(norm1[0], 0.0), jnp.where(norm1[0] > 0.0, norm1[1], 0.0))
    tall = plus(norm1, times(eps, beta2))
    x = minus(bd, times(h00, bc))
    y = plus(minus(minus(cd, times(h00, cc)), times(h00, bd)), times(times(h00, h00), bc))
    x_over = over(x, beta2)
    y_over = over(y, tall)
    norm2 = plus(minus(dd, scaled(times(h00, cd), 2.0)), times(times(h00, h00), cc))
    norm2 = minus(norm2, plus(times(x, x_over), times(eps, times(x_over, x_over))))
    norm2 = minus(norm2, plus(times(y, y_over), times(times(eps, beta2), times(y_over, y_over))))
    norm2 = plus(norm2, scaled(times(times(x_over, y_over), times(eps, h00)), 2.0))
    norm2 = over(norm2, tall)

    beta = jnp.sqrt(beta2[0])
    e00 = h00[0]
    e10 = jnp.sqrt(tall[0] / beta2[0])
    e01 = x_over[0] / e10
    e11 = y_over[0]
    e21 = jnp.sqrt(jnp.maximum(norm2[0], 0.0) + epsilon)

    g00 = e00 * e00 + e10 * e10
    g01 = e00 * e01 + e10 * e11
    g11 = e01 * e01 + e11 * e11 + e21 * e21
    l00 = jnp.sqrt(g00)
    l10 = g01 / l00
    l11 = jnp.sqrt(g11 - l10 * l10)
    m0 = beta * e00 / l00
    m1 = (beta * e01 - l10 * m0) / l11
    y1 = m1 / l11
    y0 = (m0 - l10 * y1) / l00
    k0 = (y0 - y1 * e00 / e10) / beta
    k1 = y1 / (e10 * beta)

    table = jnp.where(sub == 0, jnp.where(lane == 0, e00, e01), jnp.where(lane == 0, e10, e11))
    table = jnp.where(sub == 2, jnp.where(lane == 0, 0.0, e21), table)
    hess_ref[...] = table[:3, :2]
    for row in range(SUBS):
        for z in range(2):
            rows = pl.ds(z * 64 + row, SUBS, stride=SUBS)
            for c in range(6):
                out_ref[c, rows, :] = k0 * a0_ref[row, c, z] + k1 * a1_ref[row, c, z]


def tensor_table(sigma_diag, sigma_off):
    along_east = sigma_diag[0]
    along_north = sigma_diag[1]
    along_depth = sigma_diag[2]
    return jnp.stack(
        [
            along_east,
            along_north,
            along_depth,
            sigma_off[0] * jnp.sqrt(along_east * along_north),
            sigma_off[1] * jnp.sqrt(along_east * along_depth),
            sigma_off[2] * jnp.sqrt(along_north * along_depth),
        ]
    )


def call(kernel, outs, scratch=(), n=0):
    vmem = pl.BlockSpec(memory_space=pltpu.VMEM)
    return pl.pallas_call(
        kernel,
        out_shape=[jax.ShapeDtypeStruct(s, jnp.float32) for s in outs],
        in_specs=[vmem] * n,
        out_specs=[vmem] * len(outs),
        scratch_shapes=[pltpu.VMEM(s, jnp.float32) for s in scratch],
        compiler_params=pltpu.CompilerParams(vmem_limit_bytes=VMEM_LIMIT),
    )


def moved(value, axis, step):
    size = lax.axis_size(axis)
    return lax.ppermute(value, axis, [(i, (i + step) % size) for i in range(size)])


def on_device(right_side, materials, sigma_diag, sigma_off):
    table = jnp.pad(0.5 * tensor_table(sigma_diag, sigma_off), ((0, 0), (0, LANES - 8)))
    table = jnp.broadcast_to(table[:, None, :], (6, SUBS, LANES))
    tile = (SUBS, LANES)
    (own,) = call(pack_kernel, [(SUBS, 7, 2) + tile], n=2)(
        right_side.reshape(6, LANES, LANES), materials.reshape(LANES, LANES)
    )
    low = moved(own, "gy", 1)
    high = moved(own, "gy", -1)
    last = moved(own[0, 6], "gy", -2)
    to_left, to_right = call(strip_kernel, [(22, 2) + tile] * 2, n=4)(low, own, high, last)
    from_right = moved(to_left, "gx", -1)
    from_left = moved(to_right, "gx", 1)

    def rows(n, extra=0):
        return (ROWS + extra, n, 4) + tile

    a0, a1, sums = call(
        main_kernel,
        [(SUBS, 6, 2) + tile, (SUBS, 6, 2) + tile, (LANES, LANES)],
        [rows(6)] * 5
        + [(ROWS + 1, 4) + tile, rows(6, 1), rows(6), rows(8)]
        + [rows(6)] * 3
        + [rows(8, 1), rows(4, 1)],
        n=7,
    )(low, own, high, last, from_left, from_right, table)
    gathered = lax.all_to_all(sums, ("gx", "gy"), 0, 0, tiled=True)
    solution_rows, hessenberg = call(final_kernel, [(6, LANES, LANES), (3, 2)], n=3)(gathered, a0, a1)
    return solution_rows.reshape(right_side.shape), hessenberg


def solution(mesh):
    return jax.shard_map(
        on_device,
        mesh=mesh,
        in_specs=(P(None, None, None, "gy", "gx"), P(None, "gy", "gx"), P(), P()),
        out_specs=(P(None, None, None, "gy", "gx"), P()),
        check_vma=False,
    )
```

time: 658 us -> 89.6 us (0.14); the launches traced: 649 us -> 89.3 us
  blocking collectives: 391 us -> 15.5 us
  waiting for transfers between devices: 105 us -> 17.4 us
  starting transfers between devices: 95.9 us -> 10.8 us
  Pallas kernels: 0 us -> 41.4 us
  other arithmetic: 30.5 us -> 0.03 us
  local copies, waits for them, and re-layouts: 16.3 us -> 3.53 us
  between operations: 10.1 us -> 0.67 us
    psum x6 -> x0, blocking collectives: 391 us -> none  [the longest x3 196 us: on_device(): factor_value = lax.psum(jnp.sum(krylov[earlier] * applied), ('gx', 'gy'))]
    ppermute x52 -> x5, waiting for transfers between devices: 105 us -> 17.4 us  [moved(): lax.ppermute(value, axis, [(i, (i + step) % size) for i in range(size)])]
    ppermute x52 -> x5, starting transfers between devices: 95.9 us -> 10.8 us  [moved(): lax.ppermute(value, axis, [(i, (i + step) % size) for i in range(size)])]
    pallas_call x0 -> x4, Pallas kernels: none -> 41.4 us  [the longest x1 33.1 us: on_device(): call(main_kernel, [(SUBS, 6, 2) + tile, (SUBS, 6, 2) + tile, (LANES, LANE...]
    all_to_all x0 -> x1, blocking collectives: none -> 15.5 us  [on_device(): gathered = lax.all_to_all(sums, ('gx', 'gy'), 0, 0, tiled=True)]
    reduce_sum x6 -> x0, other arithmetic: 9.48 us -> none  [the longest x3 5.87 us: norm_of(): return jnp.sqrt(lax.psum(jnp.sum(values * values), ('gx', 'gy')) + epsilon)]
  transfers between devices with their start and end apart: 52 -> 5, of which waited for: 43 -> 4; matrix products, arithmetic and copies ran while one was open for 0% -> 1% of each run, Pallas kernels for 0% -> 0%
where the time goes in v1:
time: 89.6 us; the launch traced here: 89.3 us
  Pallas kernels  41.4 us (46%)
  waiting for transfers between devices  17.4 us (19%)
  blocking collectives  15.5 us (17%)
  starting transfers between devices  10.8 us (12%)
  local copies, waits for them, and re-layouts  3.53 us (4%)
    pallas_call x1, Pallas kernels, on_device(): call(main_kernel, [(SUBS, 6, 2) + tile, (SUBS, 6, 2) + tile, (LANES, LANE...  33.1 us
    ppermute x5, waiting for transfers between devices, moved(): lax.ppermute(value, axis, [(i, (i + step) % size) for i in range(size)])  17.4 us
    all_to_all x1, blocking collectives, on_device(): gathered = lax.all_to_all(sums, ('gx', 'gy'), 0, 0, tiled=True)  15.5 us
    ppermute x5, starting transfers between devices, moved(): lax.ppermute(value, axis, [(i, (i + step) % size) for i in range(size)])  10.8 us
    pallas_call x1, Pallas kernels, on_device(): call(strip_kernel, [(22, 2) + tile] * 2, n=4)(low, own, high, last)  4.08 us
    pallas_call x1, Pallas kernels, on_device(): call(final_kernel, [(6, LANES, LANES), (3, 2)], n=3)(gathered, a0, a1)  2.37 us
    unnamed x15, local copies, waits for them, and re-layouts  2.12 us
    pallas_call x1, Pallas kernels, on_device(): call(pack_kernel, [(SUBS, 7, 2) + tile], n=2)  1.85 us
  transfers between devices with their start and end apart: 5, of which 4 were waited for; matrix products, arithmetic and copies ran while one was open for 1% of the time, Pallas kernels for 0%

profile of v1, /device:TPU:1, one launch (start us, length us, event | category | flops | bytes accessed | tf_op | source)
XLA Modules:
  0.0 89.3 jit_solution(3049619046854423887)
XLA Ops:
  0.6 1.8 %shard_map.59.own_ref = f32[8,7,2,8,128]{4,3,2,1,0:T(8,128)} custom-call(f32[6,128,128]{2,1,0:T(8,128)} %bitcast.9, s32[128,128]{1,0:T(8,128)} %bitcast.11), custom_call_target="tpu_custom_call" | custom-call | tf_op jit(solution)/shard_map/pallas_call | solution.py:479
  2.5 5.8 %collective-permute-start.1 = (f32[8,7,2,8,128]{4,3,2,1,0:T(8,128)}, f32[8,7,2,8,128]{4,3,2,1,0:T(8,128)S(1)}, u32[]{:S(2)}, u32[]{:S(2)}) collective-permute-start(f32[8,7,2,8,128]{4,3,2,1,0:T(8,128)} %shard_map.59.own_ref), channel_id=1, source_target_pairs={{0,15},{1,0},{2,1},{3,2},{4,3},{5,4},{6,5},{7,6},{8,7},{9,8},{10,9... | collective-permute-start | bytes 1376264 | tf_op jit(solution)/shard_map/ppermute | solution.py:472
  8.2 0.0 collective-permute-start
  8.2 0.8 slice_bitcast_fusion
  9.0 1.7 %collective-permute-start.2 = (f32[2,8,128]{2,1,0:T(8,128)S(1)}, f32[2,8,128]{2,1,0:T(8,128)S(1)}, u32[]{:S(2)}, u32[]{:S(2)}) collective-permute-start(f32[2,8,128]{2,1,0:T(8,128)S(1)} %slice_bitcast_fusion), channel_id=1, source_target_pairs={{0,14},{1,15},{2,0},{3,1},{4,2},{5,3},{6,4},{7,5},{8,6},{9,7},{10,... | collective-permute-start | bytes 24584 | tf_op jit(solution)/shard_map/ppermute | solution.py:472
  10.7 7.1 %collective-permute-done.2.last_ref = f32[2,8,128]{2,1,0:T(8,128)S(1)} collective-permute-done((f32[2,8,128]{2,1,0:T(8,128)S(1)}, f32[2,8,128]{2,1,0:T(8,128)S(1)}, u32[]{:S(2)}, u32[]{:S(2)}) %collective-permute-start.2) | collective-permute-done | bytes 8224 | tf_op jit(solution)/shard_map/ppermute | solution.py:472
  17.8 0.0 copy-start.4
  17.8 0.0 collective-permute-done.1.high_ref
  17.8 0.0 copy-start
  17.9 5.2 %collective-permute-done.low_ref = f32[8,7,2,8,128]{4,3,2,1,0:T(8,128)S(1)} collective-permute-done((f32[8,7,2,8,128]{4,3,2,1,0:T(8,128)}, f32[8,7,2,8,128]{4,3,2,1,0:T(8,128)S(1)}, u32[]{:S(2)}, u32[]{:S(2)}) %collective-permute-start) | collective-permute-done | bytes 458784 | tf_op jit(solution)/shard_map/ppermute | solution.py:472
  23.0 0.0 copy-done.4
  23.0 0.0 copy-done
  23.0 0.0 copy-start.1
  23.0 0.8 copy-done.1
  23.8 0.0 copy-start.6
  23.8 4.1 %shard_map.60 = (f32[22,2,8,128]{3,2,1,0:T(8,128)}, f32[22,2,8,128]{3,2,1,0:T(8,128)}) custom-call(f32[8,7,2,8,128]{4,3,2,1,0:T(8,128)} %copy-done.1, f32[8,7,2,8,128]{4,3,2,1,0:T(8,128)} %shard_map.59.own_ref, f32[8,7,2,8,128]{4,3,2,1,0:T(8,128)} %copy-done, f32[2,8,128]{2,1,0:T(8,128)} %copy-done.4), custom_call_target="tpu_custom_call" | custom-call | tf_op jit(solution)/shard_map/pallas_call | solution.py:485
  27.9 0.0 copy-start.5
  27.9 3.4 %collective-permute-start.3 = (f32[22,2,8,128]{3,2,1,0:T(8,128)}, f32[22,2,8,128]{3,2,1,0:T(8,128)S(1)}, u32[]{:S(2)}, u32[]{:S(2)}) collective-permute-start(f32[22,2,8,128]{3,2,1,0:T(8,128)} %get-tuple-element.9), channel_id=1, source_target_pairs={{0,16},{16,32},{32,48},{48,64},{64,80},{80,96},{96,112},{112,0},{1... | collective-permute-start | bytes 540680 | tf_op jit(solution)/shard_map/ppermute | solution.py:472
  31.3 0.0 collective-permute-start.4
  31.3 0.0 copy-done.6
  31.3 0.0 copy-done.5
  31.3 2.7 %collective-permute-done.3.left_ref = f32[22,2,8,128]{3,2,1,0:T(8,128)S(1)} collective-permute-done((f32[22,2,8,128]{3,2,1,0:T(8,128)}, f32[22,2,8,128]{3,2,1,0:T(8,128)S(1)}, u32[]{:S(2)}, u32[]{:S(2)}) %collective-permute-start.3) | collective-permute-done | bytes 180256 | tf_op jit(solution)/shard_map/ppermute | solution.py:472
  34.0 0.0 copy-start.2
  34.0 2.4 %collective-permute-done.4.right_ref = f32[22,2,8,128]{3,2,1,0:T(8,128)S(1)} collective-permute-done((f32[22,2,8,128]{3,2,1,0:T(8,128)}, f32[22,2,8,128]{3,2,1,0:T(8,128)S(1)}, u32[]{:S(2)}, u32[]{:S(2)}) %collective-permute-start.4) | collective-permute-done | bytes 180256 | tf_op jit(solution)/shard_map/ppermute | solution.py:472
  36.4 0.0 copy-start.3
  36.4 0.6 broadcast_in_dim.2.table_ref
  37.0 0.0 copy-done.2
  37.0 0.0 copy-done.3
  37.1 33.1 %shard_map.61 = (f32[8,6,2,8,128]{4,3,2,1,0:T(8,128)}, f32[8,6,2,8,128]{4,3,2,1,0:T(8,128)}, f32[128,128]{1,0:T(8,128)}) custom-call(f32[8,7,2,8,128]{4,3,2,1,0:T(8,128)} %copy-done.1, f32[8,7,2,8,128]{4,3,2,1,0:T(8,128)} %shard_map.59.own_ref, f32[8,7,2,8,128]{4,3,2,1,0:T(8,128)} %copy-done, f32[2,8,128]{2,1,0:T(8,128)} %copy-done.4, ...), custom_call_target="tpu_custom_call" | custom-call | tf_op jit(solution)/shard_map/pallas_call | solution.py:492
  70.2 15.5 %all_to_all.11 = f32[128,1,128]{2,1,0:T(1,128)} all-to-all(f32[128,1,128]{2,1,0:T(1,128)} %bitcast.12), channel_id=1, replica_groups=mesh['gx'=8,'gy'=16] {'gx','gy'}, dimensions={0} | all-to-all | bytes 131072 | tf_op jit(solution)/shard_map/all_to_all | solution.py:501
  85.6 2.4 %shard_map.62 = (f32[6,128,128]{2,1,0:T(8,128)}, f32[3,2]{1,0:T(4,128)}) custom-call(f32[128,128]{1,0:T(8,128)} %bitcast.10, f32[8,6,2,8,128]{4,3,2,1,0:T(8,128)} %get-tuple-element.12.a0_ref, f32[8,6,2,8,128]{4,3,2,1,0:T(8,128)} %get-tuple-element.13.a1_ref), custom_call_target="tpu_custom_call" | custom-call | tf_op jit(solution)/shard_map/pallas_call | solution.py:502
  88.0 1.3 %copy.8 = f32[3,2]{0,1:T(2,128)} copy(f32[3,2]{1,0:T(4,128)} %get-tuple-element.19) | data formatting | bytes 48
  (3 shorter events, 0.0 us)
Async XLA Ops:
  2.5 15.4 %collective-permute-start.1 = (f32[8,7,2,8,128]{4,3,2,1,0:T(8,128)}, f32[8,7,2,8,128]{4,3,2,1,0:T(8,128)S(1)}, u32[]{:S(2)}, u32[]{:S(2)}) collective-permute-start(f32[8,7,2,8,128]{4,3,2,1,0:T(8,128)} %shard_map.59.own_ref), channel_id=1, source_target_pairs={{0,15},{1,0},{2,1},{3,2},{4,3},{5,4},{6,5},{7,6},{8,7},{9,8},{10,9... | collective-permute-start | bytes 1376264 | tf_op jit(solution)/shard_map/ppermute | solution.py:472
  8.2 14.8 %collective-permute-start = (f32[8,7,2,8,128]{4,3,2,1,0:T(8,128)}, f32[8,7,2,8,128]{4,3,2,1,0:T(8,128)S(1)}, u32[]{:S(2)}, u32[]{:S(2)}) collective-permute-start(f32[8,7,2,8,128]{4,3,2,1,0:T(8,128)} %shard_map.59.own_ref), channel_id=1, source_target_pairs={{0,1},{1,2},{2,3},{3,4},{4,5},{5,6},{6,7},{7,8},{8,9},{9,10},{10,1... | collective-permute-start | bytes 1376264 | tf_op jit(solution)/shard_map/ppermute | solution.py:472
  9.0 8.8 %collective-permute-start.2 = (f32[2,8,128]{2,1,0:T(8,128)S(1)}, f32[2,8,128]{2,1,0:T(8,128)S(1)}, u32[]{:S(2)}, u32[]{:S(2)}) collective-permute-start(f32[2,8,128]{2,1,0:T(8,128)S(1)} %slice_bitcast_fusion), channel_id=1, source_target_pairs={{0,14},{1,15},{2,0},{3,1},{4,2},{5,3},{6,4},{7,5},{8,6},{9,7},{10,... | collective-permute-start | bytes 24584 | tf_op jit(solution)/shard_map/ppermute | solution.py:472
  17.8 5.2 %copy-start.4 = (f32[2,8,128]{2,1,0:T(8,128)}, f32[2,8,128]{2,1,0:T(8,128)S(1)}, u32[]{:S(2)}) copy-start(f32[2,8,128]{2,1,0:T(8,128)S(1)} %collective-permute-done.2.last_ref) | copy-start | bytes 24580
  17.8 5.2 %copy-start = (f32[8,7,2,8,128]{4,3,2,1,0:T(8,128)}, f32[8,7,2,8,128]{4,3,2,1,0:T(8,128)S(1)}, u32[]{:S(2)}) copy-start(f32[8,7,2,8,128]{4,3,2,1,0:T(8,128)S(1)} %collective-permute-done.1.high_ref) | copy-start | bytes 1376260
  23.0 0.8 copy-start.1
  23.8 7.5 %copy-start.6 = (f32[3,8]{1,0:T(4,128)S(1)}, f32[3,8]{1,0:T(4,128)}, u32[]{:S(2)}) copy-start(f32[3,8]{1,0:T(4,128)} %param.7) | copy-start | bytes 292
  27.9 3.4 %copy-start.5 = (f32[3,8]{1,0:T(4,128)S(1)}, f32[3,8]{1,0:T(4,128)}, u32[]{:S(2)}) copy-start(f32[3,8]{1,0:T(4,128)} %param.6) | copy-start | bytes 292
  27.9 6.1 %collective-permute-start.3 = (f32[22,2,8,128]{3,2,1,0:T(8,128)}, f32[22,2,8,128]{3,2,1,0:T(8,128)S(1)}, u32[]{:S(2)}, u32[]{:S(2)}) collective-permute-start(f32[22,2,8,128]{3,2,1,0:T(8,128)} %get-tuple-element.9), channel_id=1, source_target_pairs={{0,16},{16,32},{32,48},{48,64},{64,80},{80,96},{96,112},{112,0},{1... | collective-permute-start | bytes 540680 | tf_op jit(solution)/shard_map/ppermute | solution.py:472
  31.3 5.1 %collective-permute-start.4 = (f32[22,2,8,128]{3,2,1,0:T(8,128)}, f32[22,2,8,128]{3,2,1,0:T(8,128)S(1)}, u32[]{:S(2)}, u32[]{:S(2)}) collective-permute-start(f32[22,2,8,128]{3,2,1,0:T(8,128)} %get-tuple-element.10), channel_id=1, source_target_pairs={{0,112},{16,0},{32,16},{48,32},{64,48},{80,64},{96,80},{112,96},{1... | collective-permute-start | bytes 540680 | tf_op jit(solution)/shard_map/ppermute | solution.py:472
  34.0 3.0 %copy-start.2 = (f32[22,2,8,128]{3,2,1,0:T(8,128)}, f32[22,2,8,128]{3,2,1,0:T(8,128)S(1)}, u32[]{:S(2)}) copy-start(f32[22,2,8,128]{3,2,1,0:T(8,128)S(1)} %collective-permute-done.3.left_ref) | copy-start | bytes 540676
  36.4 0.7 copy-start.3

commit v2 on v1

--- a/solution.py
+++ b/solution.py
@@ -12,6 +12,7 @@
 HALO = 2 * REACH
 ROWS = SUBS + 2 * HALO
 STRIP = 16
+JOINED = 14
 VMEM_LIMIT = 56 * 2**20
 
 
@@ -80,35 +81,47 @@
     lax.fori_loop(start, stop, lambda i, c: (body(i), c)[1], 0)
 
 
-def pack_kernel(rhs_ref, mat_ref, out_ref):
-    for y in range(SUBS):
+def depth_rows(y, z):
+    return pl.ds(z * SUBS * SUBS + y, SUBS, stride=SUBS)
+
+
+def strip_kernel(rhs_ref, mat_ref, diag_ref, off_ref, left_ref, right_ref, own_mat_ref, table_ref):
+    lane = lax.broadcasted_iota(jnp.int32, (SUBS, LANES), 1)
+    for z in range(2):
+        for r in range(SUBS):
+            own_mat_ref[r, z] = mat_ref[depth_rows(r, z), :].astype(jnp.float32)
+    for c in range(7):
         for z in range(2):
-            rows = pl.ds(z * 64 + y, SUBS, stride=SUBS)
-            for c in range(6):
-                out_ref[y, c, z] = rhs_ref[c, rows, :]
-            out_ref[y, 6, z] = mat_ref[rows, :].astype(jnp.float32)
-
-
-def strip_kernel(low_ref, own_ref, high_ref, last_ref, left_ref, right_ref):
-    lane = lax.broadcasted_iota(jnp.int32, (SUBS, LANES), 1)
-    for group, ref in enumerate((low_ref, own_ref, high_ref)):
-
-        def channel(c, ref=ref, group=group):
-            for z in range(2):
-                left = ref[0, c, z]
-                right = pltpu.roll(left, STRIP, 1)
-                for r in range(1, SUBS):
-                    tile = ref[r, c, z]
-                    here = (lane >= STRIP * r) & (lane < STRIP * (r + 1))
-                    left = jnp.where(here, pltpu.roll(tile, STRIP * r, 1), left)
-                    right = jnp.where(here, pltpu.roll(tile, (STRIP * (r + 1)) % LANES, 1), right)
-                left_ref[group * 7 + c, z] = left
-                right_ref[group * 7 + c, z] = right
-
-        loop(0, 7, channel)
-    for z in range(2):
-        left_ref[21, z] = last_ref[z]
-        right_ref[21, z] = pltpu.roll(last_ref[z], STRIP, 1)
+            for r in range(SUBS):
+                tile = own_mat_ref[r, z] if c == 6 else rhs_ref[c, depth_rows(r, z), :]
+                west = pltpu.roll(tile, STRIP * r, 1) if r else tile
+                east = pltpu.roll(tile, STRIP * (r + 1), 1) if r < SUBS - 1 else tile
+                if r == 0:
+                    left, right = west, east
+                else:
+                    here = lane >= STRIP * r
+                    left, right = jnp.where(here, west, left), jnp.where(here, east, right)
+            left_ref[c, z] = left
+            right_ref[c, z] = right
+    x, n, d = [jnp.broadcast_to(0.5 * diag_ref[c : c + 1, :], (SUBS, SUBS)) for c in range(3)]
+    entries = [x, n, d]
+    for c, (f, g) in enumerate(((x, n), (x, d), (n, d))):
+        entries.append(jnp.broadcast_to(off_ref[c : c + 1, :], (SUBS, SUBS)) * jnp.sqrt(f * g))
+    for c in range(6):
+        table_ref[c, :, :] = jnp.zeros((SUBS, LANES), jnp.float32)
+        table_ref[c, :, :SUBS] = entries[c]
+
+
+def wavefront(stages):
+    edges = sorted({e + lag for _, start, stop, lag in stages for e in (start, stop)})
+    for start, stop in zip(edges, edges[1:]):
+        active = [st for st in stages if st[1] + st[3] <= start and stop <= st[2] + st[3]]
+
+        def step(s, active=active):
+            for body, _, _, lag in reversed(active):
+                body(s - lag)
+
+        loop(start, stop, step)
 
 
 def iterate(sh, v, out, u, s2, coef, z1, t1, p, node, flux, a, b):
@@ -168,7 +181,8 @@
         for c, value in enumerate(values):
             put(ref, row, base + c, value)
 
-    store(z1, a, jacobi(a, load(v, a), 0.7))
+    def zeroth(y):
+        store(z1, y, jacobi(y, load(v, y), 0.7))
 
     def first(y):
         ahead = jacobi(y + 1, load(v, y + 1), 0.7)
@@ -177,8 +191,6 @@
         rest = [r - w for r, w in zip(load(v, y), applied)]
         store(t1, y, rest)
         store(p, y, jacobi(y, rest, 0.6))
-
-    loop(a, b - 1, first)
 
     def second(y):
         applied = operator(y, load(p, y), load(p, y + 1))
@@ -191,8 +203,6 @@
             source.append(((sh.west(x) - x) + (before - n)) + (sh.below(d) - d))
         store(node, y, source)
         store(node, y, nodal(y, source, 0.8), 2)
-
-    loop(a + 1, b - 2, second)
 
     def third(y):
         w = [get(node, y, 2 + part) for part in range(2)]
@@ -215,8 +225,6 @@
         fix = nodal(y, rest, 0.5)
         store(node, y, [w[part] + fix[part] for part in range(2)], 4)
 
-    loop(a + 2, b - 3, third)
-
     def lift(y):
         w = [get(node, y, 4 + part) for part in range(2)]
         result = []
@@ -233,13 +241,18 @@
         store(u, y, result)
         return result
 
-    lift(a + 3)
-
     def fourth(y):
         ahead = lift(y + 1)
         store(out, y, operator(y, load(u, y), ahead))
 
-    loop(a + 3, b - 4, fourth)
+    return [
+        (zeroth, a, a + 1, 0),
+        (first, a, b - 1, 1),
+        (second, a + 1, b - 2, 3),
+        (third, a + 2, b - 3, 5),
+        (lift, a + 3, a + 4, 7),
+        (fourth, a + 3, b - 4, 8),
+    ]
 
 
 def two_sum(a, b):
@@ -249,7 +262,7 @@
 
 
 def main_kernel(
-    low_ref, own_ref, high_ref, last_ref, left_ref, right_ref, table_ref,
+    low_ref, own_ref, high_ref, near_low_ref, near_high_ref, last_ref, left_ref, right_ref, own_mat_ref, table_ref,
     a0_ref, a1_ref, sums_ref,
     v, c0, c1, u0, u1, mat, pair, s2, coef, z1, t1, p, node, flux,
 ):
@@ -257,34 +270,42 @@
     lane = lax.broadcasted_iota(jnp.int32, (SUBS, LANES), 1)
     near = lane < LANES // 2
 
-    def halo(strip, z, r):
-        east = pltpu.roll(right_ref[strip, z], lax.rem(LANES - STRIP * r, LANES), 1)
-        west = pltpu.roll(left_ref[strip, z], lax.rem(2 * LANES - STRIP - STRIP * r, LANES), 1)
+    def halo(left, right, r):
+        east = pltpu.roll(right, lax.rem(LANES - STRIP * r, LANES), 1)
+        west = pltpu.roll(left, lax.rem(2 * LANES - STRIP - STRIP * r, LANES), 1)
         return jnp.where(near, east, west)
 
-    for group, ref in enumerate((low_ref, own_ref, high_ref)):
-
-        def unpack(r, ref=ref, group=group):
-            y = group * SUBS + r
+    def unpack(group, rhs, strips, cells):
+        def body(y):
+            r = y - group * SUBS
             for z in range(2):
                 for c in range(6):
-                    v[y, c, 2 * z] = ref[r, c, z]
-                    v[y, c, 2 * z + 1] = halo(group * 7 + c, z, r)
-                mat[y, 2 * z] = ref[r, 6, z]
-                mat[y, 2 * z + 1] = halo(group * 7 + 6, z, r)
-
-        loop(0, SUBS, unpack)
-    for z in range(2):
-        mat[ROWS, 2 * z] = last_ref[z]
-        mat[ROWS, 2 * z + 1] = halo(21, z, 0)
+                    v[y, c, 2 * z] = rhs[c, depth_rows(r, z), :]
+                    v[y, c, 2 * z + 1] = halo(*strips(c, z), r)
+                mat[y, 2 * z] = cells(r, z)
+                mat[y, 2 * z + 1] = halo(*strips(6, z), r)
+
+        return (body, group * SUBS, group * SUBS + SUBS, 0)
+
+    def own_strips(c, z):
+        return left_ref[c, z], right_ref[c, z]
+
+    def strips_of(ref):
+        return lambda c, z: (ref[2 * c + z], ref[JOINED + 2 * c + z])
+
+    def cells_of(ref):
+        return lambda r, z: ref[2 * JOINED + 2 * r + z]
+
+    def beyond(y):
+        for z in range(2):
+            mat[y, 2 * z] = last_ref[4 + z]
+            mat[y, 2 * z + 1] = halo(last_ref[z], last_ref[2 + z], 0)
 
     def pairs(y):
         ids = [mat[y, k].astype(jnp.int32) for k in range(4)]
         for c in range(6):
             cell = Field(jnp.take_along_axis(table_ref[c], i, axis=1) for i in ids)
             put(pair, y, c, cell + sh.east(cell))
-
-    loop(0, ROWS + 1, pairs)
 
     def tensors(y):
         s = [get(pair, y, c) + get(pair, y + 1, c) for c in range(6)]
@@ -299,10 +320,18 @@
         put(coef, y, 6, 6.0 * inverse)
         put(coef, y, 7, shift * inverse)
 
-    loop(0, ROWS, tensors)
-
-    iterate(sh, v, c0, u0, s2, coef, z1, t1, p, node, flux, 0, ROWS)
-    iterate(sh, c0, c1, u1, s2, coef, z1, t1, p, node, flux, REACH, ROWS - REACH)
+    wavefront(
+        [
+            unpack(0, low_ref, strips_of(near_low_ref), cells_of(near_low_ref)),
+            unpack(1, own_ref, own_strips, lambda r, z: own_mat_ref[r, z]),
+            unpack(2, high_ref, strips_of(near_high_ref), cells_of(near_high_ref)),
+            (beyond, ROWS, ROWS + 1, 0),
+            (pairs, 0, ROWS + 1, 1),
+            (tensors, 0, ROWS, 3),
+        ]
+    )
+    wavefront(iterate(sh, v, c0, u0, s2, coef, z1, t1, p, node, flux, 0, ROWS))
+    wavefront(iterate(sh, c0, c1, u1, s2, coef, z1, t1, p, node, flux, REACH, ROWS - REACH))
 
     def dots(r, sums):
         y = HALO + r
@@ -375,7 +404,7 @@
     return quick(q, (r[0] + r[1]) / y[0])
 
 
-def final_kernel(sums_ref, a0_ref, a1_ref, out_ref, hess_ref):
+def final_kernel(sums_ref, a0_ref, a1_ref, result_ref, hess_ref, out_ref, done):
     lane = lax.broadcasted_iota(jnp.int32, (SUBS, LANES), 1)
     sub = lax.broadcasted_iota(jnp.int32, (SUBS, LANES), 0)
     total = sums_ref[pl.ds(0, SUBS), :]
@@ -432,27 +461,15 @@
     table = jnp.where(sub == 0, jnp.where(lane == 0, e00, e01), jnp.where(lane == 0, e10, e11))
     table = jnp.where(sub == 2, jnp.where(lane == 0, 0.0, e21), table)
     hess_ref[...] = table[:3, :2]
-    for row in range(SUBS):
-        for z in range(2):
-            rows = pl.ds(z * 64 + row, SUBS, stride=SUBS)
-            for c in range(6):
-                out_ref[c, rows, :] = k0 * a0_ref[row, c, z] + k1 * a1_ref[row, c, z]
-
-
-def tensor_table(sigma_diag, sigma_off):
-    along_east = sigma_diag[0]
-    along_north = sigma_diag[1]
-    along_depth = sigma_diag[2]
-    return jnp.stack(
-        [
-            along_east,
-            along_north,
-            along_depth,
-            sigma_off[0] * jnp.sqrt(along_east * along_north),
-            sigma_off[1] * jnp.sqrt(along_east * along_depth),
-            sigma_off[2] * jnp.sqrt(along_north * along_depth),
-        ]
-    )
+    copies = []
+    for c in range(6):
+        for row in range(SUBS):
+            for z in range(2):
+                out_ref[c, depth_rows(row, z), :] = k0 * a0_ref[row, c, z] + k1 * a1_ref[row, c, z]
+        copies.append(pltpu.make_async_copy(out_ref.at[c], result_ref.at[c], done.at[c]))
+        copies[-1].start()
+    for copy in copies:
+        copy.wait()
 
 
 def call(kernel, outs, scratch=(), n=0):
@@ -473,18 +490,22 @@
 
 
 def on_device(right_side, materials, sigma_diag, sigma_off):
-    table = jnp.pad(0.5 * tensor_table(sigma_diag, sigma_off), ((0, 0), (0, LANES - 8)))
-    table = jnp.broadcast_to(table[:, None, :], (6, SUBS, LANES))
     tile = (SUBS, LANES)
-    (own,) = call(pack_kernel, [(SUBS, 7, 2) + tile], n=2)(
-        right_side.reshape(6, LANES, LANES), materials.reshape(LANES, LANES)
-    )
-    low = moved(own, "gy", 1)
-    high = moved(own, "gy", -1)
-    last = moved(own[0, 6], "gy", -2)
-    to_left, to_right = call(strip_kernel, [(22, 2) + tile] * 2, n=4)(low, own, high, last)
+    rhs = right_side.reshape(6, LANES, LANES)
+    low = moved(rhs, "gy", 1)
+    high = moved(rhs, "gy", -1)
+    to_left, to_right, cells, table = call(
+        strip_kernel, [(7, 2) + tile] * 2 + [(SUBS, 2) + tile, (6,) + tile], n=4
+    )(rhs, materials.reshape(LANES, LANES), sigma_diag, sigma_off)
     from_right = moved(to_left, "gx", -1)
     from_left = moved(to_right, "gx", 1)
+    joined = jnp.concatenate([part.reshape((-1,) + tile) for part in (from_left, from_right, cells)])
+    near_low = moved(joined, "gy", 1)
+    near_high = moved(joined, "gy", -1)
+    first_row = jnp.concatenate(
+        [joined[k : k + 2] for k in (JOINED - 2, 2 * JOINED - 2, 2 * JOINED)]
+    )
+    last = moved(first_row, "gy", -2)
 
     def rows(n, extra=0):
         return (ROWS + extra, n, 4) + tile
@@ -496,11 +517,22 @@
         + [(ROWS + 1, 4) + tile, rows(6, 1), rows(6), rows(8)]
         + [rows(6)] * 3
         + [rows(8, 1), rows(4, 1)],
-        n=7,
-    )(low, own, high, last, from_left, from_right, table)
+        n=10,
+    )(low, rhs, high, near_low, near_high, last, from_left, from_right, cells, table)
     gathered = lax.all_to_all(sums, ("gx", "gy"), 0, 0, tiled=True)
-    solution_rows, hessenberg = call(final_kernel, [(6, LANES, LANES), (3, 2)], n=3)(gathered, a0, a1)
-    return solution_rows.reshape(right_side.shape), hessenberg
+    vmem = pl.BlockSpec(memory_space=pltpu.VMEM)
+    result, hessenberg = pl.pallas_call(
+        final_kernel,
+        out_shape=[
+            jax.ShapeDtypeStruct((6, LANES, LANES), jnp.float32),
+            jax.ShapeDtypeStruct((3, 2), jnp.float32),
+        ],
+        in_specs=[vmem] * 3,
+        out_specs=[pl.BlockSpec(memory_space=pl.ANY), vmem],
+        scratch_shapes=[pltpu.VMEM((6, LANES, LANES), jnp.float32), pltpu.SemaphoreType.DMA((6,))],
+        compiler_params=pltpu.CompilerParams(vmem_limit_bytes=VMEM_LIMIT),
+    )(gathered, a0, a1)
+    return result.reshape(right_side.shape), hessenberg
 
 
 def solution(mesh):

time: 89.6 us -> 72.5 us (0.81)
  Pallas kernels: 41.4 us -> 25 us
  waiting for transfers between devices: 17.4 us -> 12.3 us
  starting transfers between devices: 10.8 us -> 14.7 us
    pallas_call x1, Pallas kernels: 33.1 us -> 20.1 us  [on_device(): call(main_kernel, [(SUBS, 6, 2) + tile, (SUBS, 6, 2) + tile, (LANES, LANE...]
    ppermute x5 -> x7, waiting for transfers between devices: 17.4 us -> 12.3 us  [moved(): lax.ppermute(value, axis, [(i, (i + step) % size) for i in range(size)])]
    ppermute x5 -> x7, starting transfers between devices: 10.8 us -> 14.7 us  [moved(): lax.ppermute(value, axis, [(i, (i + step) % size) for i in range(size)])]
    pallas_call x3 -> x2, Pallas kernels: 8.3 us -> 4.92 us  [the longest x1 2.92 us: on_device(): pl.pallas_call(final_kernel, out_shape=[jax.ShapeDtypeStruct((6, LANES, L...]
  transfers between devices with their start and end apart: 5 -> 7, of which waited for: 4 -> 4; matrix products, arithmetic and copies ran while one was open for 1% -> 2% of each run, Pallas kernels for 0% -> 3%
where the time goes in v2:
time: 72.5 us; the launch traced here: 72.2 us
  Pallas kernels  25 us (34%)
  blocking collectives  15.7 us (22%)
  starting transfers between devices  14.7 us (20%)
  waiting for transfers between devices  12.3 us (17%)
  local copies, waits for them, and re-layouts  2.94 us (4%)
  other arithmetic  0.88 us (1%)
    pallas_call x1, Pallas kernels, on_device(): call(main_kernel, [(SUBS, 6, 2) + tile, (SUBS, 6, 2) + tile, (LANES, LANE...  20.1 us
    all_to_all x1, blocking collectives, on_device(): gathered = lax.all_to_all(sums, ('gx', 'gy'), 0, 0, tiled=True)  15.7 us
    ppermute x7, starting transfers between devices, moved(): lax.ppermute(value, axis, [(i, (i + step) % size) for i in range(size)])  14.7 us
    ppermute x7, waiting for transfers between devices, moved(): lax.ppermute(value, axis, [(i, (i + step) % size) for i in range(size)])  12.3 us
    pallas_call x1, Pallas kernels, on_device(): pl.pallas_call(final_kernel, out_shape=[jax.ShapeDtypeStruct((6, LANES, L...  2.92 us
    unnamed x15, local copies, waits for them, and re-layouts  2.24 us
    pallas_call x1, Pallas kernels, on_device(): call(strip_kernel, [(7, 2) + tile] * 2 + [(SUBS, 2) + tile, (6,) + tile],...  2.01 us
  transfers between devices with their start and end apart: 7, of which 4 were waited for; matrix products, arithmetic and copies ran while one was open for 2% of the time, Pallas kernels for 3%

profile of v2, /device:TPU:1, one launch (start us, length us, event | category | flops | bytes accessed | tf_op | source)
XLA Modules:
  0.0 72.2 jit_solution(2281440757591562948)
XLA Ops:
  0.6 5.8 %collective-permute-start.1 = (f32[6,128,128]{2,1,0:T(8,128)}, f32[6,128,128]{2,1,0:T(8,128)S(1)}, u32[]{:S(2)}, u32[]{:S(2)}) collective-permute-start(f32[6,128,128]{2,1,0:T(8,128)} %bitcast.16), channel_id=1, source_target_pairs={{0,15},{1,0},{2,1},{3,2},{4,3},{5,4},{6,5},{7,6},{8,7},{9,8},{10,9... | collective-permute-start | bytes 1179656 | tf_op jit(solution)/shard_map/ppermute | solution.py:489
  6.5 0.0 collective-permute-start
  6.5 2.0 %shard_map.59 = (f32[7,2,8,128]{3,2,1,0:T(8,128)}, f32[7,2,8,128]{3,2,1,0:T(8,128)}, f32[8,2,8,128]{3,2,1,0:T(8,128)}, f32[6,8,128]{2,1,0:T(8,128)}) custom-call(f32[6,128,128]{2,1,0:T(8,128)} %bitcast.18, s32[128,128]{1,0:T(8,128)} %bitcast.24, f32[3,8]{1,0:T(4,128)} %diag_ref.1, f32[3,8]{1,0:T(4,128)} %off_ref.1), custom_call_target="tpu_custom_call" | custom-call | tf_op jit(solution)/shard_map/pallas_call | solution.py:497
  8.5 2.5 %collective-permute-start.2 = (f32[7,2,8,128]{3,2,1,0:T(8,128)}, f32[7,2,8,128]{3,2,1,0:T(8,128)S(1)}, u32[]{:S(2)}, u32[]{:S(2)}) collective-permute-start(f32[7,2,8,128]{3,2,1,0:T(8,128)} %get-tuple-element.11), channel_id=1, source_target_pairs={{0,16},{16,32},{32,48},{48,64},{64,80},{80,96},{96,112},{112,0},{1... | collective-permute-start | bytes 172040 | tf_op jit(solution)/shard_map/ppermute | solution.py:489
  10.9 0.0 collective-permute-start.3
  10.9 0.7 slice_bitcast_fusion.2
  11.6 0.9 %collective-permute-done.2.left_ref = f32[7,2,8,128]{3,2,1,0:T(8,128)S(1)} collective-permute-done((f32[7,2,8,128]{3,2,1,0:T(8,128)}, f32[7,2,8,128]{3,2,1,0:T(8,128)S(1)}, u32[]{:S(2)}, u32[]{:S(2)}) %collective-permute-start.2) | collective-permute-done | bytes 57376 | tf_op jit(solution)/shard_map/ppermute | solution.py:489
  12.5 0.0 copy-start.2
  12.5 2.5 %collective-permute-done.3.right_ref = f32[7,2,8,128]{3,2,1,0:T(8,128)S(1)} collective-permute-done((f32[7,2,8,128]{3,2,1,0:T(8,128)}, f32[7,2,8,128]{3,2,1,0:T(8,128)S(1)}, u32[]{:S(2)}, u32[]{:S(2)}) %collective-permute-start.3) | collective-permute-done | bytes 57376 | tf_op jit(solution)/shard_map/ppermute | solution.py:489
  15.1 0.0 copy-start.3
  15.1 0.9 %pad_maximum_fusion = f32[44,8,128]{2,1,0:T(8,128)S(1)} fusion(f32[16,8,128]{2,1,0:T(8,128)} %bitcast.20, f32[14,8,128]{2,1,0:T(8,128)S(1)} %bitcast.22, f32[14,8,128]{2,1,0:T(8,128)S(1)} %bitcast.21), kind=kLoop, calls=%fused_computation | loop fusion | flops 90112 | bytes 360448 | tf_op jit(solution)/shard_map/concatenate | solution.py:502
  15.9 5.1 %collective-permute-start.5 = (f32[44,8,128]{2,1,0:T(8,128)S(1)}, f32[44,8,128]{2,1,0:T(8,128)S(1)}, u32[]{:S(2)}, u32[]{:S(2)}) collective-permute-start(f32[44,8,128]{2,1,0:T(8,128)S(1)} %pad_maximum_fusion), channel_id=1, source_target_pairs={{0,15},{1,0},{2,1},{3,2},{4,3},{5,4},{6,5},{7,6},{8,7},{9,8},{10,9... | collective-permute-start | bytes 540680 | tf_op jit(solution)/shard_map/ppermute | solution.py:489
  21.0 0.0 collective-permute-start.4
  21.0 0.0 copy-done.2
  21.0 0.0 copy-done.3
  21.1 1.3 %collective-permute-start.6 = (f32[6,8,128]{2,1,0:T(8,128)S(1)}, f32[6,8,128]{2,1,0:T(8,128)S(1)}, u32[]{:S(2)}, u32[]{:S(2)}) collective-permute-start(f32[6,8,128]{2,1,0:T(8,128)S(1)} %pad_maximum_fusion.1), channel_id=1, source_target_pairs={{0,14},{1,15},{2,0},{3,1},{4,2},{5,3},{6,4},{7,5},{8,6},{9,7},{10,... | collective-permute-start | bytes 73736 | tf_op jit(solution)/shard_map/ppermute | solution.py:489
  22.4 3.5 %collective-permute-done.6.last_ref = f32[6,8,128]{2,1,0:T(8,128)S(1)} collective-permute-done((f32[6,8,128]{2,1,0:T(8,128)S(1)}, f32[6,8,128]{2,1,0:T(8,128)S(1)}, u32[]{:S(2)}, u32[]{:S(2)}) %collective-permute-start.6) | collective-permute-done | bytes 24608 | tf_op jit(solution)/shard_map/ppermute | solution.py:489
  25.9 0.0 copy-start.6
  25.9 0.0 collective-permute-done.5.near_high_ref
  25.9 0.0 copy-start.4
  25.9 5.3 %collective-permute-done.4.near_low_ref = f32[44,8,128]{2,1,0:T(8,128)S(1)} collective-permute-done((f32[44,8,128]{2,1,0:T(8,128)S(1)}, f32[44,8,128]{2,1,0:T(8,128)S(1)}, u32[]{:S(2)}, u32[]{:S(2)}) %collective-permute-start.4) | collective-permute-done | bytes 180256 | tf_op jit(solution)/shard_map/ppermute | solution.py:489
  31.2 0.0 copy-start.5
  31.2 0.0 collective-permute-done.1.high_ref
  31.2 0.0 copy-start
  31.2 0.0 collective-permute-done.low_ref
  31.3 0.0 copy-start.1
  31.3 0.0 copy-done.6
  31.3 0.0 copy-done.4
  31.3 0.6 copy-done.5
  31.9 0.1 copy-done
  32.1 0.1 copy-done.1
  32.2 20.1 %shard_map.60 = (f32[8,6,2,8,128]{4,3,2,1,0:T(8,128)}, f32[8,6,2,8,128]{4,3,2,1,0:T(8,128)}, f32[128,128]{1,0:T(8,128)}) custom-call(f32[6,128,128]{2,1,0:T(8,128)} %copy-done.1, f32[6,128,128]{2,1,0:T(8,128)} %bitcast.19, f32[6,128,128]{2,1,0:T(8,128)} %copy-done, f32[44,8,128]{2,1,0:T(8,128)} %copy-done.5, f32[44,8,128]{2,1,0:T(8,128)} %copy-done.4, ...), custom_call_target="tpu_custom_call" | custom-call | tf_op jit(solution)/shard_map/pallas_call | solution.py:513
  52.3 15.7 %all_to_all.11 = f32[128,1,128]{2,1,0:T(1,128)} all-to-all(f32[128,1,128]{2,1,0:T(1,128)} %bitcast.25), channel_id=1, replica_groups=mesh['gx'=8,'gy'=16] {'gx','gy'}, dimensions={0} | all-to-all | bytes 131072 | tf_op jit(solution)/shard_map/all_to_all | solution.py:522
  67.9 2.9 %shard_map.61 = (f32[6,128,128]{2,1,0:T(8,128)}, f32[3,2]{1,0:T(4,128)}) custom-call(f32[128,128]{1,0:T(8,128)} %bitcast.23, f32[8,6,2,8,128]{4,3,2,1,0:T(8,128)} %get-tuple-element.16.a0_ref, f32[8,6,2,8,128]{4,3,2,1,0:T(8,128)} %get-tuple-element.17.a1_ref), custom_call_target="tpu_custom_call" | custom-call | tf_op jit(solution)/shard_map/pallas_call | solution.py:524
  70.8 1.3 %copy.8 = f32[3,2]{0,1:T(2,128)} copy(f32[3,2]{1,0:T(4,128)} %get-tuple-element.23) | data formatting | bytes 48
  (3 shorter events, 0.0 us)
Async XLA Ops:
  0.6 30.6 %collective-permute-start.1 = (f32[6,128,128]{2,1,0:T(8,128)}, f32[6,128,128]{2,1,0:T(8,128)S(1)}, u32[]{:S(2)}, u32[]{:S(2)}) collective-permute-start(f32[6,128,128]{2,1,0:T(8,128)} %bitcast.16), channel_id=1, source_target_pairs={{0,15},{1,0},{2,1},{3,2},{4,3},{5,4},{6,5},{7,6},{8,7},{9,8},{10,9... | collective-permute-start | bytes 1179656 | tf_op jit(solution)/shard_map/ppermute | solution.py:489
  6.5 24.8 %collective-permute-start = (f32[6,128,128]{2,1,0:T(8,128)}, f32[6,128,128]{2,1,0:T(8,128)S(1)}, u32[]{:S(2)}, u32[]{:S(2)}) collective-permute-start(f32[6,128,128]{2,1,0:T(8,128)} %bitcast.17), channel_id=1, source_target_pairs={{0,1},{1,2},{2,3},{3,4},{4,5},{5,6},{6,7},{7,8},{8,9},{9,10},{10,1... | collective-permute-start | bytes 1179656 | tf_op jit(solution)/shard_map/ppermute | solution.py:489
  8.5 4.0 %collective-permute-start.2 = (f32[7,2,8,128]{3,2,1,0:T(8,128)}, f32[7,2,8,128]{3,2,1,0:T(8,128)S(1)}, u32[]{:S(2)}, u32[]{:S(2)}) collective-permute-start(f32[7,2,8,128]{3,2,1,0:T(8,128)} %get-tuple-element.11), channel_id=1, source_target_pairs={{0,16},{16,32},{32,48},{48,64},{64,80},{80,96},{96,112},{112,0},{1... | collective-permute-start | bytes 172040 | tf_op jit(solution)/shard_map/ppermute | solution.py:489
  10.9 4.1 %collective-permute-start.3 = (f32[7,2,8,128]{3,2,1,0:T(8,128)}, f32[7,2,8,128]{3,2,1,0:T(8,128)S(1)}, u32[]{:S(2)}, u32[]{:S(2)}) collective-permute-start(f32[7,2,8,128]{3,2,1,0:T(8,128)} %get-tuple-element.12), channel_id=1, source_target_pairs={{0,112},{16,0},{32,16},{48,32},{64,48},{80,64},{96,80},{112,96},{1... | collective-permute-start | bytes 172040 | tf_op jit(solution)/shard_map/ppermute | solution.py:489
  12.5 8.5 %copy-start.2 = (f32[7,2,8,128]{3,2,1,0:T(8,128)}, f32[7,2,8,128]{3,2,1,0:T(8,128)S(1)}, u32[]{:S(2)}) copy-start(f32[7,2,8,128]{3,2,1,0:T(8,128)S(1)} %collective-permute-done.2.left_ref) | copy-start | bytes 172036
  15.1 6.0 %copy-start.3 = (f32[7,2,8,128]{3,2,1,0:T(8,128)}, f32[7,2,8,128]{3,2,1,0:T(8,128)S(1)}, u32[]{:S(2)}) copy-start(f32[7,2,8,128]{3,2,1,0:T(8,128)S(1)} %collective-permute-done.3.right_ref) | copy-start | bytes 172036
  15.9 10.0 %collective-permute-start.5 = (f32[44,8,128]{2,1,0:T(8,128)S(1)}, f32[44,8,128]{2,1,0:T(8,128)S(1)}, u32[]{:S(2)}, u32[]{:S(2)}) collective-permute-start(f32[44,8,128]{2,1,0:T(8,128)S(1)} %pad_maximum_fusion), channel_id=1, source_target_pairs={{0,15},{1,0},{2,1},{3,2},{4,3},{5,4},{6,5},{7,6},{8,7},{9,8},{10,9... | collective-permute-start | bytes 540680 | tf_op jit(solution)/shard_map/ppermute | solution.py:489
  21.0 10.2 %collective-permute-start.4 = (f32[44,8,128]{2,1,0:T(8,128)S(1)}, f32[44,8,128]{2,1,0:T(8,128)S(1)}, u32[]{:S(2)}, u32[]{:S(2)}) collective-permute-start(f32[44,8,128]{2,1,0:T(8,128)S(1)} %pad_maximum_fusion), channel_id=1, source_target_pairs={{0,1},{1,2},{2,3},{3,4},{4,5},{5,6},{6,7},{7,8},{8,9},{9,10},{10,1... | collective-permute-start | bytes 540680 | tf_op jit(solution)/shard_map/ppermute | solution.py:489
  21.1 4.9 %collective-permute-start.6 = (f32[6,8,128]{2,1,0:T(8,128)S(1)}, f32[6,8,128]{2,1,0:T(8,128)S(1)}, u32[]{:S(2)}, u32[]{:S(2)}) collective-permute-start(f32[6,8,128]{2,1,0:T(8,128)S(1)} %pad_maximum_fusion.1), channel_id=1, source_target_pairs={{0,14},{1,15},{2,0},{3,1},{4,2},{5,3},{6,4},{7,5},{8,6},{9,7},{10,... | collective-permute-start | bytes 73736 | tf_op jit(solution)/shard_map/ppermute | solution.py:489
  25.9 5.3 %copy-start.6 = (f32[6,8,128]{2,1,0:T(8,128)}, f32[6,8,128]{2,1,0:T(8,128)S(1)}, u32[]{:S(2)}) copy-start(f32[6,8,128]{2,1,0:T(8,128)S(1)} %collective-permute-done.6.last_ref) | copy-start | bytes 73732
  25.9 5.3 %copy-start.4 = (f32[44,8,128]{2,1,0:T(8,128)}, f32[44,8,128]{2,1,0:T(8,128)S(1)}, u32[]{:S(2)}) copy-start(f32[44,8,128]{2,1,0:T(8,128)S(1)} %collective-permute-done.5.near_high_ref) | copy-start | bytes 540676
  31.2 0.7 copy-start.5
  31.2 0.8 %copy-start = (f32[6,128,128]{2,1,0:T(8,128)}, f32[6,128,128]{2,1,0:T(8,128)S(1)}, u32[]{:S(2)}) copy-start(f32[6,128,128]{2,1,0:T(8,128)S(1)} %collective-permute-done.1.high_ref) | copy-start | bytes 1179652
  31.3 0.9 %copy-start.1 = (f32[6,128,128]{2,1,0:T(8,128)}, f32[6,128,128]{2,1,0:T(8,128)S(1)}, u32[]{:S(2)}) copy-start(f32[6,128,128]{2,1,0:T(8,128)S(1)} %collective-permute-done.low_ref) | copy-start | bytes 1179652

commit v3 on v2

--- a/solution.py
+++ b/solution.py
@@ -12,8 +12,8 @@
 HALO = 2 * REACH
 ROWS = SUBS + 2 * HALO
 STRIP = 16
-JOINED = 14
-VMEM_LIMIT = 56 * 2**20
+PACK = 32
+VMEM_LIMIT = 44 * 2**20
 
 
 class Field:
@@ -85,24 +85,26 @@
     return pl.ds(z * SUBS * SUBS + y, SUBS, stride=SUBS)
 
 
-def strip_kernel(rhs_ref, mat_ref, diag_ref, off_ref, left_ref, right_ref, own_mat_ref, table_ref):
+def strip_kernel(rhs_ref, mat_ref, diag_ref, off_ref, strip_ref, cells_ref, table_ref):
     lane = lax.broadcasted_iota(jnp.int32, (SUBS, LANES), 1)
+    half = STRIP // 2
+
+    def packed(tiles, offset):
+        result = None
+        for r, tile in enumerate(tiles):
+            shift = (STRIP * r + offset) % LANES
+            moved_tile = pltpu.roll(tile, shift, 1) if shift else tile
+            result = moved_tile if r == 0 else jnp.where(lane >= STRIP * r, moved_tile, result)
+        return result
+
     for z in range(2):
+        cells = [mat_ref[depth_rows(r, z), :].astype(jnp.float32) for r in range(SUBS)]
         for r in range(SUBS):
-            own_mat_ref[r, z] = mat_ref[depth_rows(r, z), :].astype(jnp.float32)
-    for c in range(7):
-        for z in range(2):
-            for r in range(SUBS):
-                tile = own_mat_ref[r, z] if c == 6 else rhs_ref[c, depth_rows(r, z), :]
-                west = pltpu.roll(tile, STRIP * r, 1) if r else tile
-                east = pltpu.roll(tile, STRIP * (r + 1), 1) if r < SUBS - 1 else tile
-                if r == 0:
-                    left, right = west, east
-                else:
-                    here = lane >= STRIP * r
-                    left, right = jnp.where(here, west, left), jnp.where(here, east, right)
-            left_ref[c, z] = left
-            right_ref[c, z] = right
+            cells_ref[2 * r + z] = cells[r]
+        strip_ref[12 + z] = packed(cells, half)
+        strip_ref[14 + z] = packed(cells, 0)
+        for c in range(6):
+            strip_ref[2 * c + z] = packed([rhs_ref[c, depth_rows(r, z), :] for r in range(SUBS)], half)
     x, n, d = [jnp.broadcast_to(0.5 * diag_ref[c : c + 1, :], (SUBS, SUBS)) for c in range(3)]
     entries = [x, n, d]
     for c, (f, g) in enumerate(((x, n), (x, d), (n, d))):
@@ -110,11 +112,20 @@
     for c in range(6):
         table_ref[c, :, :] = jnp.zeros((SUBS, LANES), jnp.float32)
         table_ref[c, :, :SUBS] = entries[c]
-
-
-def wavefront(stages):
-    edges = sorted({e + lag for _, start, stop, lag in stages for e in (start, stop)})
+    for c in range(6):
+        single = table_ref[c]
+        table_ref[c] = jnp.take_along_axis(single, lane // SUBS, axis=1) + jnp.take_along_axis(
+            single, lane % SUBS, axis=1
+        )
+
+
+def wavefront(stages, events=()):
+    edges = {e + lag for _, start, stop, lag in stages for e in (start, stop)}
+    edges = sorted(edges | {at for at, _ in events})
     for start, stop in zip(edges, edges[1:]):
+        for at, body in events:
+            if at == start:
+                body()
         active = [st for st in stages if st[1] + st[3] <= start and stop <= st[2] + st[3]]
 
         def step(s, active=active):
@@ -124,7 +135,7 @@
         loop(start, stop, step)
 
 
-def iterate(sh, v, out, u, s2, coef, z1, t1, p, node, flux, a, b):
+def iterate(sh, v, out, u, keep, s2, coef, z1, t1, p, node, flux, a, b):
     def fluxes(e, above_row):
         bx = (above_row[1] - e[2]) - (sh.above(e[1]) - e[1])
         by = (sh.above(e[0]) - e[0]) - (sh.east(e[2]) - e[2])
@@ -239,6 +250,9 @@
                     slope = sh.above(w[part]) - w[part]
                 result.append((get(z1, y, k) + get(p, y, k)) + slope)
         store(u, y, result)
+        for k in range(6):
+            for z in range(2):
+                keep[y, k, z] = result[k].parts[2 * z]
         return result
 
     def fourth(y):
@@ -262,50 +276,69 @@
 
 
 def main_kernel(
-    low_ref, own_ref, high_ref, near_low_ref, near_high_ref, last_ref, left_ref, right_ref, own_mat_ref, table_ref,
+    low_ref, own_ref, high_ref, low_pack_ref, own_pack_ref, high_pack_ref, last_ref, table_ref,
     a0_ref, a1_ref, sums_ref,
-    v, c0, c1, u0, u1, mat, pair, s2, coef, z1, t1, p, node, flux,
+    v, c0, c1, u, mat, index, pair, s2, coef, z1, t1, p, node, flux,
+    keep0, keep1, bulk, packs, last, table, arrived, left,
 ):
     sh = Shifts()
     lane = lax.broadcasted_iota(jnp.int32, (SUBS, LANES), 1)
-    near = lane < LANES // 2
-
-    def halo(left, right, r):
-        east = pltpu.roll(right, lax.rem(LANES - STRIP * r, LANES), 1)
-        west = pltpu.roll(left, lax.rem(2 * LANES - STRIP - STRIP * r, LANES), 1)
-        return jnp.where(near, east, west)
-
-    def unpack(group, rhs, strips, cells):
+    sub = lax.broadcasted_iota(jnp.int32, (SUBS, LANES), 0)
+    copies = [
+        pltpu.make_async_copy(low_pack_ref, packs.at[0], arrived.at[0]),
+        pltpu.make_async_copy(table_ref, table, arrived.at[1]),
+        pltpu.make_async_copy(low_ref, bulk.at[0], arrived.at[2]),
+        pltpu.make_async_copy(own_pack_ref, packs.at[1], arrived.at[3]),
+        pltpu.make_async_copy(own_ref, bulk.at[1], arrived.at[4]),
+        pltpu.make_async_copy(high_pack_ref, packs.at[2], arrived.at[5]),
+        pltpu.make_async_copy(high_ref, bulk.at[2], arrived.at[6]),
+        pltpu.make_async_copy(last_ref, last, arrived.at[7]),
+    ]
+    for copy in copies:
+        copy.start()
+
+    def await_copies(*which):
+        def body():
+            for k in which:
+                copies[k].wait()
+
+        return body
+
+    def spread(strip, r):
+        return pltpu.roll(strip, lax.rem(2 * LANES - STRIP // 2 - STRIP * r, LANES), 1)
+
+    def cell_halo(strip, beyond_strip, r):
+        ninth = pltpu.roll(beyond_strip, lax.rem(LANES - STRIP * r, LANES), 1)
+        return jnp.where(lane == STRIP // 2, ninth, spread(strip, r))
+
+    def unpack(group):
         def body(y):
             r = y - group * SUBS
             for z in range(2):
                 for c in range(6):
-                    v[y, c, 2 * z] = rhs[c, depth_rows(r, z), :]
-                    v[y, c, 2 * z + 1] = halo(*strips(c, z), r)
-                mat[y, 2 * z] = cells(r, z)
-                mat[y, 2 * z + 1] = halo(*strips(6, z), r)
+                    v[y, c, 2 * z] = bulk[group, c, depth_rows(r, z), :]
+                    v[y, c, 2 * z + 1] = spread(packs[group, 2 * c + z], r)
+                mat[y, 2 * z] = packs[group, 16 + 2 * r + z]
+                mat[y, 2 * z + 1] = cell_halo(packs[group, 12 + z], packs[group, 14 + z], r)
 
         return (body, group * SUBS, group * SUBS + SUBS, 0)
-
-    def own_strips(c, z):
-        return left_ref[c, z], right_ref[c, z]
-
-    def strips_of(ref):
-        return lambda c, z: (ref[2 * c + z], ref[JOINED + 2 * c + z])
-
-    def cells_of(ref):
-        return lambda r, z: ref[2 * JOINED + 2 * r + z]
 
     def beyond(y):
         for z in range(2):
-            mat[y, 2 * z] = last_ref[4 + z]
-            mat[y, 2 * z + 1] = halo(last_ref[z], last_ref[2 + z], 0)
+            mat[y, 2 * z] = last[4 + z]
+            mat[y, 2 * z + 1] = cell_halo(last[z], last[2 + z], 0)
+
+    def indices(y):
+        ids = Field(mat[y, k] for k in range(4))
+        both = 8.0 * ids + sh.east(ids)
+        for k in range(4):
+            index[y, k] = both.parts[k].astype(jnp.int32)
 
     def pairs(y):
-        ids = [mat[y, k].astype(jnp.int32) for k in range(4)]
-        for c in range(6):
-            cell = Field(jnp.take_along_axis(table_ref[c], i, axis=1) for i in ids)
-            put(pair, y, c, cell + sh.east(cell))
+        for k in range(4):
+            which = index[y, k]
+            for c in range(6):
+                pair[y, c, k] = jnp.take_along_axis(table[c], which, axis=1)
 
     def tensors(y):
         s = [get(pair, y, c) + get(pair, y + 1, c) for c in range(6)]
@@ -322,24 +355,36 @@
 
     wavefront(
         [
-            unpack(0, low_ref, strips_of(near_low_ref), cells_of(near_low_ref)),
-            unpack(1, own_ref, own_strips, lambda r, z: own_mat_ref[r, z]),
-            unpack(2, high_ref, strips_of(near_high_ref), cells_of(near_high_ref)),
+            unpack(0),
+            unpack(1),
+            unpack(2),
             (beyond, ROWS, ROWS + 1, 0),
-            (pairs, 0, ROWS + 1, 1),
-            (tensors, 0, ROWS, 3),
-        ]
-    )
-    wavefront(iterate(sh, v, c0, u0, s2, coef, z1, t1, p, node, flux, 0, ROWS))
-    wavefront(iterate(sh, c0, c1, u1, s2, coef, z1, t1, p, node, flux, REACH, ROWS - REACH))
+            (indices, 0, ROWS + 1, 1),
+            (pairs, 0, ROWS + 1, 2),
+            (tensors, 0, ROWS, 4),
+        ],
+        [
+            (0, await_copies(0, 1, 2)),
+            (SUBS, await_copies(3, 4)),
+            (2 * SUBS, await_copies(5, 6)),
+            (ROWS, await_copies(7)),
+        ],
+    )
+    own = pl.ds(HALO, SUBS)
+    wavefront(iterate(sh, v, c0, u, keep0, s2, coef, z1, t1, p, node, flux, 0, ROWS))
+    first_out = pltpu.make_async_copy(keep0.at[own], a0_ref, left.at[0])
+    first_out.start()
+    wavefront(
+        iterate(sh, c0, c1, u, keep1, s2, coef, z1, t1, p, node, flux, REACH, ROWS - REACH)
+    )
+    second_out = pltpu.make_async_copy(keep1.at[own], a1_ref, left.at[1])
+    second_out.start()
 
     def dots(r, sums):
         y = HALO + r
         sums = list(sums)
         for c in range(6):
             for z in range(2):
-                a0_ref[r, c, z] = u0[y, c, 2 * z]
-                a1_ref[r, c, z] = u1[y, c, 2 * z]
                 f, g, h = v[y, c, 2 * z], c0[y, c, 2 * z], c1[y, c, 2 * z]
                 for k, term in enumerate((f * f, f * g, g * g, f * h, g * h, h * h)):
                     sums[k] = sums[k] + term
@@ -349,17 +394,23 @@
     sums = lax.fori_loop(0, SUBS, dots, (zero,) * 6)
     row = zero
     for k, total in enumerate(sums):
-        rest = zero
-        for axis, size in ((0, SUBS), (1, LANES)):
-            step = size // 2
-            while step:
-                total, error = two_sum(total, pltpu.roll(total, step, axis))
-                rest = rest + pltpu.roll(rest, step, axis) + error
-                step //= 2
-        row = jnp.where(lane == k, total, row)
-        row = jnp.where(lane == 6 + k, rest, row)
+        for step in (4, 2, 1):
+            total = total + pltpu.roll(total, step, 0)
+        row = jnp.where(sub == k, total, row)
+    row = jnp.broadcast_to(jnp.sum(row, axis=1, keepdims=True), (SUBS, LANES))
+    row = jnp.where(lane == sub, row, 0.0)
+    for step in (4, 2, 1):
+        row = row + pltpu.roll(row, step, 0)
     for k in range(16):
         sums_ref[pl.ds(k * SUBS, SUBS), :] = row
+    first_out.wait()
+    second_out.wait()
+
+
+def two_sum(a, b):
+    s = a + b
+    t = s - a
+    return s, (a - (s - t)) + (b - t)
 
 
 def two_product(a, b):
@@ -404,24 +455,32 @@
     return quick(q, (r[0] + r[1]) / y[0])
 
 
-def final_kernel(sums_ref, a0_ref, a1_ref, result_ref, hess_ref, out_ref, done):
+def final_kernel(sums_ref, a0_ref, a1_ref, result_ref, hess_ref, out, a0, a1, done):
     lane = lax.broadcasted_iota(jnp.int32, (SUBS, LANES), 1)
     sub = lax.broadcasted_iota(jnp.int32, (SUBS, LANES), 0)
-    total = sums_ref[pl.ds(0, SUBS), :]
-    rest = jnp.zeros_like(total)
-    for k in range(1, 16):
-        total, error = two_sum(total, sums_ref[pl.ds(k * SUBS, SUBS), :])
-        rest = rest + error
+    arriving = [
+        pltpu.make_async_copy(a0_ref, a0, done.at[6]),
+        pltpu.make_async_copy(a1_ref, a1, done.at[7]),
+    ]
+    for copy in arriving:
+        copy.start()
+    level = [(sums_ref[pl.ds(k * SUBS, SUBS), :], None) for k in range(16)]
+    while len(level) > 1:
+        pairs = []
+        for (f, f_rest), (g, g_rest) in zip(level[::2], level[1::2]):
+            total, error = two_sum(f, g)
+            pairs.append((total, error if f_rest is None else error + (f_rest + g_rest)))
+        level = pairs
+    total, rest = level[0]
     for step in (4, 2, 1):
         total, error = two_sum(total, pltpu.roll(total, step, 0))
         rest = rest + pltpu.roll(rest, step, 0) + error
-    rest = rest + pltpu.roll(total, LANES - 6, 1)
-
-    def pick(values, k):
-        one = jnp.sum(jnp.where(lane == k, values, 0.0), axis=1, keepdims=True)
-        return jnp.broadcast_to(one, (SUBS, LANES))
-
-    bb, bc, cc, bd, cd, dd = [quick(pick(total, k), pick(rest, k)) for k in range(6)]
+
+    def columns(values):
+        picked = jnp.sum(jnp.where(lane == sub, values, 0.0), axis=1, keepdims=True)
+        return [jnp.broadcast_to(picked[k : k + 1], (SUBS, LANES)) for k in range(6)]
+
+    bb, bc, cc, bd, cd, dd = [quick(f, g) for f, g in zip(columns(total), columns(rest))]
     eps = (jnp.full((SUBS, LANES), epsilon, jnp.float32), jnp.zeros((SUBS, LANES), jnp.float32))
     beta2 = plus(bb, eps)
     h00 = over(bc, beta2)
@@ -458,28 +517,34 @@
     k0 = (y0 - y1 * e00 / e10) / beta
     k1 = y1 / (e10 * beta)
 
-    table = jnp.where(sub == 0, jnp.where(lane == 0, e00, e01), jnp.where(lane == 0, e10, e11))
-    table = jnp.where(sub == 2, jnp.where(lane == 0, 0.0, e21), table)
-    hess_ref[...] = table[:3, :2]
+    table = jnp.where(lane == 0, e00, jnp.where(lane == 1, e10, 0.0))
+    later = jnp.where(lane == 0, e01, jnp.where(lane == 1, e11, e21))
+    hess_ref[...] = jnp.where(sub == 0, table, later)[:2, :3]
+    for copy in arriving:
+        copy.wait()
     copies = []
     for c in range(6):
         for row in range(SUBS):
             for z in range(2):
-                out_ref[c, depth_rows(row, z), :] = k0 * a0_ref[row, c, z] + k1 * a1_ref[row, c, z]
-        copies.append(pltpu.make_async_copy(out_ref.at[c], result_ref.at[c], done.at[c]))
+                out[c, depth_rows(row, z), :] = k0 * a0[row, c, z] + k1 * a1[row, c, z]
+        copies.append(pltpu.make_async_copy(out.at[c], result_ref.at[c], done.at[c]))
         copies[-1].start()
     for copy in copies:
         copy.wait()
 
 
-def call(kernel, outs, scratch=(), n=0):
-    vmem = pl.BlockSpec(memory_space=pltpu.VMEM)
+VMEM = pl.BlockSpec(memory_space=pltpu.VMEM)
+ANY = pl.BlockSpec(memory_space=pl.ANY)
+
+
+def call(kernel, outs, ins, scratch=(), semaphores=()):
     return pl.pallas_call(
         kernel,
-        out_shape=[jax.ShapeDtypeStruct(s, jnp.float32) for s in outs],
-        in_specs=[vmem] * n,
-        out_specs=[vmem] * len(outs),
-        scratch_shapes=[pltpu.VMEM(s, jnp.float32) for s in scratch],
+        out_shape=[jax.ShapeDtypeStruct(shape, jnp.float32) for shape, _ in outs],
+        in_specs=ins,
+        out_specs=[spec for _, spec in outs],
+        scratch_shapes=[pltpu.VMEM(shape, dtype) for shape, dtype in scratch]
+        + [pltpu.SemaphoreType.DMA((n,)) for n in semaphores],
         compiler_params=pltpu.CompilerParams(vmem_limit_bytes=VMEM_LIMIT),
     )
 
@@ -489,50 +554,69 @@
     return lax.ppermute(value, axis, [(i, (i + step) % size) for i in range(size)])
 
 
+TILE = (SUBS, LANES)
+KEPT = (SUBS, 6, 2) + TILE
+BLOCK = (6, LANES, LANES)
+
+
+def floats(*shapes):
+    return [(shape, jnp.float32) for shape in shapes]
+
+
+def rows(n, extra=0):
+    return (ROWS + extra, n, 4) + TILE
+
+
+def strip_call():
+    return call(
+        strip_kernel, [((16,) + TILE, VMEM), ((16,) + TILE, VMEM), ((6,) + TILE, VMEM)], [VMEM] * 4
+    )
+
+
+def main_call():
+    return call(
+        main_kernel,
+        [(KEPT, ANY), (KEPT, ANY), ((LANES, LANES), VMEM)],
+        [ANY] * 8,
+        floats(*[rows(6)] * 4, (ROWS + 1, 4) + TILE)
+        + [((ROWS + 1, 4) + TILE, jnp.int32)]
+        + floats(rows(6, 1), rows(6), rows(8), *[rows(6)] * 3, rows(8, 1), rows(4, 1))
+        + floats((ROWS, 6, 2) + TILE, (ROWS, 6, 2) + TILE)
+        + floats((3,) + BLOCK, (3, PACK) + TILE, (6,) + TILE, (6,) + TILE),
+        (8, 2),
+    )
+
+
+def final_call():
+    return call(
+        final_kernel,
+        [(BLOCK, ANY), ((2, 3), VMEM)],
+        [VMEM, ANY, ANY],
+        floats(BLOCK, KEPT, KEPT),
+        (8,),
+    )
+
+
 def on_device(right_side, materials, sigma_diag, sigma_off):
-    tile = (SUBS, LANES)
-    rhs = right_side.reshape(6, LANES, LANES)
-    low = moved(rhs, "gy", 1)
-    high = moved(rhs, "gy", -1)
-    to_left, to_right, cells, table = call(
-        strip_kernel, [(7, 2) + tile] * 2 + [(SUBS, 2) + tile, (6,) + tile], n=4
-    )(rhs, materials.reshape(LANES, LANES), sigma_diag, sigma_off)
-    from_right = moved(to_left, "gx", -1)
-    from_left = moved(to_right, "gx", 1)
-    joined = jnp.concatenate([part.reshape((-1,) + tile) for part in (from_left, from_right, cells)])
-    near_low = moved(joined, "gy", 1)
-    near_high = moved(joined, "gy", -1)
-    first_row = jnp.concatenate(
-        [joined[k : k + 2] for k in (JOINED - 2, 2 * JOINED - 2, 2 * JOINED)]
-    )
-    last = moved(first_row, "gy", -2)
-
-    def rows(n, extra=0):
-        return (ROWS + extra, n, 4) + tile
-
-    a0, a1, sums = call(
-        main_kernel,
-        [(SUBS, 6, 2) + tile, (SUBS, 6, 2) + tile, (LANES, LANES)],
-        [rows(6)] * 5
-        + [(ROWS + 1, 4) + tile, rows(6, 1), rows(6), rows(8)]
-        + [rows(6)] * 3
-        + [rows(8, 1), rows(4, 1)],
-        n=10,
-    )(low, rhs, high, near_low, near_high, last, from_left, from_right, cells, table)
+    rhs = right_side.reshape(BLOCK)
+    strips, cells, table = strip_call()(
+        rhs, materials.reshape(LANES, LANES), sigma_diag, sigma_off
+    )
+    from_right = moved(strips, "gx", -1)
+    from_left = moved(strips, "gx", 1)
+    bulk, strips = lax.optimization_barrier((rhs, strips))
+    low = moved(bulk, "gy", 1)
+    high = moved(bulk, "gy", -1)
+    lane = lax.broadcasted_iota(jnp.int32, (14,) + TILE, 2)
+    mixed = jnp.where(lane % STRIP < STRIP // 2, from_left[:14], from_right[:14])
+    pack = jnp.concatenate([mixed, from_right[14:], cells])
+    low_pack = moved(pack, "gy", 1)
+    high_pack = moved(pack, "gy", -1)
+    last = moved(pack[12:18], "gy", -2)
+    a0, a1, sums = main_call()(low, rhs, high, low_pack, pack, high_pack, last, table)
     gathered = lax.all_to_all(sums, ("gx", "gy"), 0, 0, tiled=True)
-    vmem = pl.BlockSpec(memory_space=pltpu.VMEM)
-    result, hessenberg = pl.pallas_call(
-        final_kernel,
-        out_shape=[
-            jax.ShapeDtypeStruct((6, LANES, LANES), jnp.float32),
-            jax.ShapeDtypeStruct((3, 2), jnp.float32),
-        ],
-        in_specs=[vmem] * 3,
-        out_specs=[pl.BlockSpec(memory_space=pl.ANY), vmem],
-        scratch_shapes=[pltpu.VMEM((6, LANES, LANES), jnp.float32), pltpu.SemaphoreType.DMA((6,))],
-        compiler_params=pltpu.CompilerParams(vmem_limit_bytes=VMEM_LIMIT),
-    )(gathered, a0, a1)
-    return result.reshape(right_side.shape), hessenberg
+    result, hessenberg = final_call()(gathered, a0, a1)
+    return result.reshape(right_side.shape), hessenberg.T
 
 
 def solution(mesh):

time: 72.5 us -> 63.6 us (0.88)
  Pallas kernels: 25 us -> 19.5 us
  waiting for transfers between devices: 12.3 us -> 8.87 us
  blocking collectives: 15.7 us -> 17 us
  other arithmetic: 0.88 us -> 0.03 us
    pallas_call x3, Pallas kernels: 25 us -> 19.5 us  [the longest x1 17.2 us: on_device(): main_call()(low, rhs, high, low_pack, pack, high_pack, last, table)]
    ppermute x7, waiting for transfers between devices: 12.3 us -> 8.87 us  [moved(): lax.ppermute(value, axis, [(i, (i + step) % size) for i in range(size)])]
    all_to_all x1, blocking collectives: 15.7 us -> 17 us  [on_device(): gathered = lax.all_to_all(sums, ('gx', 'gy'), 0, 0, tiled=True)]
    unnamed x15 -> x8, local copies, waits for them, and re-layouts: 2.24 us -> 3.19 us
    concatenate x2 -> x1, other arithmetic: 0.88 us -> 0.01 us  [on_device(): pack = jnp.concatenate([mixed, from_right[14:], cells])]
  transfers between devices with their start and end apart: 7 -> 7, of which waited for: 4 -> 2; matrix products, arithmetic and copies ran while one was open for 2% -> 0% of each run, Pallas kernels for 3% -> 0%
where the time goes in v3:
time: 63.6 us; the launch traced here: 63.4 us
  Pallas kernels  19.5 us (31%)
  blocking collectives  17 us (27%)
  starting transfers between devices  14.1 us (22%)
  waiting for transfers between devices  8.87 us (14%)
  local copies, waits for them, and re-layouts  3.2 us (5%)
  between operations  0.7 us (1%)
    pallas_call x1, Pallas kernels, on_device(): main_call()(low, rhs, high, low_pack, pack, high_pack, last, table)  17.2 us
    all_to_all x1, blocking collectives, on_device(): gathered = lax.all_to_all(sums, ('gx', 'gy'), 0, 0, tiled=True)  17 us
    ppermute x7, starting transfers between devices, moved(): lax.ppermute(value, axis, [(i, (i + step) % size) for i in range(size)])  14.1 us
    ppermute x7, waiting for transfers between devices, moved(): lax.ppermute(value, axis, [(i, (i + step) % size) for i in range(size)])  8.87 us
    unnamed x8, local copies, waits for them, and re-layouts  3.19 us
    pallas_call x1, Pallas kernels, on_device(): result, hessenberg = final_call()(gathered, a0, a1)  2.07 us
  transfers between devices with their start and end apart: 7, of which 2 were waited for; matrix products, arithmetic and copies ran while one was open for 0% of the time, Pallas kernels for 0%

profile of v3, /device:TPU:1, one launch (start us, length us, event | category | flops | bytes accessed | tf_op | source)
XLA Modules:
  0.0 63.4 jit_solution(4014500435717741553)
XLA Ops:
  0.6 0.0 copy-start.2
  0.6 0.7 %copy-done.2 = f32[3,8]{1,0:T(4,128)S(1)} copy-done((f32[3,8]{1,0:T(4,128)S(1)}, f32[3,8]{1,0:T(4,128)}, u32[]{:S(2)}) %copy-start.2) | copy-done | bytes 120
  1.3 0.0 copy-start
  1.3 1.0 %copy-done = f32[3,2,16,8,128]{4,3,2,1,0:T(8,128)S(1)} copy-done((f32[3,2,16,8,128]{4,3,2,1,0:T(8,128)S(1)}, f32[3,2,16,8,128]{4,3,2,1,0:T(8,128)}, u32[]{:S(2)}) %copy-start) | copy-done | bytes 393240
  2.3 0.0 copy-start.1
  2.3 0.8 %copy-done.1 = s32[16,8,128]{2,1,0:T(8,128)S(1)} copy-done((s32[16,8,128]{2,1,0:T(8,128)S(1)}, s32[16,8,128]{2,1,0:T(8,128)}, u32[]{:S(2)}) %copy-start.1) | copy-done | bytes 65560
  3.1 0.0 copy-start.3
  3.2 0.7 %copy-done.3 = f32[3,8]{1,0:T(4,128)S(1)} copy-done((f32[3,8]{1,0:T(4,128)S(1)}, f32[3,8]{1,0:T(4,128)}, u32[]{:S(2)}) %copy-start.3) | copy-done | bytes 120
  3.8 0.2 shard_map.59
  4.1 1.4 %collective-permute-start.3 = (f32[16,8,128]{2,1,0:T(8,128)S(1)}, f32[16,8,128]{2,1,0:T(8,128)S(1)}, u32[]{:S(2)}, u32[]{:S(2)}) collective-permute-start(f32[16,8,128]{2,1,0:T(8,128)S(1)} %get-tuple-element.11), channel_id=1, source_target_pairs={{0,112},{16,0},{32,16},{48,32},{64,48},{80,64},{96,80},{112,96},{1... | collective-permute-start | bytes 196616 | tf_op jit(solution)/shard_map/ppermute | solution.py:554
  5.5 1.6 %collective-permute-start.2 = (f32[16,8,128]{2,1,0:T(8,128)S(1)}, f32[16,8,128]{2,1,0:T(8,128)S(1)}, u32[]{:S(2)}, u32[]{:S(2)}) collective-permute-start(f32[16,8,128]{2,1,0:T(8,128)S(1)} %get-tuple-element.11), channel_id=1, source_target_pairs={{0,16},{16,32},{32,48},{48,64},{64,80},{80,96},{96,112},{112,0},{1... | collective-permute-start | bytes 196616 | tf_op jit(solution)/shard_map/ppermute | solution.py:554
  7.1 4.9 %collective-permute-start.1 = (f32[6,128,128]{2,1,0:T(8,128)S(1)}, f32[6,128,128]{2,1,0:T(8,128)S(1)}, u32[]{:S(2)}, u32[]{:S(2)}) collective-permute-start(f32[6,128,128]{2,1,0:T(8,128)S(1)} %bitcast.9), channel_id=1, source_target_pairs={{0,15},{1,0},{2,1},{3,2},{4,3},{5,4},{6,5},{7,6},{8,7},{9,8},{10,9... | collective-permute-start | bytes 1179656 | tf_op jit(solution)/shard_map/ppermute | solution.py:554
  12.1 0.0 collective-permute-start
  12.1 0.0 collective-permute-done.3
  12.1 0.0 collective-permute-done.2
  12.1 4.8 %collective-permute-start.5 = (f32[32,8,128]{2,1,0:T(8,128)S(1)}, f32[32,8,128]{2,1,0:T(8,128)S(1)}, u32[]{:S(2)}, u32[]{:S(2)}) collective-permute-start(f32[32,8,128]{2,1,0:T(8,128)S(1)} %pad_maximum_fusion.own_pack_ref), channel_id=1, source_target_pairs={{0,15},{1,0},{2,1},{3,2},{4,3},{5,4},{6,5},{7,6},{8,7},{9,8},{10,9... | collective-permute-start | bytes 393224 | tf_op jit(solution)/shard_map/ppermute | solution.py:554
  17.0 0.0 collective-permute-start.4
  17.0 1.3 %collective-permute-start.6 = (f32[6,8,128]{2,1,0:T(8,128)S(1)}, f32[6,8,128]{2,1,0:T(8,128)S(1)}, u32[]{:S(2)}, u32[]{:S(2)}) collective-permute-start(f32[6,8,128]{2,1,0:T(8,128)S(1)} %slice.19), channel_id=1, source_target_pairs={{0,14},{1,15},{2,0},{3,1},{4,2},{5,3},{6,4},{7,5},{8,6},{9,7},{10,... | collective-permute-start | bytes 73736 | tf_op jit(solution)/shard_map/ppermute | solution.py:554
  18.2 3.6 %collective-permute-done.6.last_ref = f32[6,8,128]{2,1,0:T(8,128)S(1)} collective-permute-done((f32[6,8,128]{2,1,0:T(8,128)S(1)}, f32[6,8,128]{2,1,0:T(8,128)S(1)}, u32[]{:S(2)}, u32[]{:S(2)}) %collective-permute-start.6) | collective-permute-done | bytes 24608 | tf_op jit(solution)/shard_map/ppermute | solution.py:554
  21.9 0.0 collective-permute-done.5.high_pack_ref
  21.9 5.2 %collective-permute-done.4.low_pack_ref = f32[32,8,128]{2,1,0:T(8,128)S(1)} collective-permute-done((f32[32,8,128]{2,1,0:T(8,128)S(1)}, f32[32,8,128]{2,1,0:T(8,128)S(1)}, u32[]{:S(2)}, u32[]{:S(2)}) %collective-permute-start.4) | collective-permute-done | bytes 131104 | tf_op jit(solution)/shard_map/ppermute | solution.py:554
  27.1 0.0 collective-permute-done.1.high_ref
  27.1 0.0 collective-permute-done.low_ref
  27.1 17.2 %shard_map.60 = (f32[8,6,2,8,128]{4,3,2,1,0:T(8,128)S(1)}, f32[8,6,2,8,128]{4,3,2,1,0:T(8,128)S(1)}, f32[128,128]{1,0:T(8,128)S(1)}) custom-call(f32[6,128,128]{2,1,0:T(8,128)S(1)} %collective-permute-done.low_ref, f32[6,128,128]{2,1,0:T(8,128)S(1)} %bitcast.11, f32[6,128,128]{2,1,0:T(8,128)S(1)} %collective-permute-done.1.high_ref, ...), custom_call_target="tpu_custom_call" | custom-call | tf_op jit(solution)/shard_map/pallas_call | solution.py:616
  44.3 17.0 %all_to_all.11 = f32[128,1,128]{2,1,0:T(1,128)S(1)} all-to-all(f32[128,1,128]{2,1,0:T(1,128)S(1)} %bitcast.14), channel_id=1, replica_groups=mesh['gx'=8,'gy'=16] {'gx','gy'}, dimensions={0} | all-to-all | bytes 131072 | tf_op jit(solution)/shard_map/all_to_all | solution.py:617
  61.3 2.1 %shard_map.61 = (f32[6,128,128]{2,1,0:T(8,128)}, f32[2,3]{1,0:T(2,128)}) custom-call(f32[128,128]{1,0:T(8,128)S(1)} %bitcast.12, f32[8,6,2,8,128]{4,3,2,1,0:T(8,128)S(1)} %get-tuple-element.16.a0_ref, f32[8,6,2,8,128]{4,3,2,1,0:T(8,128)S(1)} %get-tuple-element.17.a1_ref), custom_call_target="tpu_custom_call" | custom-call | tf_op jit(solution)/shard_map/pallas_call | solution.py:618
  (6 shorter events, 0.0 us)
Async XLA Ops:
  0.6 0.7 %copy-start.2 = (f32[3,8]{1,0:T(4,128)S(1)}, f32[3,8]{1,0:T(4,128)}, u32[]{:S(2)}) copy-start(f32[3,8]{1,0:T(4,128)} %diag_ref.1) | copy-start | bytes 292
  1.3 1.0 %copy-start = (f32[3,2,16,8,128]{4,3,2,1,0:T(8,128)S(1)}, f32[3,2,16,8,128]{4,3,2,1,0:T(8,128)}, u32[]{:S(2)}) copy-start(f32[3,2,16,8,128]{4,3,2,1,0:T(8,128)} %param.4) | copy-start | bytes 1179652
  2.3 0.8 %copy-start.1 = (s32[16,8,128]{2,1,0:T(8,128)S(1)}, s32[16,8,128]{2,1,0:T(8,128)}, u32[]{:S(2)}) copy-start(s32[16,8,128]{2,1,0:T(8,128)} %param.5) | copy-start | bytes 196612
  3.1 0.7 %copy-start.3 = (f32[3,8]{1,0:T(4,128)S(1)}, f32[3,8]{1,0:T(4,128)}, u32[]{:S(2)}) copy-start(f32[3,8]{1,0:T(4,128)} %off_ref.1) | copy-start | bytes 292
  4.1 8.0 %collective-permute-start.3 = (f32[16,8,128]{2,1,0:T(8,128)S(1)}, f32[16,8,128]{2,1,0:T(8,128)S(1)}, u32[]{:S(2)}, u32[]{:S(2)}) collective-permute-start(f32[16,8,128]{2,1,0:T(8,128)S(1)} %get-tuple-element.11), channel_id=1, source_target_pairs={{0,112},{16,0},{32,16},{48,32},{64,48},{80,64},{96,80},{112,96},{1... | collective-permute-start | bytes 196616 | tf_op jit(solution)/shard_map/ppermute | solution.py:554
  5.5 6.6 %collective-permute-start.2 = (f32[16,8,128]{2,1,0:T(8,128)S(1)}, f32[16,8,128]{2,1,0:T(8,128)S(1)}, u32[]{:S(2)}, u32[]{:S(2)}) collective-permute-start(f32[16,8,128]{2,1,0:T(8,128)S(1)} %get-tuple-element.11), channel_id=1, source_target_pairs={{0,16},{16,32},{32,48},{48,64},{64,80},{80,96},{96,112},{112,0},{1... | collective-permute-start | bytes 196616 | tf_op jit(solution)/shard_map/ppermute | solution.py:554
  7.1 20.0 %collective-permute-start.1 = (f32[6,128,128]{2,1,0:T(8,128)S(1)}, f32[6,128,128]{2,1,0:T(8,128)S(1)}, u32[]{:S(2)}, u32[]{:S(2)}) collective-permute-start(f32[6,128,128]{2,1,0:T(8,128)S(1)} %bitcast.9), channel_id=1, source_target_pairs={{0,15},{1,0},{2,1},{3,2},{4,3},{5,4},{6,5},{7,6},{8,7},{9,8},{10,9... | collective-permute-start | bytes 1179656 | tf_op jit(solution)/shard_map/ppermute | solution.py:554
  12.1 15.1 %collective-permute-start = (f32[6,128,128]{2,1,0:T(8,128)S(1)}, f32[6,128,128]{2,1,0:T(8,128)S(1)}, u32[]{:S(2)}, u32[]{:S(2)}) collective-permute-start(f32[6,128,128]{2,1,0:T(8,128)S(1)} %bitcast.10), channel_id=1, source_target_pairs={{0,1},{1,2},{2,3},{3,4},{4,5},{5,6},{6,7},{7,8},{8,9},{9,10},{10,1... | collective-permute-start | bytes 1179656 | tf_op jit(solution)/shard_map/ppermute | solution.py:554
  12.1 9.7 %collective-permute-start.5 = (f32[32,8,128]{2,1,0:T(8,128)S(1)}, f32[32,8,128]{2,1,0:T(8,128)S(1)}, u32[]{:S(2)}, u32[]{:S(2)}) collective-permute-start(f32[32,8,128]{2,1,0:T(8,128)S(1)} %pad_maximum_fusion.own_pack_ref), channel_id=1, source_target_pairs={{0,15},{1,0},{2,1},{3,2},{4,3},{5,4},{6,5},{7,6},{8,7},{9,8},{10,9... | collective-permute-start | bytes 393224 | tf_op jit(solution)/shard_map/ppermute | solution.py:554
  17.0 10.1 %collective-permute-start.4 = (f32[32,8,128]{2,1,0:T(8,128)S(1)}, f32[32,8,128]{2,1,0:T(8,128)S(1)}, u32[]{:S(2)}, u32[]{:S(2)}) collective-permute-start(f32[32,8,128]{2,1,0:T(8,128)S(1)} %pad_maximum_fusion.own_pack_ref), channel_id=1, source_target_pairs={{0,1},{1,2},{2,3},{3,4},{4,5},{5,6},{6,7},{7,8},{8,9},{9,10},{10,1... | collective-permute-start | bytes 393224 | tf_op jit(solution)/shard_map/ppermute | solution.py:554
  17.0 4.9 %collective-permute-start.6 = (f32[6,8,128]{2,1,0:T(8,128)S(1)}, f32[6,8,128]{2,1,0:T(8,128)S(1)}, u32[]{:S(2)}, u32[]{:S(2)}) collective-permute-start(f32[6,8,128]{2,1,0:T(8,128)S(1)} %slice.19), channel_id=1, source_target_pairs={{0,14},{1,15},{2,0},{3,1},{4,2},{5,3},{6,4},{7,5},{8,6},{9,7},{10,... | collective-permute-start | bytes 73736 | tf_op jit(solution)/shard_map/ppermute | solution.py:554

commit v4 on v3

--- a/solution.py
+++ b/solution.py
@@ -12,7 +12,8 @@
 HALO = 2 * REACH
 ROWS = SUBS + 2 * HALO
 STRIP = 16
-PACK = 32
+CHUNK = 4
+CHUNKS = ROWS // CHUNK
 VMEM_LIMIT = 44 * 2**20
 
 
@@ -85,26 +86,26 @@
     return pl.ds(z * SUBS * SUBS + y, SUBS, stride=SUBS)
 
 
-def strip_kernel(rhs_ref, mat_ref, diag_ref, off_ref, strip_ref, cells_ref, table_ref):
+def packed(tiles, offset):
     lane = lax.broadcasted_iota(jnp.int32, (SUBS, LANES), 1)
-    half = STRIP // 2
-
-    def packed(tiles, offset):
-        result = None
-        for r, tile in enumerate(tiles):
-            shift = (STRIP * r + offset) % LANES
-            moved_tile = pltpu.roll(tile, shift, 1) if shift else tile
-            result = moved_tile if r == 0 else jnp.where(lane >= STRIP * r, moved_tile, result)
-        return result
-
+    result = None
+    for r, tile in enumerate(tiles):
+        shift = (STRIP * r + offset) % LANES
+        moved_tile = pltpu.roll(tile, shift, 1) if shift else tile
+        result = moved_tile if r == 0 else jnp.where(lane >= STRIP * r, moved_tile, result)
+    return result
+
+
+def cell_strip_kernel(low_ref, own_ref, high_ref, last_ref, diag_ref, off_ref, strip_ref, table_ref):
+    lane = lax.broadcasted_iota(jnp.int32, (SUBS, LANES), 1)
     for z in range(2):
-        cells = [mat_ref[depth_rows(r, z), :].astype(jnp.float32) for r in range(SUBS)]
-        for r in range(SUBS):
-            cells_ref[2 * r + z] = cells[r]
-        strip_ref[12 + z] = packed(cells, half)
+        for group, ref in enumerate((low_ref, own_ref, high_ref)):
+            cells = [ref[depth_rows(r, z), :].astype(jnp.float32) for r in range(SUBS)]
+            strip_ref[2 * group + z] = packed(cells, STRIP // 2)
+            strip_ref[8 + 2 * group + z] = packed(cells, 0)
+        cells = [last_ref[pl.ds(z * SUBS, SUBS), :].astype(jnp.float32)]
+        strip_ref[6 + z] = packed(cells, STRIP // 2)
         strip_ref[14 + z] = packed(cells, 0)
-        for c in range(6):
-            strip_ref[2 * c + z] = packed([rhs_ref[c, depth_rows(r, z), :] for r in range(SUBS)], half)
     x, n, d = [jnp.broadcast_to(0.5 * diag_ref[c : c + 1, :], (SUBS, SUBS)) for c in range(3)]
     entries = [x, n, d]
     for c, (f, g) in enumerate(((x, n), (x, d), (n, d))):
@@ -119,6 +120,107 @@
         )
 
 
+def strip_kernel(low_ref, own_ref, high_ref, strip_ref):
+    for group, ref in enumerate((low_ref, own_ref, high_ref)):
+        for c in range(6):
+            for z in range(2):
+                strip_ref[12 * group + 2 * c + z] = packed(
+                    [ref[c, depth_rows(r, z), :] for r in range(SUBS)], STRIP // 2
+                )
+
+
+def spread(strip, r):
+    return pltpu.roll(strip, lax.rem(2 * LANES - STRIP // 2 - STRIP * r, LANES), 1)
+
+
+def tensor_kernel(
+    low_ref, own_ref, high_ref, last_ref, left_ref, right_ref, table_ref,
+    s2_ref, coef_ref,
+    mat, index, pair, s2, coef, out_sem,
+):
+    sh = Shifts()
+    lane = lax.broadcasted_iota(jnp.int32, (SUBS, LANES), 1)
+    west = lane % STRIP < STRIP // 2
+
+    def cell_halo(k, r):
+        strip = jnp.where(west, left_ref[k], right_ref[k])
+        ninth = pltpu.roll(right_ref[8 + k], lax.rem(LANES - STRIP * r, LANES), 1)
+        return jnp.where(lane == STRIP // 2, ninth, spread(strip, r))
+
+    def unpack(group, ref):
+        def body(y):
+            r = y - group * SUBS
+            for z in range(2):
+                mat[y, 2 * z] = ref[depth_rows(r, z), :].astype(jnp.float32)
+                mat[y, 2 * z + 1] = cell_halo(2 * group + z, r)
+
+        return (body, group * SUBS, group * SUBS + SUBS, 0)
+
+    def beyond(y):
+        for z in range(2):
+            mat[y, 2 * z] = last_ref[pl.ds(z * SUBS, SUBS), :].astype(jnp.float32)
+            mat[y, 2 * z + 1] = cell_halo(6 + z, 0)
+
+    def indices(y):
+        ids = Field(mat[y, k] for k in range(4))
+        both = 8.0 * ids + sh.east(ids)
+        for k in range(4):
+            index[y, k] = both.parts[k].astype(jnp.int32)
+
+    def pairs(y):
+        for k in range(4):
+            which = index[y, k]
+            for c in range(6):
+                pair[y, c, k] = jnp.take_along_axis(table_ref[c], which, axis=1)
+
+    def tensors(y):
+        s = [get(pair, y, c) + get(pair, y + 1, c) for c in range(6)]
+        for c in range(6):
+            put(s2, y, c, s[c])
+        for c in range(3):
+            inverse = 1.0 / (s[c] * s[c] + 16.0)
+            put(coef, y, c, 4.0 * inverse)
+            put(coef, y, 3 + c, s[c] * inverse)
+        shift = 2.0 * ((s[0] + s[1]) + s[2])
+        inverse = 1.0 / (shift * shift + 36.0)
+        put(coef, y, 6, 6.0 * inverse)
+        put(coef, y, 7, shift * inverse)
+
+    copies = chunk_copies(s2, s2_ref, coef, coef_ref, out_sem)
+
+    def send(k):
+        def body():
+            copies[2 * k].start()
+            copies[2 * k + 1].start()
+
+        return body
+
+    wavefront(
+        [
+            unpack(0, low_ref),
+            unpack(1, own_ref),
+            unpack(2, high_ref),
+            (beyond, ROWS, ROWS + 1, 0),
+            (indices, 0, ROWS + 1, 1),
+            (pairs, 0, ROWS + 1, 2),
+            (tensors, 0, ROWS, 4),
+        ],
+        [(CHUNK * (k + 1) + 4, send(k)) for k in range(CHUNKS - 1)],
+    )
+    send(CHUNKS - 1)()
+    for copy in copies:
+        copy.wait()
+
+
+def chunk_copies(s2_from, s2_to, coef_from, coef_to, semaphores):
+    copies = []
+    for k in range(CHUNKS):
+        part = pl.ds(CHUNK * k, CHUNK)
+        for j, (f, t) in enumerate(((s2_from, s2_to), (coef_from, coef_to))):
+            copies.append(pltpu.make_async_copy(f.at[part], t.at[part], semaphores.at[2 * k + j]))
+    return copies
+
+
 def wavefront(stages, events=()):
     edges = {e + lag for _, start, stop, lag in stages for e in (start, stop)}
     edges = sorted(edges | {at for at, _ in events})
@@ -135,7 +237,7 @@
         loop(start, stop, step)
 
 
-def iterate(sh, v, out, u, keep, s2, coef, z1, t1, p, node, flux, a, b):
+def iterate(sh, v, out, u, keep, s2, coef, z1, t1, p, node, flux, a, b, wait=0):
     def fluxes(e, above_row):
         bx = (above_row[1] - e[2]) - (sh.above(e[1]) - e[1])
         by = (sh.above(e[0]) - e[0]) - (sh.east(e[2]) - e[2])
@@ -260,124 +362,67 @@
         store(out, y, operator(y, load(u, y), ahead))
 
     return [
-        (zeroth, a, a + 1, 0),
-        (first, a, b - 1, 1),
-        (second, a + 1, b - 2, 3),
-        (third, a + 2, b - 3, 5),
-        (lift, a + 3, a + 4, 7),
-        (fourth, a + 3, b - 4, 8),
+        (zeroth, a, a + 1, wait),
+        (first, a, b - 1, wait + 1),
+        (second, a + 1, b - 2, wait + 3),
+        (third, a + 2, b - 3, wait + 5),
+        (lift, a + 3, a + 4, wait + 7),
+        (fourth, a + 3, b - 4, wait + 8),
     ]
 
 
-def two_sum(a, b):
-    s = a + b
-    t = s - a
-    return s, (a - (s - t)) + (b - t)
-
-
 def main_kernel(
-    low_ref, own_ref, high_ref, low_pack_ref, own_pack_ref, high_pack_ref, last_ref, table_ref,
+    low_ref, own_ref, high_ref, left_ref, right_ref, s2_ref, coef_ref,
     a0_ref, a1_ref, sums_ref,
-    v, c0, c1, u, mat, index, pair, s2, coef, z1, t1, p, node, flux,
-    keep0, keep1, bulk, packs, last, table, arrived, left,
+    v, c0, c1, u, s2, coef, z1, t1, p, node, flux,
+    keep0, keep1, bulk, left_strip, right_strip, arrived, tensors_in, out_sem,
 ):
     sh = Shifts()
     lane = lax.broadcasted_iota(jnp.int32, (SUBS, LANES), 1)
     sub = lax.broadcasted_iota(jnp.int32, (SUBS, LANES), 0)
+    west = lane % STRIP < STRIP // 2
     copies = [
-        pltpu.make_async_copy(low_pack_ref, packs.at[0], arrived.at[0]),
-        pltpu.make_async_copy(table_ref, table, arrived.at[1]),
-        pltpu.make_async_copy(low_ref, bulk.at[0], arrived.at[2]),
-        pltpu.make_async_copy(own_pack_ref, packs.at[1], arrived.at[3]),
-        pltpu.make_async_copy(own_ref, bulk.at[1], arrived.at[4]),
-        pltpu.make_async_copy(high_pack_ref, packs.at[2], arrived.at[5]),
-        pltpu.make_async_copy(high_ref, bulk.at[2], arrived.at[6]),
-        pltpu.make_async_copy(last_ref, last, arrived.at[7]),
+        pltpu.make_async_copy(left_ref, left_strip, arrived.at[0]),
+        pltpu.make_async_copy(right_ref, right_strip, arrived.at[1]),
     ]
-    for copy in copies:
+    for group, ref in enumerate((low_ref, own_ref, high_ref)):
+        copies.append(pltpu.make_async_copy(ref, bulk.at[group], arrived.at[2 + group]))
+    tensor_copies = chunk_copies(s2_ref, s2, coef_ref, coef, tensors_in)
+    for copy in copies[:3] + tensor_copies[:4] + copies[3:] + tensor_copies[4:]:
         copy.start()
 
-    def await_copies(*which):
+    def awaited(*waiting):
         def body():
-            for k in which:
-                copies[k].wait()
+            for copy in waiting:
+                copy.wait()
 
         return body
-
-    def spread(strip, r):
-        return pltpu.roll(strip, lax.rem(2 * LANES - STRIP // 2 - STRIP * r, LANES), 1)
-
-    def cell_halo(strip, beyond_strip, r):
-        ninth = pltpu.roll(beyond_strip, lax.rem(LANES - STRIP * r, LANES), 1)
-        return jnp.where(lane == STRIP // 2, ninth, spread(strip, r))
 
     def unpack(group):
         def body(y):
             r = y - group * SUBS
             for z in range(2):
                 for c in range(6):
+                    k = 12 * group + 2 * c + z
                     v[y, c, 2 * z] = bulk[group, c, depth_rows(r, z), :]
-                    v[y, c, 2 * z + 1] = spread(packs[group, 2 * c + z], r)
-                mat[y, 2 * z] = packs[group, 16 + 2 * r + z]
-                mat[y, 2 * z + 1] = cell_halo(packs[group, 12 + z], packs[group, 14 + z], r)
+                    v[y, c, 2 * z + 1] = spread(jnp.where(west, left_strip[k], right_strip[k]), r)
 
         return (body, group * SUBS, group * SUBS + SUBS, 0)
 
-    def beyond(y):
-        for z in range(2):
-            mat[y, 2 * z] = last[4 + z]
-            mat[y, 2 * z + 1] = cell_halo(last[z], last[2 + z], 0)
-
-    def indices(y):
-        ids = Field(mat[y, k] for k in range(4))
-        both = 8.0 * ids + sh.east(ids)
-        for k in range(4):
-            index[y, k] = both.parts[k].astype(jnp.int32)
-
-    def pairs(y):
-        for k in range(4):
-            which = index[y, k]
-            for c in range(6):
-                pair[y, c, k] = jnp.take_along_axis(table[c], which, axis=1)
-
-    def tensors(y):
-        s = [get(pair, y, c) + get(pair, y + 1, c) for c in range(6)]
-        for c in range(6):
-            put(s2, y, c, s[c])
-        for c in range(3):
-            inverse = 1.0 / (s[c] * s[c] + 16.0)
-            put(coef, y, c, 4.0 * inverse)
-            put(coef, y, 3 + c, s[c] * inverse)
-        shift = 2.0 * ((s[0] + s[1]) + s[2])
-        inverse = 1.0 / (shift * shift + 36.0)
-        put(coef, y, 6, 6.0 * inverse)
-        put(coef, y, 7, shift * inverse)
-
+    own = pl.ds(HALO, SUBS)
     wavefront(
-        [
-            unpack(0),
-            unpack(1),
-            unpack(2),
-            (beyond, ROWS, ROWS + 1, 0),
-            (indices, 0, ROWS + 1, 1),
-            (pairs, 0, ROWS + 1, 2),
-            (tensors, 0, ROWS, 4),
-        ],
-        [
-            (0, await_copies(0, 1, 2)),
-            (SUBS, await_copies(3, 4)),
-            (2 * SUBS, await_copies(5, 6)),
-            (ROWS, await_copies(7)),
-        ],
-    )
-    own = pl.ds(HALO, SUBS)
-    wavefront(iterate(sh, v, c0, u, keep0, s2, coef, z1, t1, p, node, flux, 0, ROWS))
-    first_out = pltpu.make_async_copy(keep0.at[own], a0_ref, left.at[0])
+        [unpack(0), unpack(1), unpack(2)]
+        + iterate(sh, v, c0, u, keep0, s2, coef, z1, t1, p, node, flux, 0, ROWS, 1),
+        [(0, awaited(*copies[:3]))]
+        + [(CHUNK * k + 1, awaited(*tensor_copies[2 * k : 2 * k + 2])) for k in range(CHUNKS)]
+        + [(SUBS, awaited(copies[3])), (2 * SUBS, awaited(copies[4]))],
+    )
+    first_out = pltpu.make_async_copy(keep0.at[own], a0_ref, out_sem.at[0])
     first_out.start()
     wavefront(
         iterate(sh, c0, c1, u, keep1, s2, coef, z1, t1, p, node, flux, REACH, ROWS - REACH)
     )
-    second_out = pltpu.make_async_copy(keep1.at[own], a1_ref, left.at[1])
+    second_out = pltpu.make_async_copy(keep1.at[own], a1_ref, out_sem.at[1])
     second_out.start()
 
     def dots(r, sums):
@@ -567,9 +612,23 @@
     return (ROWS + extra, n, 4) + TILE
 
 
+def cell_strip_call():
+    return call(cell_strip_kernel, [((16,) + TILE, VMEM), ((6,) + TILE, VMEM)], [VMEM] * 6)
+
+
 def strip_call():
+    return call(strip_kernel, [((36,) + TILE, VMEM)], [VMEM] * 3)
+
+
+def tensor_call():
     return call(
-        strip_kernel, [((16,) + TILE, VMEM), ((16,) + TILE, VMEM), ((6,) + TILE, VMEM)], [VMEM] * 4
+        tensor_kernel,
+        [(rows(6), ANY), (rows(8), ANY)],
+        [VMEM] * 7,
+        floats((ROWS + 1, 4) + TILE)
+        + [((ROWS + 1, 4) + TILE, jnp.int32)]
+        + floats(rows(6, 1), rows(6), rows(8)),
+        (2 * CHUNKS,),
     )
 
 
@@ -577,13 +636,11 @@
     return call(
         main_kernel,
         [(KEPT, ANY), (KEPT, ANY), ((LANES, LANES), VMEM)],
-        [ANY] * 8,
-        floats(*[rows(6)] * 4, (ROWS + 1, 4) + TILE)
-        + [((ROWS + 1, 4) + TILE, jnp.int32)]
-        + floats(rows(6, 1), rows(6), rows(8), *[rows(6)] * 3, rows(8, 1), rows(4, 1))
+        [ANY] * 7,
+        floats(*[rows(6)] * 5, rows(8), *[rows(6)] * 3, rows(8, 1), rows(4, 1))
         + floats((ROWS, 6, 2) + TILE, (ROWS, 6, 2) + TILE)
-        + floats((3,) + BLOCK, (3, PACK) + TILE, (6,) + TILE, (6,) + TILE),
-        (8, 2),
+        + floats((3,) + BLOCK, (36,) + TILE, (36,) + TILE),
+        (5, 2 * CHUNKS, 2),
     )
 
 
@@ -599,21 +656,26 @@
 
 def on_device(right_side, materials, sigma_diag, sigma_off):
     rhs = right_side.reshape(BLOCK)
-    strips, cells, table = strip_call()(
-        rhs, materials.reshape(LANES, LANES), sigma_diag, sigma_off
-    )
-    from_right = moved(strips, "gx", -1)
-    from_left = moved(strips, "gx", 1)
-    bulk, strips = lax.optimization_barrier((rhs, strips))
+    cells = materials.reshape(LANES, LANES)
+    low_cells = moved(cells, "gy", 1)
+    high_cells = moved(cells, "gy", -1)
+    first_row = materials[:, 0, :]
+    bulk, first_row = lax.optimization_barrier((rhs, first_row))
+    last = moved(first_row, "gy", -2)
     low = moved(bulk, "gy", 1)
     high = moved(bulk, "gy", -1)
-    lane = lax.broadcasted_iota(jnp.int32, (14,) + TILE, 2)
-    mixed = jnp.where(lane % STRIP < STRIP // 2, from_left[:14], from_right[:14])
-    pack = jnp.concatenate([mixed, from_right[14:], cells])
-    low_pack = moved(pack, "gy", 1)
-    high_pack = moved(pack, "gy", -1)
-    last = moved(pack[12:18], "gy", -2)
-    a0, a1, sums = main_call()(low, rhs, high, low_pack, pack, high_pack, last, table)
+    cell_strips, table = cell_strip_call()(
+        low_cells, cells, high_cells, last, sigma_diag, sigma_off
+    )
+    s2, coef = tensor_call()(
+        low_cells, cells, high_cells, last,
+        moved(cell_strips, "gx", 1), moved(cell_strips, "gx", -1), table,
+    )
+    low, high, s2, coef = lax.optimization_barrier((low, high, s2, coef))
+    (strips,) = strip_call()(low, rhs, high)
+    a0, a1, sums = main_call()(
+        low, rhs, high, moved(strips, "gx", 1), moved(strips, "gx", -1), s2, coef
+    )
     gathered = lax.all_to_all(sums, ("gx", "gy"), 0, 0, tiled=True)
     result, hessenberg = final_call()(gathered, a0, a1)
     return result.reshape(right_side.shape), hessenberg.T

time: 63.6 us -> 75.8 us (1.19)
  starting transfers between devices: 14.1 us -> 18.9 us
  waiting for transfers between devices: 8.87 us -> 12.8 us
  Pallas kernels: 19.5 us -> 22.9 us
  local copies, waits for them, and re-layouts: 3.2 us -> 4.04 us
  blocking collectives: 17 us -> 16.2 us
    ppermute x7 -> x9, starting transfers between devices: 14.1 us -> 18.9 us  [moved(): lax.ppermute(value, axis, [(i, (i + step) % size) for i in range(size)])]
    ppermute x7 -> x9, waiting for transfers between devices: 8.87 us -> 12.8 us  [moved(): lax.ppermute(value, axis, [(i, (i + step) % size) for i in range(size)])]
    pallas_call x2 -> x4, Pallas kernels: 17.4 us -> 20.8 us  [the longest x1 15.9 us: on_device(): main_call()]
    slice x2 -> x1, local copies, waits for them, and re-layouts: 0.01 us -> 0.85 us  [on_device(): first_row = materials[:, 0, :]]
    all_to_all x1, blocking collectives: 17 us -> 16.2 us  [on_device(): gathered = lax.all_to_all(sums, ('gx', 'gy'), 0, 0, tiled=True)]
  transfers between devices with their start and end apart: 7 -> 9, of which waited for: 2 -> 5; matrix products, arithmetic and copies ran while one was open for 0% -> 0% of each run, Pallas kernels for 0% -> 6%
where the time goes in v4:
time: 75.8 us; the launch traced here: 75.5 us
  Pallas kernels  22.9 us (30%)
  starting transfers between devices  18.9 us (25%)
  blocking collectives  16.2 us (21%)
  waiting for transfers between devices  12.8 us (17%)
  local copies, waits for them, and re-layouts  4.04 us (5%)
    ppermute x9, starting transfers between devices, moved(): lax.ppermute(value, axis, [(i, (i + step) % size) for i in range(size)])  18.9 us
    all_to_all x1, blocking collectives, on_device(): gathered = lax.all_to_all(sums, ('gx', 'gy'), 0, 0, tiled=True)  16.2 us
    pallas_call x1, Pallas kernels, on_device(): main_call()  15.9 us
    ppermute x9, waiting for transfers between devices, moved(): lax.ppermute(value, axis, [(i, (i + step) % size) for i in range(size)])  12.8 us
    pallas_call x1, Pallas kernels, on_device(): tensor_call()  4.36 us
    unnamed x8, local copies, waits for them, and re-layouts  3.19 us
    pallas_call x1, Pallas kernels, on_device(): result, hessenberg = final_call()(gathered, a0, a1)  2.07 us
  transfers between devices with their start and end apart: 9, of which 5 were waited for; matrix products, arithmetic and copies ran while one was open for 0% of the time, Pallas kernels for 6%

profile of v4, /device:TPU:1, one launch (start us, length us, event | category | flops | bytes accessed | tf_op | source)
XLA Modules:
  0.0 75.5 jit_solution(4956478627520652628)
XLA Ops:
  0.6 0.8 %slice.3 = s32[16,1,128]{2,1,0:T(1,128)S(1)} slice(s32[16,8,128]{2,1,0:T(8,128)} %param.5), slice={[0:16], [0:1], [0:128]} | slice | bytes 16384 | tf_op jit(solution)/shard_map/slice | solution.py:662
  1.5 5.8 %collective-permute-start.1 = (f32[6,128,128]{2,1,0:T(8,128)}, f32[6,128,128]{2,1,0:T(8,128)S(1)}, u32[]{:S(2)}, u32[]{:S(2)}) collective-permute-start(f32[6,128,128]{2,1,0:T(8,128)} %bitcast.11), channel_id=1, source_target_pairs={{0,15},{1,0},{2,1},{3,2},{4,3},{5,4},{6,5},{7,6},{8,7},{9,8},{10,9... | collective-permute-start | bytes 1179656 | tf_op jit(solution)/shard_map/ppermute | solution.py:599
  7.2 0.0 collective-permute-start
  7.2 4.8 %collective-permute-start.3 = (s32[128,128]{1,0:T(8,128)}, s32[128,128]{1,0:T(8,128)S(1)}, u32[]{:S(2)}, u32[]{:S(2)}) collective-permute-start(s32[128,128]{1,0:T(8,128)} %bitcast.15), channel_id=1, source_target_pairs={{0,15},{1,0},{2,1},{3,2},{4,3},{5,4},{6,5},{7,6},{8,7},{9,8},{10,9... | collective-permute-start | bytes 196616 | tf_op jit(solution)/shard_map/ppermute | solution.py:599
  12.0 0.0 collective-permute-start.2
  12.0 1.2 %collective-permute-start.4 = (s32[16,128]{1,0:T(8,128)S(1)}, s32[16,128]{1,0:T(8,128)S(1)}, u32[]{:S(2)}, u32[]{:S(2)}) collective-permute-start(s32[16,128]{1,0:T(8,128)S(1)} %bitcast.21), channel_id=1, source_target_pairs={{0,14},{1,15},{2,0},{3,1},{4,2},{5,3},{6,4},{7,5},{8,6},{9,7},{10,... | collective-permute-start | bytes 24584 | tf_op jit(solution)/shard_map/ppermute | solution.py:599
  13.2 3.6 %collective-permute-done.4.last_ref = s32[16,128]{1,0:T(8,128)S(1)} collective-permute-done((s32[16,128]{1,0:T(8,128)S(1)}, s32[16,128]{1,0:T(8,128)S(1)}, u32[]{:S(2)}, u32[]{:S(2)}) %collective-permute-start.4) | collective-permute-done | bytes 8224 | tf_op jit(solution)/shard_map/ppermute | solution.py:599
  16.8 0.0 collective-permute-done.3.high_ref
  16.8 5.2 %collective-permute-done.2.low_ref = s32[128,128]{1,0:T(8,128)S(1)} collective-permute-done((s32[128,128]{1,0:T(8,128)}, s32[128,128]{1,0:T(8,128)S(1)}, u32[]{:S(2)}, u32[]{:S(2)}) %collective-permute-start.2) | collective-permute-done | bytes 65568 | tf_op jit(solution)/shard_map/ppermute | solution.py:599
  22.0 0.0 copy-start.1
  22.0 0.8 %copy-done.1 = s32[16,8,128]{2,1,0:T(8,128)S(1)} copy-done((s32[16,8,128]{2,1,0:T(8,128)S(1)}, s32[16,8,128]{2,1,0:T(8,128)}, u32[]{:S(2)}) %copy-start.1) | copy-done | bytes 65560
  22.9 0.0 copy-start.2
  22.9 0.7 copy-done.2
  23.5 0.0 copy-start.3
  23.5 0.7 copy-done.3
  24.2 0.2 shard_map.59
  24.4 1.9 %collective-permute-start.6 = (f32[16,8,128]{2,1,0:T(8,128)S(1)}, f32[16,8,128]{2,1,0:T(8,128)S(1)}, u32[]{:S(2)}, u32[]{:S(2)}) collective-permute-start(f32[16,8,128]{2,1,0:T(8,128)S(1)} %get-tuple-element.19), channel_id=1, source_target_pairs={{0,112},{16,0},{32,16},{48,32},{64,48},{80,64},{96,80},{112,96},{1... | collective-permute-start | bytes 196616 | tf_op jit(solution)/shard_map/ppermute | solution.py:599
  26.3 1.5 %collective-permute-start.5 = (f32[16,8,128]{2,1,0:T(8,128)S(1)}, f32[16,8,128]{2,1,0:T(8,128)S(1)}, u32[]{:S(2)}, u32[]{:S(2)}) collective-permute-start(f32[16,8,128]{2,1,0:T(8,128)S(1)} %get-tuple-element.19), channel_id=1, source_target_pairs={{0,16},{16,32},{32,48},{48,64},{64,80},{80,96},{96,112},{112,0},{1... | collective-permute-start | bytes 196616 | tf_op jit(solution)/shard_map/ppermute | solution.py:599
  27.8 1.9 %collective-permute-done.6.right_ref = f32[16,8,128]{2,1,0:T(8,128)S(1)} collective-permute-done((f32[16,8,128]{2,1,0:T(8,128)S(1)}, f32[16,8,128]{2,1,0:T(8,128)S(1)}, u32[]{:S(2)}, u32[]{:S(2)}) %collective-permute-start.6) | collective-permute-done | bytes 65568 | tf_op jit(solution)/shard_map/ppermute | solution.py:599
  29.8 0.0 collective-permute-done.5.left_ref
  29.8 4.4 %shard_map.60 = (f32[24,6,4,8,128]{4,3,2,1,0:T(8,128)S(1)}, f32[24,8,4,8,128]{4,3,2,1,0:T(8,128)S(1)}) custom-call(s32[128,128]{1,0:T(8,128)S(1)} %collective-permute-done.2.low_ref, s32[128,128]{1,0:T(8,128)S(1)} %bitcast.18, s32[128,128]{1,0:T(8,128)S(1)} %collective-permute-done.3.high_ref, s32[16,128]{1,0:T(8,128)S(1)} %collective-permute-done.4.last_ref, ...), custom_call_target="tpu_custom_call" | custom-call | tf_op jit(solution)/shard_map/pallas_call | solution.py:670
  34.1 0.0 collective-permute-done.1.high_ref
  34.1 0.0 collective-permute-done.low_ref
  34.1 0.0 copy-start
  34.2 1.0 %copy-done = f32[3,2,16,8,128]{4,3,2,1,0:T(8,128)S(1)} copy-done((f32[3,2,16,8,128]{4,3,2,1,0:T(8,128)S(1)}, f32[3,2,16,8,128]{4,3,2,1,0:T(8,128)}, u32[]{:S(2)}) %copy-start) | copy-done | bytes 393240
  35.1 0.4 shard_map.61
  35.5 3.7 %collective-permute-start.8 = (f32[36,8,128]{2,1,0:T(8,128)S(1)}, f32[36,8,128]{2,1,0:T(8,128)S(1)}, u32[]{:S(2)}, u32[]{:S(2)}) collective-permute-start(f32[36,8,128]{2,1,0:T(8,128)S(1)} %shard_map.61), channel_id=1, source_target_pairs={{0,112},{16,0},{32,16},{48,32},{64,48},{80,64},{96,80},{112,96},{1... | collective-permute-start | bytes 442376 | tf_op jit(solution)/shard_map/ppermute | solution.py:599
  39.2 0.0 collective-permute-start.7
  39.2 1.0 %collective-permute-done.8.right_ref = f32[36,8,128]{2,1,0:T(8,128)S(1)} collective-permute-done((f32[36,8,128]{2,1,0:T(8,128)S(1)}, f32[36,8,128]{2,1,0:T(8,128)S(1)}, u32[]{:S(2)}, u32[]{:S(2)}) %collective-permute-start.8) | collective-permute-done | bytes 147488 | tf_op jit(solution)/shard_map/ppermute | solution.py:599
  40.2 1.1 %collective-permute-done.7.left_ref = f32[36,8,128]{2,1,0:T(8,128)S(1)} collective-permute-done((f32[36,8,128]{2,1,0:T(8,128)S(1)}, f32[36,8,128]{2,1,0:T(8,128)S(1)}, u32[]{:S(2)}, u32[]{:S(2)}) %collective-permute-start.7) | collective-permute-done | bytes 147488 | tf_op jit(solution)/shard_map/ppermute | solution.py:599
  41.3 15.9 %shard_map.62 = (f32[8,6,2,8,128]{4,3,2,1,0:T(8,128)S(1)}, f32[8,6,2,8,128]{4,3,2,1,0:T(8,128)S(1)}, f32[128,128]{1,0:T(8,128)S(1)}) custom-call(f32[6,128,128]{2,1,0:T(8,128)S(1)} %collective-permute-done.low_ref, f32[6,128,128]{2,1,0:T(8,128)S(1)} %bitcast.14, f32[6,128,128]{2,1,0:T(8,128)S(1)} %collective-permute-done.1.high_ref, ...), custom_call_target="tpu_custom_call" | custom-call | tf_op jit(solution)/shard_map/pallas_call | solution.py:676
  57.2 16.2 %all_to_all.11 = f32[128,1,128]{2,1,0:T(1,128)S(1)} all-to-all(f32[128,1,128]{2,1,0:T(1,128)S(1)} %bitcast.20), channel_id=1, replica_groups=mesh['gx'=8,'gy'=16] {'gx','gy'}, dimensions={0} | all-to-all | bytes 131072 | tf_op jit(solution)/shard_map/all_to_all | solution.py:679
  73.4 2.1 %shard_map.63 = (f32[6,128,128]{2,1,0:T(8,128)}, f32[2,3]{1,0:T(2,128)}) custom-call(f32[128,128]{1,0:T(8,128)S(1)} %bitcast.19, f32[8,6,2,8,128]{4,3,2,1,0:T(8,128)S(1)} %get-tuple-element.28.a0_ref, f32[8,6,2,8,128]{4,3,2,1,0:T(8,128)S(1)} %get-tuple-element.29.a1_ref), custom_call_target="tpu_custom_call" | custom-call | tf_op jit(solution)/shard_map/pallas_call | solution.py:680
Async XLA Ops:
  1.5 32.7 %collective-permute-start.1 = (f32[6,128,128]{2,1,0:T(8,128)}, f32[6,128,128]{2,1,0:T(8,128)S(1)}, u32[]{:S(2)}, u32[]{:S(2)}) collective-permute-start(f32[6,128,128]{2,1,0:T(8,128)} %bitcast.11), channel_id=1, source_target_pairs={{0,15},{1,0},{2,1},{3,2},{4,3},{5,4},{6,5},{7,6},{8,7},{9,8},{10,9... | collective-permute-start | bytes 1179656 | tf_op jit(solution)/shard_map/ppermute | solution.py:599
  7.2 26.9 %collective-permute-start = (f32[6,128,128]{2,1,0:T(8,128)}, f32[6,128,128]{2,1,0:T(8,128)S(1)}, u32[]{:S(2)}, u32[]{:S(2)}) collective-permute-start(f32[6,128,128]{2,1,0:T(8,128)} %bitcast.12), channel_id=1, source_target_pairs={{0,1},{1,2},{2,3},{3,4},{4,5},{5,6},{6,7},{7,8},{8,9},{9,10},{10,1... | collective-permute-start | bytes 1179656 | tf_op jit(solution)/shard_map/ppermute | solution.py:599
  7.2 9.6 %collective-permute-start.3 = (s32[128,128]{1,0:T(8,128)}, s32[128,128]{1,0:T(8,128)S(1)}, u32[]{:S(2)}, u32[]{:S(2)}) collective-permute-start(s32[128,128]{1,0:T(8,128)} %bitcast.15), channel_id=1, source_target_pairs={{0,15},{1,0},{2,1},{3,2},{4,3},{5,4},{6,5},{7,6},{8,7},{9,8},{10,9... | collective-permute-start | bytes 196616 | tf_op jit(solution)/shard_map/ppermute | solution.py:599
  12.0 10.0 %collective-permute-start.2 = (s32[128,128]{1,0:T(8,128)}, s32[128,128]{1,0:T(8,128)S(1)}, u32[]{:S(2)}, u32[]{:S(2)}) collective-permute-start(s32[128,128]{1,0:T(8,128)} %bitcast.16), channel_id=1, source_target_pairs={{0,1},{1,2},{2,3},{3,4},{4,5},{5,6},{6,7},{7,8},{8,9},{9,10},{10,1... | collective-permute-start | bytes 196616 | tf_op jit(solution)/shard_map/ppermute | solution.py:599
  12.0 4.8 %collective-permute-start.4 = (s32[16,128]{1,0:T(8,128)S(1)}, s32[16,128]{1,0:T(8,128)S(1)}, u32[]{:S(2)}, u32[]{:S(2)}) collective-permute-start(s32[16,128]{1,0:T(8,128)S(1)} %bitcast.21), channel_id=1, source_target_pairs={{0,14},{1,15},{2,0},{3,1},{4,2},{5,3},{6,4},{7,5},{8,6},{9,7},{10,... | collective-permute-start | bytes 24584 | tf_op jit(solution)/shard_map/ppermute | solution.py:599
  22.0 0.8 %copy-start.1 = (s32[16,8,128]{2,1,0:T(8,128)S(1)}, s32[16,8,128]{2,1,0:T(8,128)}, u32[]{:S(2)}) copy-start(s32[16,8,128]{2,1,0:T(8,128)} %param.5) | copy-start | bytes 196612
  22.9 0.7 copy-start.2
  23.5 0.7 copy-start.3
  24.4 5.4 %collective-permute-start.6 = (f32[16,8,128]{2,1,0:T(8,128)S(1)}, f32[16,8,128]{2,1,0:T(8,128)S(1)}, u32[]{:S(2)}, u32[]{:S(2)}) collective-permute-start(f32[16,8,128]{2,1,0:T(8,128)S(1)} %get-tuple-element.19), channel_id=1, source_target_pairs={{0,112},{16,0},{32,16},{48,32},{64,48},{80,64},{96,80},{112,96},{1... | collective-permute-start | bytes 196616 | tf_op jit(solution)/shard_map/ppermute | solution.py:599
  26.3 3.5 %collective-permute-start.5 = (f32[16,8,128]{2,1,0:T(8,128)S(1)}, f32[16,8,128]{2,1,0:T(8,128)S(1)}, u32[]{:S(2)}, u32[]{:S(2)}) collective-permute-start(f32[16,8,128]{2,1,0:T(8,128)S(1)} %get-tuple-element.19), channel_id=1, source_target_pairs={{0,16},{16,32},{32,48},{48,64},{64,80},{80,96},{96,112},{112,0},{1... | collective-permute-start | bytes 196616 | tf_op jit(solution)/shard_map/ppermute | solution.py:599
  34.1 1.0 %copy-start = (f32[3,2,16,8,128]{4,3,2,1,0:T(8,128)S(1)}, f32[3,2,16,8,128]{4,3,2,1,0:T(8,128)}, u32[]{:S(2)}) copy-start(f32[3,2,16,8,128]{4,3,2,1,0:T(8,128)} %param.4) | copy-start | bytes 1179652
  35.5 4.7 %collective-permute-start.8 = (f32[36,8,128]{2,1,0:T(8,128)S(1)}, f32[36,8,128]{2,1,0:T(8,128)S(1)}, u32[]{:S(2)}, u32[]{:S(2)}) collective-permute-start(f32[36,8,128]{2,1,0:T(8,128)S(1)} %shard_map.61), channel_id=1, source_target_pairs={{0,112},{16,0},{32,16},{48,32},{64,48},{80,64},{96,80},{112,96},{1... | collective-permute-start | bytes 442376 | tf_op jit(solution)/shard_map/ppermute | solution.py:599
  39.2 2.1 %collective-permute-start.7 = (f32[36,8,128]{2,1,0:T(8,128)S(1)}, f32[36,8,128]{2,1,0:T(8,128)S(1)}, u32[]{:S(2)}, u32[]{:S(2)}) collective-permute-start(f32[36,8,128]{2,1,0:T(8,128)S(1)} %shard_map.61), channel_id=1, source_target_pairs={{0,16},{16,32},{32,48},{48,64},{64,80},{80,96},{96,112},{112,0},{1... | collective-permute-start | bytes 442376 | tf_op jit(solution)/shard_map/ppermute | solution.py:599

commit v5 on v3

--- a/solution.py
+++ b/solution.py
@@ -85,7 +85,16 @@
     return pl.ds(z * SUBS * SUBS + y, SUBS, stride=SUBS)
 
 
-def strip_kernel(rhs_ref, mat_ref, diag_ref, off_ref, strip_ref, cells_ref, table_ref):
+def strip_kernel(
+    rhs_in, mat_in, diag_in, off_in, strip_ref, cells_ref, table_ref,
+    rhs_ref, mat_ref, diag_ref, off_ref, arrived,
+):
+    pairs = ((mat_in, mat_ref), (rhs_in, rhs_ref), (diag_in, diag_ref), (off_in, off_ref))
+    copies = [pltpu.make_async_copy(f, t, arrived.at[k]) for k, (f, t) in enumerate(pairs)]
+    for copy in copies:
+        copy.start()
+    for copy in copies:
+        copy.wait()
     lane = lax.broadcasted_iota(jnp.int32, (SUBS, LANES), 1)
     half = STRIP // 2
 
@@ -276,7 +285,7 @@
 
 
 def main_kernel(
-    low_ref, own_ref, high_ref, low_pack_ref, own_pack_ref, high_pack_ref, last_ref, table_ref,
+    odd_ref, own_ref, first_ref, second_ref, own_pack_ref, first_pack_ref, second_pack_ref, last_ref, table_ref,
     a0_ref, a1_ref, sums_ref,
     v, c0, c1, u, mat, index, pair, s2, coef, z1, t1, p, node, flux,
     keep0, keep1, bulk, packs, last, table, arrived, left,
@@ -284,23 +293,21 @@
     sh = Shifts()
     lane = lax.broadcasted_iota(jnp.int32, (SUBS, LANES), 1)
     sub = lax.broadcasted_iota(jnp.int32, (SUBS, LANES), 0)
-    copies = [
-        pltpu.make_async_copy(low_pack_ref, packs.at[0], arrived.at[0]),
-        pltpu.make_async_copy(table_ref, table, arrived.at[1]),
-        pltpu.make_async_copy(low_ref, bulk.at[0], arrived.at[2]),
-        pltpu.make_async_copy(own_pack_ref, packs.at[1], arrived.at[3]),
-        pltpu.make_async_copy(own_ref, bulk.at[1], arrived.at[4]),
-        pltpu.make_async_copy(high_pack_ref, packs.at[2], arrived.at[5]),
-        pltpu.make_async_copy(high_ref, bulk.at[2], arrived.at[6]),
-        pltpu.make_async_copy(last_ref, last, arrived.at[7]),
-    ]
-    for copy in copies:
-        copy.start()
-
-    def await_copies(*which):
+    odd = odd_ref[0]
+    first, second = 2 - 2 * odd, 2 * odd
+    for ref, slot in ((second_pack_ref, second), (first_pack_ref, first), (own_pack_ref, 1)):
+        pltpu.make_async_copy(ref, packs.at[slot], arrived.at[slot]).start()
+    for ref, slot in ((second_ref, second), (first_ref, first), (own_ref, 1)):
+        pltpu.make_async_copy(ref, bulk.at[slot], arrived.at[3 + slot]).start()
+    last_copy = pltpu.make_async_copy(last_ref, last, arrived.at[6])
+    table_copy = pltpu.make_async_copy(table_ref, table, arrived.at[7])
+    last_copy.start()
+    table_copy.start()
+
+    def await_group(slot):
         def body():
-            for k in which:
-                copies[k].wait()
+            pltpu.make_async_copy(own_pack_ref, packs.at[slot], arrived.at[slot]).wait()
+            pltpu.make_async_copy(own_ref, bulk.at[slot], arrived.at[3 + slot]).wait()
 
         return body
 
@@ -364,10 +371,11 @@
             (tensors, 0, ROWS, 4),
         ],
         [
-            (0, await_copies(0, 1, 2)),
-            (SUBS, await_copies(3, 4)),
-            (2 * SUBS, await_copies(5, 6)),
-            (ROWS, await_copies(7)),
+            (0, await_group(0)),
+            (1, table_copy.wait),
+            (SUBS, await_group(1)),
+            (2 * SUBS, await_group(2)),
+            (ROWS, last_copy.wait),
         ],
     )
     own = pl.ds(HALO, SUBS)
@@ -535,9 +543,10 @@
 
 VMEM = pl.BlockSpec(memory_space=pltpu.VMEM)
 ANY = pl.BlockSpec(memory_space=pl.ANY)
-
-
-def call(kernel, outs, ins, scratch=(), semaphores=()):
+SMEM = pl.BlockSpec(memory_space=pltpu.SMEM)
+
+
+def call(kernel, outs, ins, scratch=(), semaphores=(), limit=VMEM_LIMIT):
     return pl.pallas_call(
         kernel,
         out_shape=[jax.ShapeDtypeStruct(shape, jnp.float32) for shape, _ in outs],
@@ -545,7 +554,7 @@
         out_specs=[spec for _, spec in outs],
         scratch_shapes=[pltpu.VMEM(shape, dtype) for shape, dtype in scratch]
         + [pltpu.SemaphoreType.DMA((n,)) for n in semaphores],
-        compiler_params=pltpu.CompilerParams(vmem_limit_bytes=VMEM_LIMIT),
+        compiler_params=pltpu.CompilerParams(vmem_limit_bytes=limit),
     )
 
 
@@ -569,7 +578,12 @@
 
 def strip_call():
     return call(
-        strip_kernel, [((16,) + TILE, VMEM), ((16,) + TILE, VMEM), ((6,) + TILE, VMEM)], [VMEM] * 4
+        strip_kernel,
+        [((16,) + TILE, VMEM), ((16,) + TILE, VMEM), ((6,) + TILE, VMEM)],
+        [ANY] * 4,
+        floats(BLOCK) + [((LANES, LANES), jnp.int32)] + floats((3, SUBS), (3, SUBS)),
+        (4,),
+        60 * 2**20,
     )
 
 
@@ -577,7 +591,7 @@
     return call(
         main_kernel,
         [(KEPT, ANY), (KEPT, ANY), ((LANES, LANES), VMEM)],
-        [ANY] * 8,
+        [SMEM] + [ANY] * 8,
         floats(*[rows(6)] * 4, (ROWS + 1, 4) + TILE)
         + [((ROWS + 1, 4) + TILE, jnp.int32)]
         + floats(rows(6, 1), rows(6), rows(8), *[rows(6)] * 3, rows(8, 1), rows(4, 1))
@@ -597,23 +611,30 @@
     )
 
 
+def swapped(value, axis):
+    size = lax.axis_size(axis)
+    pairs = [(i, i ^ 1) for i in range(size)]
+    others = [((i + 1) % size, (j + 1) % size) for i, j in pairs]
+    second = lax.ppermute(value, axis, others)
+    return lax.ppermute(value, axis, pairs), second
+
+
 def on_device(right_side, materials, sigma_diag, sigma_off):
     rhs = right_side.reshape(BLOCK)
+    bulk = swapped(rhs, "gy")
     strips, cells, table = strip_call()(
         rhs, materials.reshape(LANES, LANES), sigma_diag, sigma_off
     )
-    from_right = moved(strips, "gx", -1)
-    from_left = moved(strips, "gx", 1)
-    bulk, strips = lax.optimization_barrier((rhs, strips))
-    low = moved(bulk, "gy", 1)
-    high = moved(bulk, "gy", -1)
+    first, second = swapped(strips, "gx")
+    odd = lax.axis_index("gx") % 2 == 1
     lane = lax.broadcasted_iota(jnp.int32, (14,) + TILE, 2)
-    mixed = jnp.where(lane % STRIP < STRIP // 2, from_left[:14], from_right[:14])
-    pack = jnp.concatenate([mixed, from_right[14:], cells])
-    low_pack = moved(pack, "gy", 1)
-    high_pack = moved(pack, "gy", -1)
+    mixed = jnp.where((lane % STRIP < STRIP // 2) == odd, first[:14], second[:14])
+    pack = jnp.concatenate([mixed, jnp.where(odd, second[14:], first[14:]), cells])
+    packs = swapped(pack, "gy")
     last = moved(pack[12:18], "gy", -2)
-    a0, a1, sums = main_call()(low, rhs, high, low_pack, pack, high_pack, last, table)
+    a0, a1, sums = main_call()(
+        lax.axis_index("gy").reshape(1) % 2, rhs, *bulk, pack, *packs, last, table
+    )
     gathered = lax.all_to_all(sums, ("gx", "gy"), 0, 0, tiled=True)
     result, hessenberg = final_call()(gathered, a0, a1)
     return result.reshape(right_side.shape), hessenberg.T

time: 63.6 us -> 63.2 us (level)
  waiting for transfers between devices: 8.87 us -> 6.31 us
  local copies, waits for them, and re-layouts: 3.2 us -> 0.81 us
  starting transfers between devices: 14.1 us -> 16 us
  Pallas kernels: 19.5 us -> 21.3 us
  blocking collectives: 17 us -> 17.8 us
    ppermute x0 -> x6, starting transfers between devices: none -> 11.6 us  [the longest x3 9.19 us: swapped(): second = lax.ppermute(value, axis, others)]
    ppermute x7 -> x1, starting transfers between devices: 14.1 us -> 4.42 us  [moved(): lax.ppermute(value, axis, [(i, (i + step) % size) for i in range(size)])]
    ppermute x7 -> x1, waiting for transfers between devices: 8.87 us -> 5.3 us  [moved(): lax.ppermute(value, axis, [(i, (i + step) % size) for i in range(size)])]
    unnamed x8 -> x6, local copies, waits for them, and re-layouts: 3.19 us -> 0.81 us
    pallas_call x1, Pallas kernels: 0.23 us -> 1.99 us  [on_device(): strip_call()(rhs, materials.reshape(LANES, LANES), sigma_diag, sigma_off)]
    ppermute x0 -> x6, waiting for transfers between devices: none -> 1.01 us  [the longest x3 1 us: swapped(): return (lax.ppermute(value, axis, pairs), second)]
    all_to_all x1, blocking collectives: 17 us -> 17.8 us  [on_device(): gathered = lax.all_to_all(sums, ('gx', 'gy'), 0, 0, tiled=True)]
where the time goes in v5:
time: 63.2 us; the launch traced here: 63 us
  Pallas kernels  21.3 us (34%)
  blocking collectives  17.8 us (28%)
  starting transfers between devices  16 us (25%)
  waiting for transfers between devices  6.31 us (10%)
  local copies, waits for them, and re-layouts  0.81 us (1%)
  between operations  0.71 us (1%)
    all_to_all x1, blocking collectives, on_device(): gathered = lax.all_to_all(sums, ('gx', 'gy'), 0, 0, tiled=True)  17.8 us
    pallas_call x1, Pallas kernels, on_device(): main_call()  17.2 us
    ppermute x3, starting transfers between devices, swapped(): second = lax.ppermute(value, axis, others)  9.19 us
    ppermute x1, waiting for transfers between devices, moved(): lax.ppermute(value, axis, [(i, (i + step) % size) for i in range(size)])  5.3 us
    ppermute x1, starting transfers between devices, moved(): lax.ppermute(value, axis, [(i, (i + step) % size) for i in range(size)])  4.42 us
    ppermute x3, starting transfers between devices, swapped(): return (lax.ppermute(value, axis, pairs), second)  2.43 us
    pallas_call x1, Pallas kernels, on_device(): result, hessenberg = final_call()(gathered, a0, a1)  2.07 us
    pallas_call x1, Pallas kernels, on_device(): strip_call()(rhs, materials.reshape(LANES, LANES), sigma_diag, sigma_off)  1.99 us
  transfers between devices with their start and end apart: 7, of which 2 were waited for; matrix products, arithmetic and copies ran while one was open for 0% of the time, Pallas kernels for 0%

profile of v5, /device:TPU:1, one launch (start us, length us, event | category | flops | bytes accessed | tf_op | source)
XLA Modules:
  0.0 63.0 jit_solution(12850040669630236035)
XLA Ops:
  0.6 0.0 copy-start
  0.6 2.0 %shard_map.59 = (f32[16,8,128]{2,1,0:T(8,128)}, f32[16,8,128]{2,1,0:T(8,128)}, f32[6,8,128]{2,1,0:T(8,128)}) custom-call(f32[6,128,128]{2,1,0:T(8,128)} %bitcast.9, s32[128,128]{1,0:T(8,128)} %bitcast.15, f32[3,8]{1,0:T(4,128)} %diag_in.1, f32[3,8]{1,0:T(4,128)} %off_in.1), custom_call_target="tpu_custom_call" | custom-call | tf_op jit(solution)/shard_map/pallas_call | solution.py:625
  2.6 3.1 %collective-permute-start.3 = (f32[16,8,128]{2,1,0:T(8,128)}, f32[16,8,128]{2,1,0:T(8,128)S(1)}, u32[]{:S(2)}, u32[]{:S(2)}) collective-permute-start(f32[16,8,128]{2,1,0:T(8,128)} %get-tuple-element.10), channel_id=1, source_target_pairs={{16,32},{32,16},{48,64},{64,48},{80,96},{96,80},{112,0},{0,112},{1... | collective-permute-start | bytes 196616 | tf_op jit(solution)/shard_map/ppermute | solution.py:618
  5.7 2.0 %collective-permute-start.2 = (f32[16,8,128]{2,1,0:T(8,128)}, f32[16,8,128]{2,1,0:T(8,128)S(1)}, u32[]{:S(2)}, u32[]{:S(2)}) collective-permute-start(f32[16,8,128]{2,1,0:T(8,128)} %get-tuple-element.10), channel_id=1, source_target_pairs={{0,16},{16,0},{32,48},{48,32},{64,80},{80,64},{96,112},{112,96},{1... | collective-permute-start | bytes 196616 | tf_op jit(solution)/shard_map/ppermute | solution.py:619
  7.7 0.0 copy-done
  7.7 4.9 %collective-permute-start.1 = (f32[6,128,128]{2,1,0:T(8,128)S(1)}, f32[6,128,128]{2,1,0:T(8,128)S(1)}, u32[]{:S(2)}, u32[]{:S(2)}) collective-permute-start(f32[6,128,128]{2,1,0:T(8,128)S(1)} %bitcast.10), channel_id=1, source_target_pairs={{1,2},{2,1},{3,4},{4,3},{5,6},{6,5},{7,8},{8,7},{9,10},{10,9},{11,... | collective-permute-start | bytes 1179656 | tf_op jit(solution)/shard_map/ppermute | solution.py:618
  12.6 0.0 collective-permute-start
  12.6 0.0 collective-permute-done.3
  12.7 0.0 collective-permute-done.2
  12.7 0.0 copy-start.2
  12.7 0.8 %copy-done.2 = f32[16,8,128]{2,1,0:T(8,128)S(1)} copy-done((f32[16,8,128]{2,1,0:T(8,128)S(1)}, f32[16,8,128]{2,1,0:T(8,128)}, u32[]{:S(2)}) %copy-start.2) | copy-done | bytes 65560
  13.5 1.2 %collective-permute-start.5 = (f32[32,8,128]{2,1,0:T(8,128)S(1)}, f32[32,8,128]{2,1,0:T(8,128)S(1)}, u32[]{:S(2)}, u32[]{:S(2)}) collective-permute-start(f32[32,8,128]{2,1,0:T(8,128)S(1)} %pad_maximum_fusion.own_pack_ref), channel_id=1, source_target_pairs={{1,2},{2,1},{3,4},{4,3},{5,6},{6,5},{7,8},{8,7},{9,10},{10,9},{11,... | collective-permute-start | bytes 393224 | tf_op jit(solution)/shard_map/ppermute | solution.py:618
  14.7 0.5 collective-permute-start.4
  15.1 0.0 copy-start.1
  15.2 4.4 %collective-permute-start.6 = (f32[6,8,128]{2,1,0:T(8,128)S(1)}, f32[6,8,128]{2,1,0:T(8,128)S(1)}, u32[]{:S(2)}, u32[]{:S(2)}) collective-permute-start(f32[6,8,128]{2,1,0:T(8,128)S(1)} %slice.24), channel_id=1, source_target_pairs={{0,14},{1,15},{2,0},{3,1},{4,2},{5,3},{6,4},{7,5},{8,6},{9,7},{10,... | collective-permute-start | bytes 73736 | tf_op jit(solution)/shard_map/ppermute | solution.py:563
  19.6 5.3 %collective-permute-done.6.last_ref = f32[6,8,128]{2,1,0:T(8,128)S(1)} collective-permute-done((f32[6,8,128]{2,1,0:T(8,128)S(1)}, f32[6,8,128]{2,1,0:T(8,128)S(1)}, u32[]{:S(2)}, u32[]{:S(2)}) %collective-permute-start.6) | collective-permute-done | bytes 24608 | tf_op jit(solution)/shard_map/ppermute | solution.py:563
  24.9 0.0 collective-permute-done.5.second_pack_ref
  24.9 1.0 %collective-permute-done.4.first_pack_ref = f32[32,8,128]{2,1,0:T(8,128)S(1)} collective-permute-done((f32[32,8,128]{2,1,0:T(8,128)S(1)}, f32[32,8,128]{2,1,0:T(8,128)S(1)}, u32[]{:S(2)}, u32[]{:S(2)}) %collective-permute-start.4) | collective-permute-done | bytes 131104 | tf_op jit(solution)/shard_map/ppermute | solution.py:619
  25.9 0.0 collective-permute-done.1.second_ref
  25.9 0.0 collective-permute-done.first_ref
  25.9 0.0 copy-done.1
  25.9 17.2 %shard_map.60 = (f32[8,6,2,8,128]{4,3,2,1,0:T(8,128)S(1)}, f32[8,6,2,8,128]{4,3,2,1,0:T(8,128)S(1)}, f32[128,128]{1,0:T(8,128)S(1)}) custom-call(s32[1]{0:T(128)S(6)} %select_n.31.odd_ref, f32[6,128,128]{2,1,0:T(8,128)S(1)} %bitcast.12, f32[6,128,128]{2,1,0:T(8,128)S(1)} %collective-permute-done.first_ref, ...), custom_call_target="tpu_custom_call" | custom-call | tf_op jit(solution)/shard_map/pallas_call | solution.py:635
  43.1 17.8 %all_to_all.11 = f32[128,1,128]{2,1,0:T(1,128)S(1)} all-to-all(f32[128,1,128]{2,1,0:T(1,128)S(1)} %bitcast.14), channel_id=1, replica_groups=mesh['gx'=8,'gy'=16] {'gx','gy'}, dimensions={0} | all-to-all | bytes 131072 | tf_op jit(solution)/shard_map/all_to_all | solution.py:638
  60.9 2.1 %shard_map.61 = (f32[6,128,128]{2,1,0:T(8,128)}, f32[2,3]{1,0:T(2,128)}) custom-call(f32[128,128]{1,0:T(8,128)S(1)} %bitcast.13, f32[8,6,2,8,128]{4,3,2,1,0:T(8,128)S(1)} %get-tuple-element.14.a0_ref, f32[8,6,2,8,128]{4,3,2,1,0:T(8,128)S(1)} %get-tuple-element.15.a1_ref), custom_call_target="tpu_custom_call" | custom-call | tf_op jit(solution)/shard_map/pallas_call | solution.py:639
  (6 shorter events, 0.0 us)
Async XLA Ops:
  0.6 7.1 %copy-start = (f32[3,2,16,8,128]{4,3,2,1,0:T(8,128)S(1)}, f32[3,2,16,8,128]{4,3,2,1,0:T(8,128)}, u32[]{:S(2)}) copy-start(f32[3,2,16,8,128]{4,3,2,1,0:T(8,128)} %param.4) | copy-start | bytes 1179652
  2.6 10.0 %collective-permute-start.3 = (f32[16,8,128]{2,1,0:T(8,128)}, f32[16,8,128]{2,1,0:T(8,128)S(1)}, u32[]{:S(2)}, u32[]{:S(2)}) collective-permute-start(f32[16,8,128]{2,1,0:T(8,128)} %get-tuple-element.10), channel_id=1, source_target_pairs={{16,32},{32,16},{48,64},{64,48},{80,96},{96,80},{112,0},{0,112},{1... | collective-permute-start | bytes 196616 | tf_op jit(solution)/shard_map/ppermute | solution.py:618
  5.7 6.9 %collective-permute-start.2 = (f32[16,8,128]{2,1,0:T(8,128)}, f32[16,8,128]{2,1,0:T(8,128)S(1)}, u32[]{:S(2)}, u32[]{:S(2)}) collective-permute-start(f32[16,8,128]{2,1,0:T(8,128)} %get-tuple-element.10), channel_id=1, source_target_pairs={{0,16},{16,0},{32,48},{48,32},{64,80},{80,64},{96,112},{112,96},{1... | collective-permute-start | bytes 196616 | tf_op jit(solution)/shard_map/ppermute | solution.py:619
  7.7 18.2 %collective-permute-start.1 = (f32[6,128,128]{2,1,0:T(8,128)S(1)}, f32[6,128,128]{2,1,0:T(8,128)S(1)}, u32[]{:S(2)}, u32[]{:S(2)}) collective-permute-start(f32[6,128,128]{2,1,0:T(8,128)S(1)} %bitcast.10), channel_id=1, source_target_pairs={{1,2},{2,1},{3,4},{4,3},{5,6},{6,5},{7,8},{8,7},{9,10},{10,9},{11,... | collective-permute-start | bytes 1179656 | tf_op jit(solution)/shard_map/ppermute | solution.py:618
  12.6 13.2 %collective-permute-start = (f32[6,128,128]{2,1,0:T(8,128)S(1)}, f32[6,128,128]{2,1,0:T(8,128)S(1)}, u32[]{:S(2)}, u32[]{:S(2)}) collective-permute-start(f32[6,128,128]{2,1,0:T(8,128)S(1)} %bitcast.11), channel_id=1, source_target_pairs={{0,1},{1,0},{2,3},{3,2},{4,5},{5,4},{6,7},{7,6},{8,9},{9,8},{10,11... | collective-permute-start | bytes 1179656 | tf_op jit(solution)/shard_map/ppermute | solution.py:619
  12.7 0.8 %copy-start.2 = (f32[16,8,128]{2,1,0:T(8,128)S(1)}, f32[16,8,128]{2,1,0:T(8,128)}, u32[]{:S(2)}) copy-start(f32[16,8,128]{2,1,0:T(8,128)} %get-tuple-element.11) | copy-start | bytes 196612
  13.5 11.4 %collective-permute-start.5 = (f32[32,8,128]{2,1,0:T(8,128)S(1)}, f32[32,8,128]{2,1,0:T(8,128)S(1)}, u32[]{:S(2)}, u32[]{:S(2)}) collective-permute-start(f32[32,8,128]{2,1,0:T(8,128)S(1)} %pad_maximum_fusion.own_pack_ref), channel_id=1, source_target_pairs={{1,2},{2,1},{3,4},{4,3},{5,6},{6,5},{7,8},{8,7},{9,10},{10,9},{11,... | collective-permute-start | bytes 393224 | tf_op jit(solution)/shard_map/ppermute | solution.py:618
  14.7 11.2 %collective-permute-start.4 = (f32[32,8,128]{2,1,0:T(8,128)S(1)}, f32[32,8,128]{2,1,0:T(8,128)S(1)}, u32[]{:S(2)}, u32[]{:S(2)}) collective-permute-start(f32[32,8,128]{2,1,0:T(8,128)S(1)} %pad_maximum_fusion.own_pack_ref), channel_id=1, source_target_pairs={{0,1},{1,0},{2,3},{3,2},{4,5},{5,4},{6,7},{7,6},{8,9},{9,8},{10,11... | collective-permute-start | bytes 393224 | tf_op jit(solution)/shard_map/ppermute | solution.py:619
  15.1 10.7 %copy-start.1 = (f32[6,8,128]{2,1,0:T(8,128)S(1)}, f32[6,8,128]{2,1,0:T(8,128)}, u32[]{:S(2)}) copy-start(f32[6,8,128]{2,1,0:T(8,128)} %get-tuple-element.12.table_ref) | copy-start | bytes 73732
  15.2 9.7 %collective-permute-start.6 = (f32[6,8,128]{2,1,0:T(8,128)S(1)}, f32[6,8,128]{2,1,0:T(8,128)S(1)}, u32[]{:S(2)}, u32[]{:S(2)}) collective-permute-start(f32[6,8,128]{2,1,0:T(8,128)S(1)} %slice.24), channel_id=1, source_target_pairs={{0,14},{1,15},{2,0},{3,1},{4,2},{5,3},{6,4},{7,5},{8,6},{9,7},{10,... | collective-permute-start | bytes 73736 | tf_op jit(solution)/shard_map/ppermute | solution.py:563

commit v6 on v5

--- a/solution.py
+++ b/solution.py
@@ -11,6 +11,7 @@
 REACH = 4
 HALO = 2 * REACH
 ROWS = SUBS + 2 * HALO
+HALF = LANES // 2
 STRIP = 16
 PACK = 32
 VMEM_LIMIT = 44 * 2**20
@@ -44,36 +45,49 @@
     def __init__(self):
         lane = lax.broadcasted_iota(jnp.int32, (SUBS, LANES), 1)
         sub = lax.broadcasted_iota(jnp.int32, (SUBS, LANES), 0)
-        self.first_lane = lane == 0
-        self.last_lane = lane == LANES - 1
-        self.first_sub = sub == 0
-        self.last_sub = sub == SUBS - 1
+        low = lane < HALF
+        self.first, self.last = sub == 0, sub == SUBS - 1
+        self.first_low, self.first_high = self.first & low, self.first & ~low
+        self.last_low, self.last_high = self.last & low, self.last & ~low
 
     def east(self, field):
-        r = [pltpu.roll(t, LANES - 1, 1) for t in field.parts]
-        return Field(jnp.where(self.last_lane, r[k ^ 1], r[k]) for k in range(4))
+        return Field(pltpu.roll(t, LANES - 1, 1) for t in field.parts)
 
     def west(self, field):
-        r = [pltpu.roll(t, 1, 1) for t in field.parts]
-        return Field(jnp.where(self.first_lane, r[k ^ 1], r[k]) for k in range(4))
+        return Field(pltpu.roll(t, 1, 1) for t in field.parts)
 
     def above(self, field):
         r = [pltpu.roll(t, SUBS - 1, 0) for t in field.parts]
-        low = [jnp.where(self.last_sub, r[2 + k], r[k]) for k in range(2)]
-        return Field(low + [jnp.where(self.last_sub, 0.0, r[2 + k]) for k in range(2)])
+        other = pltpu.roll(r[2], HALF, 1)
+        outer = jnp.where(self.last_low, other, jnp.where(self.last_high, 0.0, r[2]))
+        return Field([jnp.where(self.last, r[1], r[0]), jnp.where(self.last, 0.0, r[1]), outer])
 
     def below(self, field):
         r = [pltpu.roll(t, 1, 0) for t in field.parts]
-        low = [jnp.where(self.first_sub, 0.0, r[k]) for k in range(2)]
-        return Field(low + [jnp.where(self.first_sub, r[k], r[2 + k]) for k in range(2)])
+        other = pltpu.roll(r[2], HALF, 1)
+        outer = jnp.where(self.first_high, other, jnp.where(self.first_low, 0.0, r[2]))
+        return Field([jnp.where(self.first, 0.0, r[0]), jnp.where(self.first, r[0], r[1]), outer])
+
+
+def outer_columns(own, halo):
+    lane = lax.broadcasted_iota(jnp.int32, (SUBS, LANES), 1)
+    pieces = []
+    for z in range(2):
+        start = jnp.where(lane >= LANES - HALO, halo[z], own[z])
+        end = jnp.where(lane < HALO, halo[z], own[z])
+        pieces.append(pltpu.roll(start, HALO + HALF * z, 1))
+        pieces.append(pltpu.roll(end, 5 * HALO + HALF * z, 1))
+    low = jnp.where(lane < 3 * HALO, pieces[0], pieces[1])
+    high = jnp.where(lane < HALF + 3 * HALO, pieces[2], pieces[3])
+    return jnp.where(lane < HALF, low, high)
 
 
 def get(ref, row, c):
-    return Field(ref[row, c, k] for k in range(4))
+    return Field(ref[row, c, k] for k in range(3))
 
 
 def put(ref, row, c, field):
-    for k in range(4):
+    for k in range(3):
         ref[row, c, k] = field.parts[k]
 
 
@@ -86,17 +100,15 @@
 
 
 def strip_kernel(
-    rhs_in, mat_in, diag_in, off_in, strip_ref, cells_ref, table_ref,
-    rhs_ref, mat_ref, diag_ref, off_ref, arrived,
+    rhs_in, mat_in, diag_in, off_in, strip_ref, table_ref, rhs_ref, mat_ref, diag_ref, off_ref, arrived
 ):
-    pairs = ((mat_in, mat_ref), (rhs_in, rhs_ref), (diag_in, diag_ref), (off_in, off_ref))
+    lane = lax.broadcasted_iota(jnp.int32, (SUBS, LANES), 1)
+    half = STRIP // 2
+    pairs = [(diag_in, diag_ref), (off_in, off_ref), (mat_in, mat_ref)]
+    pairs += [(rhs_in.at[c], rhs_ref.at[c]) for c in range(6)]
     copies = [pltpu.make_async_copy(f, t, arrived.at[k]) for k, (f, t) in enumerate(pairs)]
     for copy in copies:
         copy.start()
-    for copy in copies:
-        copy.wait()
-    lane = lax.broadcasted_iota(jnp.int32, (SUBS, LANES), 1)
-    half = STRIP // 2
 
     def packed(tiles, offset):
         result = None
@@ -106,13 +118,16 @@
             result = moved_tile if r == 0 else jnp.where(lane >= STRIP * r, moved_tile, result)
         return result
 
+    copies[0].wait()
+    copies[1].wait()
+    copies[2].wait()
     for z in range(2):
         cells = [mat_ref[depth_rows(r, z), :].astype(jnp.float32) for r in range(SUBS)]
-        for r in range(SUBS):
-            cells_ref[2 * r + z] = cells[r]
         strip_ref[12 + z] = packed(cells, half)
         strip_ref[14 + z] = packed(cells, 0)
-        for c in range(6):
+    for c in range(6):
+        copies[3 + c].wait()
+        for z in range(2):
             strip_ref[2 * c + z] = packed([rhs_ref[c, depth_rows(r, z), :] for r in range(SUBS)], half)
     x, n, d = [jnp.broadcast_to(0.5 * diag_ref[c : c + 1, :], (SUBS, SUBS)) for c in range(3)]
     entries = [x, n, d]
@@ -144,7 +159,7 @@
         loop(start, stop, step)
 
 
-def iterate(sh, v, out, u, keep, s2, coef, z1, t1, p, node, flux, a, b):
+def iterate(sh, v, out, u, keep, s2, coef, z1, t1, p, node, flux, a, b, wait=0):
     def fluxes(e, above_row):
         bx = (above_row[1] - e[2]) - (sh.above(e[1]) - e[1])
         by = (sh.above(e[0]) - e[0]) - (sh.east(e[2]) - e[2])
@@ -259,29 +274,31 @@
                     slope = sh.above(w[part]) - w[part]
                 result.append((get(z1, y, k) + get(p, y, k)) + slope)
         store(u, y, result)
-        for k in range(6):
-            for z in range(2):
-                keep[y, k, z] = result[k].parts[2 * z]
         return result
 
     def fourth(y):
         ahead = lift(y + 1)
         store(out, y, operator(y, load(u, y), ahead))
 
+    def merge(y):
+        lane = lax.broadcasted_iota(jnp.int32, (SUBS, LANES), 1)
+        for c in range(6):
+            outer = u[y, c, 2]
+            for z in range(2):
+                start = pltpu.roll(outer, (LANES - HALO - HALF * z) % LANES, 1)
+                end = pltpu.roll(outer, (11 * HALO - HALF * z) % LANES, 1)
+                inner = jnp.where(lane < HALO, start, u[y, c, z])
+                keep[y - HALO, c, z] = jnp.where(lane >= LANES - HALO, end, inner)
+
     return [
-        (zeroth, a, a + 1, 0),
-        (first, a, b - 1, 1),
-        (second, a + 1, b - 2, 3),
-        (third, a + 2, b - 3, 5),
-        (lift, a + 3, a + 4, 7),
-        (fourth, a + 3, b - 4, 8),
+        (zeroth, a, a + 1, wait),
+        (first, a, b - 1, wait + 1),
+        (second, a + 1, b - 2, wait + 3),
+        (third, a + 2, b - 3, wait + 5),
+        (lift, a + 3, a + 4, wait + 7),
+        (fourth, a + 3, b - 4, wait + 8),
+        (merge, HALO, HALO + SUBS, wait + 9),
     ]
-
-
-def two_sum(a, b):
-    s = a + b
-    t = s - a
-    return s, (a - (s - t)) + (b - t)
 
 
 def main_kernel(
@@ -318,15 +335,22 @@
         ninth = pltpu.roll(beyond_strip, lax.rem(LANES - STRIP * r, LANES), 1)
         return jnp.where(lane == STRIP // 2, ninth, spread(strip, r))
 
+    def strip(group, k):
+        return packs[group, pl.ds(SUBS * k, SUBS), :]
+
+    def strip(group, k):
+        return packs[group, pl.ds(SUBS * k, SUBS), :]
+
     def unpack(group):
         def body(y):
             r = y - group * SUBS
+            for c in range(6):
+                inner = [bulk[group, c, depth_rows(r, z), :] for z in range(2)]
+                outer = outer_columns(inner, [spread(strip(group, 2 * c + z), r) for z in range(2)])
+                put(v, y, c, Field(inner + [outer]))
             for z in range(2):
-                for c in range(6):
-                    v[y, c, 2 * z] = bulk[group, c, depth_rows(r, z), :]
-                    v[y, c, 2 * z + 1] = spread(packs[group, 2 * c + z], r)
-                mat[y, 2 * z] = packs[group, 16 + 2 * r + z]
-                mat[y, 2 * z + 1] = cell_halo(packs[group, 12 + z], packs[group, 14 + z], r)
+                mat[y, 2 * z] = packs[group, depth_rows(r, 2 + z), :]
+                mat[y, 2 * z + 1] = cell_halo(strip(group, 12 + z), strip(group, 14 + z), r)
 
         return (body, group * SUBS, group * SUBS + SUBS, 0)
 
@@ -336,13 +360,15 @@
             mat[y, 2 * z + 1] = cell_halo(last[z], last[2 + z], 0)
 
     def indices(y):
-        ids = Field(mat[y, k] for k in range(4))
-        both = 8.0 * ids + sh.east(ids)
-        for k in range(4):
-            index[y, k] = both.parts[k].astype(jnp.int32)
+        ids = [mat[y, k] for k in range(4)]
+        r = [pltpu.roll(t, LANES - 1, 1) for t in ids]
+        both = [8.0 * ids[k] + jnp.where(lane == LANES - 1, r[k ^ 1], r[k]) for k in range(4)]
+        inner = both[0::2]
+        for k, part in enumerate(inner + [outer_columns(inner, both[1::2])]):
+            index[y, k] = part.astype(jnp.int32)
 
     def pairs(y):
-        for k in range(4):
+        for k in range(3):
             which = index[y, k]
             for c in range(6):
                 pair[y, c, k] = jnp.take_along_axis(table[c], which, axis=1)
@@ -369,39 +395,43 @@
             (indices, 0, ROWS + 1, 1),
             (pairs, 0, ROWS + 1, 2),
             (tensors, 0, ROWS, 4),
-        ],
+        ]
+        + iterate(sh, v, c0, u, keep0, s2, coef, z1, t1, p, node, flux, 0, ROWS, 5),
         [
             (0, await_group(0)),
-            (1, table_copy.wait),
+            (2, table_copy.wait),
             (SUBS, await_group(1)),
             (2 * SUBS, await_group(2)),
             (ROWS, last_copy.wait),
         ],
     )
-    own = pl.ds(HALO, SUBS)
-    wavefront(iterate(sh, v, c0, u, keep0, s2, coef, z1, t1, p, node, flux, 0, ROWS))
-    first_out = pltpu.make_async_copy(keep0.at[own], a0_ref, left.at[0])
+    first_out = pltpu.make_async_copy(keep0, a0_ref, left.at[0])
     first_out.start()
     wavefront(
         iterate(sh, c0, c1, u, keep1, s2, coef, z1, t1, p, node, flux, REACH, ROWS - REACH)
     )
-    second_out = pltpu.make_async_copy(keep1.at[own], a1_ref, left.at[1])
+    second_out = pltpu.make_async_copy(keep1, a1_ref, left.at[1])
     second_out.start()
 
     def dots(r, sums):
         y = HALO + r
         sums = list(sums)
         for c in range(6):
-            for z in range(2):
-                f, g, h = v[y, c, 2 * z], c0[y, c, 2 * z], c1[y, c, 2 * z]
+            for part in range(3):
+                base = 6 if part == 2 else 0
+                f, g, h = v[y, c, part], c0[y, c, part], c1[y, c, part]
                 for k, term in enumerate((f * f, f * g, g * g, f * h, g * h, h * h)):
-                    sums[k] = sums[k] + term
+                    sums[base + k] = sums[base + k] + term
         return tuple(sums)
 
     zero = jnp.zeros((SUBS, LANES), jnp.float32)
-    sums = lax.fori_loop(0, SUBS, dots, (zero,) * 6)
+    sums = lax.fori_loop(0, SUBS, dots, (zero,) * 12)
+    inner = (lane >= HALO) & (lane < LANES - HALO)
+    place = lane % HALF
+    outer = ((place >= HALO) & (place < 2 * HALO)) | ((place >= 4 * HALO) & (place < 5 * HALO))
     row = zero
-    for k, total in enumerate(sums):
+    for k in range(6):
+        total = jnp.where(inner, sums[k], 0.0) + jnp.where(outer, sums[6 + k], 0.0)
         for step in (4, 2, 1):
             total = total + pltpu.roll(total, step, 0)
         row = jnp.where(sub == k, total, row)
@@ -544,6 +574,7 @@
 VMEM = pl.BlockSpec(memory_space=pltpu.VMEM)
 ANY = pl.BlockSpec(memory_space=pl.ANY)
 SMEM = pl.BlockSpec(memory_space=pltpu.SMEM)
+HBM = pl.BlockSpec(memory_space=pltpu.HBM)
 
 
 def call(kernel, outs, ins, scratch=(), semaphores=(), limit=VMEM_LIMIT):
@@ -573,16 +604,16 @@
 
 
 def rows(n, extra=0):
-    return (ROWS + extra, n, 4) + TILE
+    return (ROWS + extra, n, 3) + TILE
 
 
 def strip_call():
     return call(
         strip_kernel,
-        [((16,) + TILE, VMEM), ((16,) + TILE, VMEM), ((6,) + TILE, VMEM)],
-        [ANY] * 4,
+        [((16,) + TILE, VMEM), ((6,) + TILE, VMEM)],
+        [HBM] * 4,
         floats(BLOCK) + [((LANES, LANES), jnp.int32)] + floats((3, SUBS), (3, SUBS)),
-        (4,),
+        (9,),
         60 * 2**20,
     )
 
@@ -591,12 +622,12 @@
     return call(
         main_kernel,
         [(KEPT, ANY), (KEPT, ANY), ((LANES, LANES), VMEM)],
-        [SMEM] + [ANY] * 8,
+        [SMEM, HBM] + [ANY] * 7,
         floats(*[rows(6)] * 4, (ROWS + 1, 4) + TILE)
-        + [((ROWS + 1, 4) + TILE, jnp.int32)]
+        + [((ROWS + 1, 3) + TILE, jnp.int32)]
         + floats(rows(6, 1), rows(6), rows(8), *[rows(6)] * 3, rows(8, 1), rows(4, 1))
-        + floats((ROWS, 6, 2) + TILE, (ROWS, 6, 2) + TILE)
-        + floats((3,) + BLOCK, (3, PACK) + TILE, (6,) + TILE, (6,) + TILE),
+        + floats(KEPT, KEPT)
+        + floats((3,) + BLOCK, (3, SUBS * PACK, LANES), (6,) + TILE, (6,) + TILE),
         (8, 2),
     )
 
@@ -622,16 +653,17 @@
 def on_device(right_side, materials, sigma_diag, sigma_off):
     rhs = right_side.reshape(BLOCK)
     bulk = swapped(rhs, "gy")
-    strips, cells, table = strip_call()(
-        rhs, materials.reshape(LANES, LANES), sigma_diag, sigma_off
-    )
+    strips, table = strip_call()(rhs, materials.reshape(LANES, LANES), sigma_diag, sigma_off)
+    first_row = materials[:, 0, :].astype(jnp.float32).reshape((2,) + TILE)
     first, second = swapped(strips, "gx")
     odd = lax.axis_index("gx") % 2 == 1
     lane = lax.broadcasted_iota(jnp.int32, (14,) + TILE, 2)
     mixed = jnp.where((lane % STRIP < STRIP // 2) == odd, first[:14], second[:14])
-    pack = jnp.concatenate([mixed, jnp.where(odd, second[14:], first[14:]), cells])
+    beyond = jnp.where(odd, second[14:], first[14:])
+    last = moved(jnp.concatenate([mixed[12:], beyond, first_row]), "gy", -2)
+    pack = jnp.concatenate([mixed, beyond, materials.astype(jnp.float32)])
+    pack = pack.reshape(SUBS * PACK, LANES)
     packs = swapped(pack, "gy")
-    last = moved(pack[12:18], "gy", -2)
     a0, a1, sums = main_call()(
         lax.axis_index("gy").reshape(1) % 2, rhs, *bulk, pack, *packs, last, table
     )

time: 63.2 us -> 66.4 us (1.051)
  Pallas kernels: 21.3 us -> 24.6 us
  local copies, waits for them, and re-layouts: 0.81 us -> 0.01 us
  waiting for transfers between devices: 6.31 us -> 7.04 us
    pallas_call x1, Pallas kernels: 17.2 us -> 20.2 us  [on_device(): main_call()]
    unnamed x6, local copies, waits for them, and re-layouts: 0.81 us -> 0.01 us
    ppermute x1, waiting for transfers between devices: 5.3 us -> 6.04 us  [moved(): lax.ppermute(value, axis, [(i, (i + step) % size) for i in range(size)])]
where the time goes in v6:
time: 66.4 us; the launch traced here: 66.2 us
  Pallas kernels  24.6 us (37%)
  blocking collectives  17.8 us (27%)
  starting transfers between devices  16 us (24%)
  waiting for transfers between devices  7.04 us (11%)
  between operations  0.76 us (1%)
    pallas_call x1, Pallas kernels, on_device(): main_call()  20.2 us
    all_to_all x1, blocking collectives, on_device(): gathered = lax.all_to_all(sums, ('gx', 'gy'), 0, 0, tiled=True)  17.8 us
    ppermute x3, starting transfers between devices, swapped(): second = lax.ppermute(value, axis, others)  9.13 us
    ppermute x1, waiting for transfers between devices, moved(): lax.ppermute(value, axis, [(i, (i + step) % size) for i in range(size)])  6.04 us
    ppermute x1, starting transfers between devices, moved(): lax.ppermute(value, axis, [(i, (i + step) % size) for i in range(size)])  4.42 us
    ppermute x3, starting transfers between devices, swapped(): return (lax.ppermute(value, axis, pairs), second)  2.49 us
    pallas_call x1, Pallas kernels, on_device(): strip_call()(rhs, materials.reshape(LANES, LANES), sigma_diag, sigma_off)  2.3 us
    pallas_call x1, Pallas kernels, on_device(): result, hessenberg = final_call()(gathered, a0, a1)  2.07 us
  transfers between devices with their start and end apart: 7, of which 2 were waited for; matrix products, arithmetic and copies ran while one was open for 0% of the time, Pallas kernels for 0%

profile of v6, /device:TPU:1, one launch (start us, length us, event | category | flops | bytes accessed | tf_op | source)
XLA Modules:
  0.0 66.2 jit_solution(3594000058322687546)
XLA Ops:
  0.6 0.0 copy-start
  0.6 0.0 copy-start.2
  0.7 2.3 %shard_map.59 = (f32[16,8,128]{2,1,0:T(8,128)}, f32[6,8,128]{2,1,0:T(8,128)}) custom-call(f32[6,128,128]{2,1,0:T(8,128)} %bitcast.12, s32[128,128]{1,0:T(8,128)} %bitcast.18, f32[3,8]{1,0:T(4,128)} %diag_in.1, f32[3,8]{1,0:T(4,128)} %off_in.1), custom_call_target="tpu_custom_call" | custom-call | tf_op jit(solution)/shard_map/pallas_call | solution.py:656
  3.0 3.1 %collective-permute-start.3 = (f32[16,8,128]{2,1,0:T(8,128)}, f32[16,8,128]{2,1,0:T(8,128)S(1)}, u32[]{:S(2)}, u32[]{:S(2)}) collective-permute-start(f32[16,8,128]{2,1,0:T(8,128)} %get-tuple-element.9), channel_id=1, source_target_pairs={{16,32},{32,16},{48,64},{64,48},{80,96},{96,80},{112,0},{0,112},{1... | collective-permute-start | bytes 196616 | tf_op jit(solution)/shard_map/ppermute | solution.py:649
  6.1 2.0 %collective-permute-start.2 = (f32[16,8,128]{2,1,0:T(8,128)}, f32[16,8,128]{2,1,0:T(8,128)S(1)}, u32[]{:S(2)}, u32[]{:S(2)}) collective-permute-start(f32[16,8,128]{2,1,0:T(8,128)} %get-tuple-element.9), channel_id=1, source_target_pairs={{0,16},{16,0},{32,48},{48,32},{64,80},{80,64},{96,112},{112,96},{1... | collective-permute-start | bytes 196616 | tf_op jit(solution)/shard_map/ppermute | solution.py:650
  8.0 0.0 copy-done
  8.0 4.9 %collective-permute-start.1 = (f32[6,128,128]{2,1,0:T(8,128)S(1)}, f32[6,128,128]{2,1,0:T(8,128)S(1)}, u32[]{:S(2)}, u32[]{:S(2)}) collective-permute-start(f32[6,128,128]{2,1,0:T(8,128)S(1)} %bitcast.13), channel_id=1, source_target_pairs={{1,2},{2,1},{3,4},{4,3},{5,6},{6,5},{7,8},{8,7},{9,10},{10,9},{11,... | collective-permute-start | bytes 1179656 | tf_op jit(solution)/shard_map/ppermute | solution.py:649
  12.9 0.0 collective-permute-start
  13.0 0.0 copy-done.2
  13.0 0.0 collective-permute-done.3
  13.0 0.0 collective-permute-done.2
  13.1 1.1 %collective-permute-start.5 = (f32[256,128]{1,0:T(8,128)S(1)}, f32[256,128]{1,0:T(8,128)S(1)}, u32[]{:S(2)}, u32[]{:S(2)}) collective-permute-start(f32[256,128]{1,0:T(8,128)S(1)} %maximum_bitcast_fusion.own_pack_ref), channel_id=1, source_target_pairs={{1,2},{2,1},{3,4},{4,3},{5,6},{6,5},{7,8},{8,7},{9,10},{10,9},{11,... | collective-permute-start | bytes 393224 | tf_op jit(solution)/shard_map/ppermute | solution.py:649
  14.2 0.5 collective-permute-start.4
  14.7 0.0 copy-start.1
  14.7 4.4 %collective-permute-start.6 = (f32[6,8,128]{2,1,0:T(8,128)S(1)}, f32[6,8,128]{2,1,0:T(8,128)S(1)}, u32[]{:S(2)}, u32[]{:S(2)}) collective-permute-start(f32[6,8,128]{2,1,0:T(8,128)S(1)} %pad_maximum_fusion), channel_id=1, source_target_pairs={{0,14},{1,15},{2,0},{3,1},{4,2},{5,3},{6,4},{7,5},{8,6},{9,7},{10,... | collective-permute-start | bytes 73736 | tf_op jit(solution)/shard_map/ppermute | solution.py:594
  19.1 6.0 %collective-permute-done.6.last_ref = f32[6,8,128]{2,1,0:T(8,128)S(1)} collective-permute-done((f32[6,8,128]{2,1,0:T(8,128)S(1)}, f32[6,8,128]{2,1,0:T(8,128)S(1)}, u32[]{:S(2)}, u32[]{:S(2)}) %collective-permute-start.6) | collective-permute-done | bytes 24608 | tf_op jit(solution)/shard_map/ppermute | solution.py:594
  25.2 0.0 collective-permute-done.5.second_pack_ref
  25.2 1.0 %collective-permute-done.4.first_pack_ref = f32[256,128]{1,0:T(8,128)S(1)} collective-permute-done((f32[256,128]{1,0:T(8,128)S(1)}, f32[256,128]{1,0:T(8,128)S(1)}, u32[]{:S(2)}, u32[]{:S(2)}) %collective-permute-start.4) | collective-permute-done | bytes 131104 | tf_op jit(solution)/shard_map/ppermute | solution.py:650
  26.2 0.0 collective-permute-done.1.second_ref
  26.2 0.0 collective-permute-done.first_ref
  26.2 0.0 copy-done.1
  26.2 20.2 %shard_map.60 = (f32[8,6,2,8,128]{4,3,2,1,0:T(8,128)S(1)}, f32[8,6,2,8,128]{4,3,2,1,0:T(8,128)S(1)}, f32[128,128]{1,0:T(8,128)S(1)}) custom-call(s32[1]{0:T(128)S(6)} %select_n.31.odd_ref, f32[6,128,128]{2,1,0:T(8,128)S(1)} %bitcast.15, f32[6,128,128]{2,1,0:T(8,128)S(1)} %collective-permute-done.first_ref, ...), custom_call_target="tpu_custom_call" | custom-call | tf_op jit(solution)/shard_map/pallas_call | solution.py:667
  46.4 17.8 %all_to_all.11 = f32[128,1,128]{2,1,0:T(1,128)S(1)} all-to-all(f32[128,1,128]{2,1,0:T(1,128)S(1)} %bitcast.17), channel_id=1, replica_groups=mesh['gx'=8,'gy'=16] {'gx','gy'}, dimensions={0} | all-to-all | bytes 131072 | tf_op jit(solution)/shard_map/all_to_all | solution.py:670
  64.2 2.1 %shard_map.61 = (f32[6,128,128]{2,1,0:T(8,128)}, f32[2,3]{1,0:T(2,128)}) custom-call(f32[128,128]{1,0:T(8,128)S(1)} %bitcast.16, f32[8,6,2,8,128]{4,3,2,1,0:T(8,128)S(1)} %get-tuple-element.12.a0_ref, f32[8,6,2,8,128]{4,3,2,1,0:T(8,128)S(1)} %get-tuple-element.13.a1_ref), custom_call_target="tpu_custom_call" | custom-call | tf_op jit(solution)/shard_map/pallas_call | solution.py:671
  (9 shorter events, 0.1 us)
Async XLA Ops:
  0.6 7.4 %copy-start = (f32[3,2,16,8,128]{4,3,2,1,0:T(8,128)S(1)}, f32[3,2,16,8,128]{4,3,2,1,0:T(8,128)}, u32[]{:S(2)}) copy-start(f32[3,2,16,8,128]{4,3,2,1,0:T(8,128)} %param.4) | copy-start | bytes 1179652
  0.6 12.3 %copy-start.2 = (s32[16,8,128]{2,1,0:T(8,128)S(1)}, s32[16,8,128]{2,1,0:T(8,128)}, u32[]{:S(2)}) copy-start(s32[16,8,128]{2,1,0:T(8,128)} %param.5) | copy-start | bytes 196612
  3.0 10.1 %collective-permute-start.3 = (f32[16,8,128]{2,1,0:T(8,128)}, f32[16,8,128]{2,1,0:T(8,128)S(1)}, u32[]{:S(2)}, u32[]{:S(2)}) collective-permute-start(f32[16,8,128]{2,1,0:T(8,128)} %get-tuple-element.9), channel_id=1, source_target_pairs={{16,32},{32,16},{48,64},{64,48},{80,96},{96,80},{112,0},{0,112},{1... | collective-permute-start | bytes 196616 | tf_op jit(solution)/shard_map/ppermute | solution.py:649
  6.1 7.0 %collective-permute-start.2 = (f32[16,8,128]{2,1,0:T(8,128)}, f32[16,8,128]{2,1,0:T(8,128)S(1)}, u32[]{:S(2)}, u32[]{:S(2)}) collective-permute-start(f32[16,8,128]{2,1,0:T(8,128)} %get-tuple-element.9), channel_id=1, source_target_pairs={{0,16},{16,0},{32,48},{48,32},{64,80},{80,64},{96,112},{112,96},{1... | collective-permute-start | bytes 196616 | tf_op jit(solution)/shard_map/ppermute | solution.py:650
  8.0 18.2 %collective-permute-start.1 = (f32[6,128,128]{2,1,0:T(8,128)S(1)}, f32[6,128,128]{2,1,0:T(8,128)S(1)}, u32[]{:S(2)}, u32[]{:S(2)}) collective-permute-start(f32[6,128,128]{2,1,0:T(8,128)S(1)} %bitcast.13), channel_id=1, source_target_pairs={{1,2},{2,1},{3,4},{4,3},{5,6},{6,5},{7,8},{8,7},{9,10},{10,9},{11,... | collective-permute-start | bytes 1179656 | tf_op jit(solution)/shard_map/ppermute | solution.py:649
  12.9 13.2 %collective-permute-start = (f32[6,128,128]{2,1,0:T(8,128)S(1)}, f32[6,128,128]{2,1,0:T(8,128)S(1)}, u32[]{:S(2)}, u32[]{:S(2)}) collective-permute-start(f32[6,128,128]{2,1,0:T(8,128)S(1)} %bitcast.14), channel_id=1, source_target_pairs={{0,1},{1,0},{2,3},{3,2},{4,5},{5,4},{6,7},{7,6},{8,9},{9,8},{10,11... | collective-permute-start | bytes 1179656 | tf_op jit(solution)/shard_map/ppermute | solution.py:650
  13.1 12.1 %collective-permute-start.5 = (f32[256,128]{1,0:T(8,128)S(1)}, f32[256,128]{1,0:T(8,128)S(1)}, u32[]{:S(2)}, u32[]{:S(2)}) collective-permute-start(f32[256,128]{1,0:T(8,128)S(1)} %maximum_bitcast_fusion.own_pack_ref), channel_id=1, source_target_pairs={{1,2},{2,1},{3,4},{4,3},{5,6},{6,5},{7,8},{8,7},{9,10},{10,9},{11,... | collective-permute-start | bytes 393224 | tf_op jit(solution)/shard_map/ppermute | solution.py:649
  14.2 12.0 %collective-permute-start.4 = (f32[256,128]{1,0:T(8,128)S(1)}, f32[256,128]{1,0:T(8,128)S(1)}, u32[]{:S(2)}, u32[]{:S(2)}) collective-permute-start(f32[256,128]{1,0:T(8,128)S(1)} %maximum_bitcast_fusion.own_pack_ref), channel_id=1, source_target_pairs={{0,1},{1,0},{2,3},{3,2},{4,5},{5,4},{6,7},{7,6},{8,9},{9,8},{10,11... | collective-permute-start | bytes 393224 | tf_op jit(solution)/shard_map/ppermute | solution.py:650
  14.7 11.5 %copy-start.1 = (f32[6,8,128]{2,1,0:T(8,128)S(1)}, f32[6,8,128]{2,1,0:T(8,128)}, u32[]{:S(2)}) copy-start(f32[6,8,128]{2,1,0:T(8,128)} %get-tuple-element.10.table_ref) | copy-start | bytes 73732
  14.7 10.5 %collective-permute-start.6 = (f32[6,8,128]{2,1,0:T(8,128)S(1)}, f32[6,8,128]{2,1,0:T(8,128)S(1)}, u32[]{:S(2)}, u32[]{:S(2)}) collective-permute-start(f32[6,8,128]{2,1,0:T(8,128)S(1)} %pad_maximum_fusion), channel_id=1, source_target_pairs={{0,14},{1,15},{2,0},{3,1},{4,2},{5,3},{6,4},{7,5},{8,6},{9,7},{10,... | collective-permute-start | bytes 73736 | tf_op jit(solution)/shard_map/ppermute | solution.py:594

commit v7 on v5

--- a/solution.py
+++ b/solution.py
@@ -86,7 +86,7 @@
 
 
 def strip_kernel(
-    rhs_in, mat_in, diag_in, off_in, strip_ref, cells_ref, table_ref,
+    rhs_in, mat_in, diag_in, off_in, strip_ref, cells_ref, table_ref, own_ref,
     rhs_ref, mat_ref, diag_ref, off_ref, arrived,
 ):
     pairs = ((mat_in, mat_ref), (rhs_in, rhs_ref), (diag_in, diag_ref), (off_in, off_ref))
@@ -95,6 +95,8 @@
         copy.start()
     for copy in copies:
         copy.wait()
+    own_copy = pltpu.make_async_copy(rhs_ref, own_ref, arrived.at[4])
+    own_copy.start()
     lane = lax.broadcasted_iota(jnp.int32, (SUBS, LANES), 1)
     half = STRIP // 2
 
@@ -126,6 +128,7 @@
         table_ref[c] = jnp.take_along_axis(single, lane // SUBS, axis=1) + jnp.take_along_axis(
             single, lane % SUBS, axis=1
         )
+    own_copy.wait()
 
 
 def wavefront(stages, events=()):
@@ -579,10 +582,10 @@
 def strip_call():
     return call(
         strip_kernel,
-        [((16,) + TILE, VMEM), ((16,) + TILE, VMEM), ((6,) + TILE, VMEM)],
+        [((16,) + TILE, VMEM), ((16,) + TILE, VMEM), ((6,) + TILE, VMEM), (BLOCK, ANY)],
         [ANY] * 4,
         floats(BLOCK) + [((LANES, LANES), jnp.int32)] + floats((3, SUBS), (3, SUBS)),
-        (4,),
+        (5,),
         60 * 2**20,
     )
 
@@ -622,7 +625,7 @@
 def on_device(right_side, materials, sigma_diag, sigma_off):
     rhs = right_side.reshape(BLOCK)
     bulk = swapped(rhs, "gy")
-    strips, cells, table = strip_call()(
+    strips, cells, table, own = strip_call()(
         rhs, materials.reshape(LANES, LANES), sigma_diag, sigma_off
     )
     first, second = swapped(strips, "gx")
@@ -633,7 +636,7 @@
     packs = swapped(pack, "gy")
     last = moved(pack[12:18], "gy", -2)
     a0, a1, sums = main_call()(
-        lax.axis_index("gy").reshape(1) % 2, rhs, *bulk, pack, *packs, last, table
+        lax.axis_index("gy").reshape(1) % 2, own, *bulk, pack, *packs, last, table
     )
     gathered = lax.all_to_all(sums, ("gx", "gy"), 0, 0, tiled=True)
     result, hessenberg = final_call()(gathered, a0, a1)

time: 63.2 us -> 62.5 us (0.989)
  waiting for transfers between devices: 6.31 us -> 2.27 us
  blocking collectives: 17.8 us -> 20.5 us
  other arithmetic: 0.03 us -> 0.87 us
  local copies, waits for them, and re-layouts: 0.81 us -> 0.01 us
    ppermute x1, waiting for transfers between devices: 5.3 us -> 0.95 us  [moved(): lax.ppermute(value, axis, [(i, (i + step) % size) for i in range(size)])]
    all_to_all x1, blocking collectives: 17.8 us -> 20.5 us  [on_device(): gathered = lax.all_to_all(sums, ('gx', 'gy'), 0, 0, tiled=True)]
    ppermute x3, waiting for transfers between devices: 0.01 us -> 0.99 us  [swapped(): second = lax.ppermute(value, axis, others)]
    concatenate x1, other arithmetic: 0.01 us -> 0.85 us  [on_device(): jnp.concatenate([mixed, jnp.where(odd, second[14:], first[14:]), cells])]
    unnamed x6 -> x4, local copies, waits for them, and re-layouts: 0.81 us -> 0.01 us
    ppermute x3, waiting for transfers between devices: 1 us -> 0.34 us  [swapped(): return (lax.ppermute(value, axis, pairs), second)]
  transfers between devices with their start and end apart: 7 -> 7, of which waited for: 2 -> 4; matrix products, arithmetic and copies ran while one was open for 0% -> 1% of each run, Pallas kernels for 0% -> 4%
where the time goes in v7:
time: 62.5 us; the launch traced here: 62.3 us
  Pallas kernels  21.8 us (35%)
  blocking collectives  20.5 us (33%)
  starting transfers between devices  16.1 us (26%)
  waiting for transfers between devices  2.27 us (4%)
  other arithmetic  0.87 us (1%)
  between operations  0.7 us (1%)
    all_to_all x1, blocking collectives, on_device(): gathered = lax.all_to_all(sums, ('gx', 'gy'), 0, 0, tiled=True)  20.5 us
    pallas_call x1, Pallas kernels, on_device(): main_call()  17.2 us
    ppermute x3, starting transfers between devices, swapped(): second = lax.ppermute(value, axis, others)  9.24 us
    ppermute x1, starting transfers between devices, moved(): lax.ppermute(value, axis, [(i, (i + step) % size) for i in range(size)])  4.44 us
    pallas_call x1, Pallas kernels, on_device(): strip_call()(rhs, materials.reshape(LANES, LANES), sigma_diag, sigma_off)  2.52 us
    ppermute x3, starting transfers between devices, swapped(): return (lax.ppermute(value, axis, pairs), second)  2.43 us
    pallas_call x1, Pallas kernels, on_device(): result, hessenberg = final_call()(gathered, a0, a1)  2.07 us
  transfers between devices with their start and end apart: 7, of which 4 were waited for; matrix products, arithmetic and copies ran while one was open for 1% of the time, Pallas kernels for 4%

profile of v7, /device:TPU:1, one launch (start us, length us, event | category | flops | bytes accessed | tf_op | source)
XLA Modules:
  0.0 62.3 jit_solution(6848613619368914147)
XLA Ops:
  0.6 5.8 %collective-permute-start.1 = (f32[6,128,128]{2,1,0:T(8,128)}, f32[6,128,128]{2,1,0:T(8,128)S(1)}, u32[]{:S(2)}, u32[]{:S(2)}) collective-permute-start(f32[6,128,128]{2,1,0:T(8,128)} %bitcast.11), channel_id=1, source_target_pairs={{1,2},{2,1},{3,4},{4,3},{5,6},{6,5},{7,8},{8,7},{9,10},{10,9},{11,... | collective-permute-start | bytes 1179656 | tf_op jit(solution)/shard_map/ppermute | solution.py:621
  6.5 0.0 collective-permute-start
  6.5 2.5 %shard_map.59 = (f32[16,8,128]{2,1,0:T(8,128)}, f32[16,8,128]{2,1,0:T(8,128)}, f32[6,8,128]{2,1,0:T(8,128)}, f32[6,128,128]{2,1,0:T(8,128)}) custom-call(f32[6,128,128]{2,1,0:T(8,128)} %bitcast.13, s32[128,128]{1,0:T(8,128)} %bitcast.14, f32[3,8]{1,0:T(4,128)} %diag_in.1, f32[3,8]{1,0:T(4,128)} %off_in.1), custom_call_target="tpu_custom_call" | custom-call | tf_op jit(solution)/shard_map/pallas_call | solution.py:628
  9.0 0.0 copy-start
  9.0 2.6 %collective-permute-start.3 = (f32[16,8,128]{2,1,0:T(8,128)}, f32[16,8,128]{2,1,0:T(8,128)S(1)}, u32[]{:S(2)}, u32[]{:S(2)}) collective-permute-start(f32[16,8,128]{2,1,0:T(8,128)} %get-tuple-element.12), channel_id=1, source_target_pairs={{16,32},{32,16},{48,64},{64,48},{80,96},{96,80},{112,0},{0,112},{1... | collective-permute-start | bytes 196616 | tf_op jit(solution)/shard_map/ppermute | solution.py:621
  11.6 1.7 %collective-permute-start.2 = (f32[16,8,128]{2,1,0:T(8,128)}, f32[16,8,128]{2,1,0:T(8,128)S(1)}, u32[]{:S(2)}, u32[]{:S(2)}) collective-permute-start(f32[16,8,128]{2,1,0:T(8,128)} %get-tuple-element.12), channel_id=1, source_target_pairs={{0,16},{16,0},{32,48},{48,32},{64,80},{80,64},{96,112},{112,96},{1... | collective-permute-start | bytes 196616 | tf_op jit(solution)/shard_map/ppermute | solution.py:622
  13.3 0.8 %collective-permute-done.3 = f32[16,8,128]{2,1,0:T(8,128)S(1)} collective-permute-done((f32[16,8,128]{2,1,0:T(8,128)}, f32[16,8,128]{2,1,0:T(8,128)S(1)}, u32[]{:S(2)}, u32[]{:S(2)}) %collective-permute-start.3) | collective-permute-done | bytes 65568 | tf_op jit(solution)/shard_map/ppermute | solution.py:621
  14.0 0.3 collective-permute-done.2
  14.4 0.9 %pad_maximum_fusion.own_pack_ref = f32[32,8,128]{2,1,0:T(8,128)S(1)} fusion(f32[16,8,128]{2,1,0:T(8,128)} %get-tuple-element.13, f32[2,8,128]{2,1,0:T(8,128)S(1)} %slice_select_fusion.1, f32[14,8,128]{2,1,0:T(8,128)S(1)} %slice_select_fusion), kind=kLoop, calls=%fused_computation | loop fusion | flops 65536 | bytes 262144 | tf_op jit(solution)/shard_map/concatenate | solution.py:635
  15.2 0.8 %collective-permute-start.5 = (f32[32,8,128]{2,1,0:T(8,128)S(1)}, f32[32,8,128]{2,1,0:T(8,128)S(1)}, u32[]{:S(2)}, u32[]{:S(2)}) collective-permute-start(f32[32,8,128]{2,1,0:T(8,128)S(1)} %pad_maximum_fusion.own_pack_ref), channel_id=1, source_target_pairs={{1,2},{2,1},{3,4},{4,3},{5,6},{6,5},{7,8},{8,7},{9,10},{10,9},{11,... | collective-permute-start | bytes 393224 | tf_op jit(solution)/shard_map/ppermute | solution.py:621
  16.1 0.8 %collective-permute-start.4 = (f32[32,8,128]{2,1,0:T(8,128)S(1)}, f32[32,8,128]{2,1,0:T(8,128)S(1)}, u32[]{:S(2)}, u32[]{:S(2)}) collective-permute-start(f32[32,8,128]{2,1,0:T(8,128)S(1)} %pad_maximum_fusion.own_pack_ref), channel_id=1, source_target_pairs={{0,1},{1,0},{2,3},{3,2},{4,5},{5,4},{6,7},{7,6},{8,9},{9,8},{10,11... | collective-permute-start | bytes 393224 | tf_op jit(solution)/shard_map/ppermute | solution.py:622
  16.8 0.0 copy-start.1
  16.9 4.4 %collective-permute-start.6 = (f32[6,8,128]{2,1,0:T(8,128)S(1)}, f32[6,8,128]{2,1,0:T(8,128)S(1)}, u32[]{:S(2)}, u32[]{:S(2)}) collective-permute-start(f32[6,8,128]{2,1,0:T(8,128)S(1)} %slice.24), channel_id=1, source_target_pairs={{0,14},{1,15},{2,0},{3,1},{4,2},{5,3},{6,4},{7,5},{8,6},{9,7},{10,... | collective-permute-start | bytes 73736 | tf_op jit(solution)/shard_map/ppermute | solution.py:566
  21.3 0.9 %collective-permute-done.6.last_ref = f32[6,8,128]{2,1,0:T(8,128)S(1)} collective-permute-done((f32[6,8,128]{2,1,0:T(8,128)S(1)}, f32[6,8,128]{2,1,0:T(8,128)S(1)}, u32[]{:S(2)}, u32[]{:S(2)}) %collective-permute-start.6) | collective-permute-done | bytes 24608 | tf_op jit(solution)/shard_map/ppermute | solution.py:566
  22.2 0.2 collective-permute-done.5.second_pack_ref
  22.5 0.0 collective-permute-done.4.first_pack_ref
  22.5 0.0 collective-permute-done.1.second_ref
  22.5 0.0 collective-permute-done.first_ref
  22.5 0.0 copy-done
  22.5 0.0 copy-done.1
  22.5 17.2 %shard_map.60 = (f32[8,6,2,8,128]{4,3,2,1,0:T(8,128)S(1)}, f32[8,6,2,8,128]{4,3,2,1,0:T(8,128)S(1)}, f32[128,128]{1,0:T(8,128)S(1)}) custom-call(s32[1]{0:T(128)S(6)} %select_n.31.odd_ref, f32[6,128,128]{2,1,0:T(8,128)S(1)} %copy-done, f32[6,128,128]{2,1,0:T(8,128)S(1)} %collective-permute-done.first_ref, ...), custom_call_target="tpu_custom_call" | custom-call | tf_op jit(solution)/shard_map/pallas_call | solution.py:638
  39.7 20.5 %all_to_all.11 = f32[128,1,128]{2,1,0:T(1,128)S(1)} all-to-all(f32[128,1,128]{2,1,0:T(1,128)S(1)} %bitcast.10), channel_id=1, replica_groups=mesh['gx'=8,'gy'=16] {'gx','gy'}, dimensions={0} | all-to-all | bytes 131072 | tf_op jit(solution)/shard_map/all_to_all | solution.py:641
  60.2 2.1 %shard_map.61 = (f32[6,128,128]{2,1,0:T(8,128)}, f32[2,3]{1,0:T(2,128)}) custom-call(f32[128,128]{1,0:T(8,128)S(1)} %bitcast.9, f32[8,6,2,8,128]{4,3,2,1,0:T(8,128)S(1)} %get-tuple-element.16.a0_ref, f32[8,6,2,8,128]{4,3,2,1,0:T(8,128)S(1)} %get-tuple-element.17.a1_ref), custom_call_target="tpu_custom_call" | custom-call | tf_op jit(solution)/shard_map/pallas_call | solution.py:642
  (5 shorter events, 0.0 us)
Async XLA Ops:
  0.6 21.8 %collective-permute-start.1 = (f32[6,128,128]{2,1,0:T(8,128)}, f32[6,128,128]{2,1,0:T(8,128)S(1)}, u32[]{:S(2)}, u32[]{:S(2)}) collective-permute-start(f32[6,128,128]{2,1,0:T(8,128)} %bitcast.11), channel_id=1, source_target_pairs={{1,2},{2,1},{3,4},{4,3},{5,6},{6,5},{7,8},{8,7},{9,10},{10,9},{11,... | collective-permute-start | bytes 1179656 | tf_op jit(solution)/shard_map/ppermute | solution.py:621
  6.5 16.0 %collective-permute-start = (f32[6,128,128]{2,1,0:T(8,128)}, f32[6,128,128]{2,1,0:T(8,128)S(1)}, u32[]{:S(2)}, u32[]{:S(2)}) collective-permute-start(f32[6,128,128]{2,1,0:T(8,128)} %bitcast.12), channel_id=1, source_target_pairs={{0,1},{1,0},{2,3},{3,2},{4,5},{5,4},{6,7},{7,6},{8,9},{9,8},{10,11... | collective-permute-start | bytes 1179656 | tf_op jit(solution)/shard_map/ppermute | solution.py:622
  9.0 13.5 %copy-start = (f32[6,128,128]{2,1,0:T(8,128)S(1)}, f32[6,128,128]{2,1,0:T(8,128)}, u32[]{:S(2)}) copy-start(f32[6,128,128]{2,1,0:T(8,128)} %get-tuple-element.11.own_ref) | copy-start | bytes 1179652
  9.0 5.0 %collective-permute-start.3 = (f32[16,8,128]{2,1,0:T(8,128)}, f32[16,8,128]{2,1,0:T(8,128)S(1)}, u32[]{:S(2)}, u32[]{:S(2)}) collective-permute-start(f32[16,8,128]{2,1,0:T(8,128)} %get-tuple-element.12), channel_id=1, source_target_pairs={{16,32},{32,16},{48,64},{64,48},{80,96},{96,80},{112,0},{0,112},{1... | collective-permute-start | bytes 196616 | tf_op jit(solution)/shard_map/ppermute | solution.py:621
  11.6 2.8 %collective-permute-start.2 = (f32[16,8,128]{2,1,0:T(8,128)}, f32[16,8,128]{2,1,0:T(8,128)S(1)}, u32[]{:S(2)}, u32[]{:S(2)}) collective-permute-start(f32[16,8,128]{2,1,0:T(8,128)} %get-tuple-element.12), channel_id=1, source_target_pairs={{0,16},{16,0},{32,48},{48,32},{64,80},{80,64},{96,112},{112,96},{1... | collective-permute-start | bytes 196616 | tf_op jit(solution)/shard_map/ppermute | solution.py:622
  15.2 7.2 %collective-permute-start.5 = (f32[32,8,128]{2,1,0:T(8,128)S(1)}, f32[32,8,128]{2,1,0:T(8,128)S(1)}, u32[]{:S(2)}, u32[]{:S(2)}) collective-permute-start(f32[32,8,128]{2,1,0:T(8,128)S(1)} %pad_maximum_fusion.own_pack_ref), channel_id=1, source_target_pairs={{1,2},{2,1},{3,4},{4,3},{5,6},{6,5},{7,8},{8,7},{9,10},{10,9},{11,... | collective-permute-start | bytes 393224 | tf_op jit(solution)/shard_map/ppermute | solution.py:621
  16.1 6.4 %collective-permute-start.4 = (f32[32,8,128]{2,1,0:T(8,128)S(1)}, f32[32,8,128]{2,1,0:T(8,128)S(1)}, u32[]{:S(2)}, u32[]{:S(2)}) collective-permute-start(f32[32,8,128]{2,1,0:T(8,128)S(1)} %pad_maximum_fusion.own_pack_ref), channel_id=1, source_target_pairs={{0,1},{1,0},{2,3},{3,2},{4,5},{5,4},{6,7},{7,6},{8,9},{9,8},{10,11... | collective-permute-start | bytes 393224 | tf_op jit(solution)/shard_map/ppermute | solution.py:622
  16.8 5.6 %copy-start.1 = (f32[6,8,128]{2,1,0:T(8,128)S(1)}, f32[6,8,128]{2,1,0:T(8,128)}, u32[]{:S(2)}) copy-start(f32[6,8,128]{2,1,0:T(8,128)} %get-tuple-element.14.table_ref) | copy-start | bytes 73732
  16.9 5.4 %collective-permute-start.6 = (f32[6,8,128]{2,1,0:T(8,128)S(1)}, f32[6,8,128]{2,1,0:T(8,128)S(1)}, u32[]{:S(2)}, u32[]{:S(2)}) collective-permute-start(f32[6,8,128]{2,1,0:T(8,128)S(1)} %slice.24), channel_id=1, source_target_pairs={{0,14},{1,15},{2,0},{3,1},{4,2},{5,3},{6,4},{7,5},{8,6},{9,7},{10,... | collective-permute-start | bytes 73736 | tf_op jit(solution)/shard_map/ppermute | solution.py:566

commit v8 on v7

--- a/solution.py
+++ b/solution.py
@@ -336,7 +336,7 @@
     def beyond(y):
         for z in range(2):
             mat[y, 2 * z] = last[4 + z]
-            mat[y, 2 * z + 1] = cell_halo(last[z], last[2 + z], 0)
+            mat[y, 2 * z + 1] = jnp.where(lane < LANES // 2, last[2 + z], last[z])
 
     def indices(y):
         ids = Field(mat[y, k] for k in range(4))
@@ -628,13 +628,16 @@
     strips, cells, table, own = strip_call()(
         rhs, materials.reshape(LANES, LANES), sigma_diag, sigma_off
     )
+    row = moved(materials[:, 0, :].astype(jnp.float32).reshape((2,) + TILE), "gy", -2)
     first, second = swapped(strips, "gx")
     odd = lax.axis_index("gx") % 2 == 1
     lane = lax.broadcasted_iota(jnp.int32, (14,) + TILE, 2)
     mixed = jnp.where((lane % STRIP < STRIP // 2) == odd, first[:14], second[:14])
     pack = jnp.concatenate([mixed, jnp.where(odd, second[14:], first[14:]), cells])
     packs = swapped(pack, "gy")
-    last = moved(pack[12:18], "gy", -2)
+    side_first, side_second = swapped(row, "gx")
+    left, right = jnp.where(odd, side_first, side_second), jnp.where(odd, side_second, side_first)
+    last = jnp.concatenate([left, right, row])
     a0, a1, sums = main_call()(
         lax.axis_index("gy").reshape(1) % 2, own, *bulk, pack, *packs, last, table
     )

time: 62.5 us -> 67.8 us (1.085)
  waiting for transfers between devices: 2.27 us -> 7.5 us
  blocking collectives: 20.5 us -> 17.6 us
  starting transfers between devices: 16.1 us -> 18.2 us
  other arithmetic: 0.87 us -> 1.73 us
    ppermute x3 -> x4, starting transfers between devices: 9.24 us -> 15.2 us  [swapped(): second = lax.ppermute(value, axis, others)]
    ppermute x1, starting transfers between devices: 4.44 us -> 1.24 us  [moved(): lax.ppermute(value, axis, [(i, (i + step) % size) for i in range(size)])]
    all_to_all x1, blocking collectives: 20.5 us -> 17.6 us  [on_device(): gathered = lax.all_to_all(sums, ('gx', 'gy'), 0, 0, tiled=True)]
    ppermute x3 -> x4, waiting for transfers between devices: 0.99 us -> 3.62 us  [swapped(): second = lax.ppermute(value, axis, others)]
    ppermute x1, waiting for transfers between devices: 0.95 us -> 2.76 us  [moved(): lax.ppermute(value, axis, [(i, (i + step) % size) for i in range(size)])]
    convert_element_type x0 -> x1, other arithmetic: none -> 0.84 us  [on_device(): materials[:, 0, :].astype(jnp.float32).reshape((2,) + TILE)]
    ppermute x3 -> x4, waiting for transfers between devices: 0.34 us -> 1.12 us  [swapped(): return (lax.ppermute(value, axis, pairs), second)]
    ppermute x3 -> x4, starting transfers between devices: 2.43 us -> 1.68 us  [swapped(): return (lax.ppermute(value, axis, pairs), second)]
  transfers between devices with their start and end apart: 7 -> 9, of which waited for: 4 -> 3; matrix products, arithmetic and copies ran while one was open for 1% -> 3% of each run, Pallas kernels for 4% -> 4%
where the time goes in v8:
time: 67.8 us; the launch traced here: 67.5 us
  Pallas kernels  21.8 us (32%)
  starting transfers between devices  18.2 us (27%)
  blocking collectives  17.6 us (26%)
  waiting for transfers between devices  7.5 us (11%)
  other arithmetic  1.73 us (3%)
  between operations  0.72 us (1%)
    all_to_all x1, blocking collectives, on_device(): gathered = lax.all_to_all(sums, ('gx', 'gy'), 0, 0, tiled=True)  17.6 us
    pallas_call x1, Pallas kernels, on_device(): main_call()  17.2 us
    ppermute x4, starting transfers between devices, swapped(): second = lax.ppermute(value, axis, others)  15.2 us
    ppermute x4, waiting for transfers between devices, swapped(): second = lax.ppermute(value, axis, others)  3.62 us
    ppermute x1, waiting for transfers between devices, moved(): lax.ppermute(value, axis, [(i, (i + step) % size) for i in range(size)])  2.76 us
    pallas_call x1, Pallas kernels, on_device(): strip_call()(rhs, materials.reshape(LANES, LANES), sigma_diag, sigma_off)  2.52 us
    pallas_call x1, Pallas kernels, on_device(): result, hessenberg = final_call()(gathered, a0, a1)  2.07 us
    ppermute x4, starting transfers between devices, swapped(): return (lax.ppermute(value, axis, pairs), second)  1.68 us
  transfers between devices with their start and end apart: 9, of which 3 were waited for; matrix products, arithmetic and copies ran while one was open for 3% of the time, Pallas kernels for 4%

profile of v8, /device:TPU:1, one launch (start us, length us, event | category | flops | bytes accessed | tf_op | source)
XLA Modules:
  0.0 67.5 jit_solution(14874061068336416901)
XLA Ops:
  0.6 5.8 %collective-permute-start.1 = (f32[6,128,128]{2,1,0:T(8,128)}, f32[6,128,128]{2,1,0:T(8,128)S(1)}, u32[]{:S(2)}, u32[]{:S(2)}) collective-permute-start(f32[6,128,128]{2,1,0:T(8,128)} %bitcast.12), channel_id=1, source_target_pairs={{1,2},{2,1},{3,4},{4,3},{5,6},{6,5},{7,8},{8,7},{9,10},{10,9},{11,... | collective-permute-start | bytes 1179656 | tf_op jit(solution)/shard_map/ppermute | solution.py:621
  6.5 0.0 collective-permute-start
  6.5 2.5 %shard_map.59 = (f32[16,8,128]{2,1,0:T(8,128)}, f32[16,8,128]{2,1,0:T(8,128)}, f32[6,8,128]{2,1,0:T(8,128)}, f32[6,128,128]{2,1,0:T(8,128)}) custom-call(f32[6,128,128]{2,1,0:T(8,128)} %bitcast.14, s32[128,128]{1,0:T(8,128)} %bitcast.15, f32[3,8]{1,0:T(4,128)} %diag_in.1, f32[3,8]{1,0:T(4,128)} %off_in.1), custom_call_target="tpu_custom_call" | custom-call | tf_op jit(solution)/shard_map/pallas_call | solution.py:628
  9.0 0.0 copy-start
  9.0 2.6 %collective-permute-start.3 = (f32[16,8,128]{2,1,0:T(8,128)}, f32[16,8,128]{2,1,0:T(8,128)S(1)}, u32[]{:S(2)}, u32[]{:S(2)}) collective-permute-start(f32[16,8,128]{2,1,0:T(8,128)} %get-tuple-element.12), channel_id=1, source_target_pairs={{16,32},{32,16},{48,64},{64,48},{80,96},{96,80},{112,0},{0,112},{1... | collective-permute-start | bytes 196616 | tf_op jit(solution)/shard_map/ppermute | solution.py:621
  11.6 1.7 %collective-permute-start.2 = (f32[16,8,128]{2,1,0:T(8,128)}, f32[16,8,128]{2,1,0:T(8,128)S(1)}, u32[]{:S(2)}, u32[]{:S(2)}) collective-permute-start(f32[16,8,128]{2,1,0:T(8,128)} %get-tuple-element.12), channel_id=1, source_target_pairs={{0,16},{16,0},{32,48},{48,32},{64,80},{80,64},{96,112},{112,96},{1... | collective-permute-start | bytes 196616 | tf_op jit(solution)/shard_map/ppermute | solution.py:622
  13.2 0.8 %slice_convert_fusion = f32[16,1,128]{2,1,0:T(1,128)S(1)} fusion(s32[16,8,128]{2,1,0:T(8,128)} %param.5), kind=kLoop, calls=%fused_computation.6 | loop fusion | flops 2048 | bytes 16384 | tf_op jit(solution)/shard_map/convert_element_type | solution.py:631
  14.1 1.2 %collective-permute-start.6 = (f32[2,8,128]{2,1,0:T(8,128)S(1)}, f32[2,8,128]{2,1,0:T(8,128)S(1)}, u32[]{:S(2)}, u32[]{:S(2)}) collective-permute-start(f32[2,8,128]{2,1,0:T(8,128)S(1)} %bitcast.16), channel_id=1, source_target_pairs={{0,14},{1,15},{2,0},{3,1},{4,2},{5,3},{6,4},{7,5},{8,6},{9,7},{10,... | collective-permute-start | bytes 24584 | tf_op jit(solution)/shard_map/ppermute | solution.py:566
  15.3 2.8 %collective-permute-done.6 = f32[2,8,128]{2,1,0:T(8,128)S(1)} collective-permute-done((f32[2,8,128]{2,1,0:T(8,128)S(1)}, f32[2,8,128]{2,1,0:T(8,128)S(1)}, u32[]{:S(2)}, u32[]{:S(2)}) %collective-permute-start.6) | collective-permute-done | bytes 8224 | tf_op jit(solution)/shard_map/ppermute | solution.py:566
  18.1 1.5 %collective-permute-start.8 = (f32[2,8,128]{2,1,0:T(8,128)S(1)}, f32[2,8,128]{2,1,0:T(8,128)S(1)}, u32[]{:S(2)}, u32[]{:S(2)}) collective-permute-start(f32[2,8,128]{2,1,0:T(8,128)S(1)} %collective-permute-done.6), channel_id=1, source_target_pairs={{16,32},{32,16},{48,64},{64,48},{80,96},{96,80},{112,0},{0,112},{1... | collective-permute-start | bytes 24584 | tf_op jit(solution)/shard_map/ppermute | solution.py:621
  19.6 0.0 collective-permute-done.3
  19.6 0.0 collective-permute-start.7
  19.6 0.0 collective-permute-done.2
  19.6 0.9 %pad_maximum_fusion.own_pack_ref = f32[32,8,128]{2,1,0:T(8,128)S(1)} fusion(f32[16,8,128]{2,1,0:T(8,128)} %get-tuple-element.13, f32[2,8,128]{2,1,0:T(8,128)S(1)} %slice_select_fusion.1, f32[14,8,128]{2,1,0:T(8,128)S(1)} %slice_select_fusion), kind=kLoop, calls=%fused_computation | loop fusion | flops 65536 | bytes 262144 | tf_op jit(solution)/shard_map/concatenate | solution.py:636
  20.5 5.3 %collective-permute-start.5 = (f32[32,8,128]{2,1,0:T(8,128)S(1)}, f32[32,8,128]{2,1,0:T(8,128)S(1)}, u32[]{:S(2)}, u32[]{:S(2)}) collective-permute-start(f32[32,8,128]{2,1,0:T(8,128)S(1)} %pad_maximum_fusion.own_pack_ref), channel_id=1, source_target_pairs={{1,2},{2,1},{3,4},{4,3},{5,6},{6,5},{7,8},{8,7},{9,10},{10,9},{11,... | collective-permute-start | bytes 393224 | tf_op jit(solution)/shard_map/ppermute | solution.py:621
  25.8 0.0 collective-permute-done.8
  25.8 0.0 collective-permute-start.4
  25.8 0.0 collective-permute-done.7
  25.9 0.0 copy-start.1
  25.9 3.6 %collective-permute-done.5.second_pack_ref = f32[32,8,128]{2,1,0:T(8,128)S(1)} collective-permute-done((f32[32,8,128]{2,1,0:T(8,128)S(1)}, f32[32,8,128]{2,1,0:T(8,128)S(1)}, u32[]{:S(2)}, u32[]{:S(2)}) %collective-permute-start.5) | collective-permute-done | bytes 131104 | tf_op jit(solution)/shard_map/ppermute | solution.py:621
  29.5 1.1 %collective-permute-done.4.first_pack_ref = f32[32,8,128]{2,1,0:T(8,128)S(1)} collective-permute-done((f32[32,8,128]{2,1,0:T(8,128)S(1)}, f32[32,8,128]{2,1,0:T(8,128)S(1)}, u32[]{:S(2)}, u32[]{:S(2)}) %collective-permute-start.4) | collective-permute-done | bytes 131104 | tf_op jit(solution)/shard_map/ppermute | solution.py:622
  30.6 0.0 collective-permute-done.1.second_ref
  30.6 0.0 collective-permute-done.first_ref
  30.6 0.0 copy-done
  30.6 0.0 copy-done.1
  30.6 17.2 %shard_map.60 = (f32[8,6,2,8,128]{4,3,2,1,0:T(8,128)S(1)}, f32[8,6,2,8,128]{4,3,2,1,0:T(8,128)S(1)}, f32[128,128]{1,0:T(8,128)S(1)}) custom-call(s32[1]{0:T(128)S(6)} %select_n.39.odd_ref, f32[6,128,128]{2,1,0:T(8,128)S(1)} %copy-done, f32[6,128,128]{2,1,0:T(8,128)S(1)} %collective-permute-done.first_ref, ...), custom_call_target="tpu_custom_call" | custom-call | tf_op jit(solution)/shard_map/pallas_call | solution.py:641
  47.9 17.6 %all_to_all.11 = f32[128,1,128]{2,1,0:T(1,128)S(1)} all-to-all(f32[128,1,128]{2,1,0:T(1,128)S(1)} %bitcast.11), channel_id=1, replica_groups=mesh['gx'=8,'gy'=16] {'gx','gy'}, dimensions={0} | all-to-all | bytes 131072 | tf_op jit(solution)/shard_map/all_to_all | solution.py:644
  65.5 2.1 %shard_map.61 = (f32[6,128,128]{2,1,0:T(8,128)}, f32[2,3]{1,0:T(2,128)}) custom-call(f32[128,128]{1,0:T(8,128)S(1)} %bitcast.10, f32[8,6,2,8,128]{4,3,2,1,0:T(8,128)S(1)} %get-tuple-element.16.a0_ref, f32[8,6,2,8,128]{4,3,2,1,0:T(8,128)S(1)} %get-tuple-element.17.a1_ref), custom_call_target="tpu_custom_call" | custom-call | tf_op jit(solution)/shard_map/pallas_call | solution.py:645
  (6 shorter events, 0.0 us)
Async XLA Ops:
  0.6 30.0 %collective-permute-start.1 = (f32[6,128,128]{2,1,0:T(8,128)}, f32[6,128,128]{2,1,0:T(8,128)S(1)}, u32[]{:S(2)}, u32[]{:S(2)}) collective-permute-start(f32[6,128,128]{2,1,0:T(8,128)} %bitcast.12), channel_id=1, source_target_pairs={{1,2},{2,1},{3,4},{4,3},{5,6},{6,5},{7,8},{8,7},{9,10},{10,9},{11,... | collective-permute-start | bytes 1179656 | tf_op jit(solution)/shard_map/ppermute | solution.py:621
  6.5 24.2 %collective-permute-start = (f32[6,128,128]{2,1,0:T(8,128)}, f32[6,128,128]{2,1,0:T(8,128)S(1)}, u32[]{:S(2)}, u32[]{:S(2)}) collective-permute-start(f32[6,128,128]{2,1,0:T(8,128)} %bitcast.13), channel_id=1, source_target_pairs={{0,1},{1,0},{2,3},{3,2},{4,5},{5,4},{6,7},{7,6},{8,9},{9,8},{10,11... | collective-permute-start | bytes 1179656 | tf_op jit(solution)/shard_map/ppermute | solution.py:622
  9.0 21.6 %copy-start = (f32[6,128,128]{2,1,0:T(8,128)S(1)}, f32[6,128,128]{2,1,0:T(8,128)}, u32[]{:S(2)}) copy-start(f32[6,128,128]{2,1,0:T(8,128)} %get-tuple-element.11.own_ref) | copy-start | bytes 1179652
  9.0 10.6 %collective-permute-start.3 = (f32[16,8,128]{2,1,0:T(8,128)}, f32[16,8,128]{2,1,0:T(8,128)S(1)}, u32[]{:S(2)}, u32[]{:S(2)}) collective-permute-start(f32[16,8,128]{2,1,0:T(8,128)} %get-tuple-element.12), channel_id=1, source_target_pairs={{16,32},{32,16},{48,64},{64,48},{80,96},{96,80},{112,0},{0,112},{1... | collective-permute-start | bytes 196616 | tf_op jit(solution)/shard_map/ppermute | solution.py:621
  11.6 8.0 %collective-permute-start.2 = (f32[16,8,128]{2,1,0:T(8,128)}, f32[16,8,128]{2,1,0:T(8,128)S(1)}, u32[]{:S(2)}, u32[]{:S(2)}) collective-permute-start(f32[16,8,128]{2,1,0:T(8,128)} %get-tuple-element.12), channel_id=1, source_target_pairs={{0,16},{16,0},{32,48},{48,32},{64,80},{80,64},{96,112},{112,96},{1... | collective-permute-start | bytes 196616 | tf_op jit(solution)/shard_map/ppermute | solution.py:622
  14.1 4.0 %collective-permute-start.6 = (f32[2,8,128]{2,1,0:T(8,128)S(1)}, f32[2,8,128]{2,1,0:T(8,128)S(1)}, u32[]{:S(2)}, u32[]{:S(2)}) collective-permute-start(f32[2,8,128]{2,1,0:T(8,128)S(1)} %bitcast.16), channel_id=1, source_target_pairs={{0,14},{1,15},{2,0},{3,1},{4,2},{5,3},{6,4},{7,5},{8,6},{9,7},{10,... | collective-permute-start | bytes 24584 | tf_op jit(solution)/shard_map/ppermute | solution.py:566
  18.1 7.7 %collective-permute-start.8 = (f32[2,8,128]{2,1,0:T(8,128)S(1)}, f32[2,8,128]{2,1,0:T(8,128)S(1)}, u32[]{:S(2)}, u32[]{:S(2)}) collective-permute-start(f32[2,8,128]{2,1,0:T(8,128)S(1)} %collective-permute-done.6), channel_id=1, source_target_pairs={{16,32},{32,16},{48,64},{64,48},{80,96},{96,80},{112,0},{0,112},{1... | collective-permute-start | bytes 24584 | tf_op jit(solution)/shard_map/ppermute | solution.py:621
  19.6 6.2 %collective-permute-start.7 = (f32[2,8,128]{2,1,0:T(8,128)S(1)}, f32[2,8,128]{2,1,0:T(8,128)S(1)}, u32[]{:S(2)}, u32[]{:S(2)}) collective-permute-start(f32[2,8,128]{2,1,0:T(8,128)S(1)} %collective-permute-done.6), channel_id=1, source_target_pairs={{0,16},{16,0},{32,48},{48,32},{64,80},{80,64},{96,112},{112,96},{1... | collective-permute-start | bytes 24584 | tf_op jit(solution)/shard_map/ppermute | solution.py:622
  20.5 9.0 %collective-permute-start.5 = (f32[32,8,128]{2,1,0:T(8,128)S(1)}, f32[32,8,128]{2,1,0:T(8,128)S(1)}, u32[]{:S(2)}, u32[]{:S(2)}) collective-permute-start(f32[32,8,128]{2,1,0:T(8,128)S(1)} %pad_maximum_fusion.own_pack_ref), channel_id=1, source_target_pairs={{1,2},{2,1},{3,4},{4,3},{5,6},{6,5},{7,8},{8,7},{9,10},{10,9},{11,... | collective-permute-start | bytes 393224 | tf_op jit(solution)/shard_map/ppermute | solution.py:621
  25.8 4.8 %collective-permute-start.4 = (f32[32,8,128]{2,1,0:T(8,128)S(1)}, f32[32,8,128]{2,1,0:T(8,128)S(1)}, u32[]{:S(2)}, u32[]{:S(2)}) collective-permute-start(f32[32,8,128]{2,1,0:T(8,128)S(1)} %pad_maximum_fusion.own_pack_ref), channel_id=1, source_target_pairs={{0,1},{1,0},{2,3},{3,2},{4,5},{5,4},{6,7},{7,6},{8,9},{9,8},{10,11... | collective-permute-start | bytes 393224 | tf_op jit(solution)/shard_map/ppermute | solution.py:622
  25.9 4.8 %copy-start.1 = (f32[6,8,128]{2,1,0:T(8,128)S(1)}, f32[6,8,128]{2,1,0:T(8,128)}, u32[]{:S(2)}) copy-start(f32[6,8,128]{2,1,0:T(8,128)} %get-tuple-element.14.table_ref) | copy-start | bytes 73732

commit v9 on v7

--- a/solution.py
+++ b/solution.py
@@ -86,7 +86,7 @@
 
 
 def strip_kernel(
-    rhs_in, mat_in, diag_in, off_in, strip_ref, cells_ref, table_ref, own_ref,
+    rhs_in, mat_in, diag_in, off_in, strip_ref, table_ref, own_ref,
     rhs_ref, mat_ref, diag_ref, off_ref, arrived,
 ):
     pairs = ((mat_in, mat_ref), (rhs_in, rhs_ref), (diag_in, diag_ref), (off_in, off_ref))
@@ -110,8 +110,6 @@
 
     for z in range(2):
         cells = [mat_ref[depth_rows(r, z), :].astype(jnp.float32) for r in range(SUBS)]
-        for r in range(SUBS):
-            cells_ref[2 * r + z] = cells[r]
         strip_ref[12 + z] = packed(cells, half)
         strip_ref[14 + z] = packed(cells, 0)
         for c in range(6):
@@ -321,15 +319,18 @@
         ninth = pltpu.roll(beyond_strip, lax.rem(LANES - STRIP * r, LANES), 1)
         return jnp.where(lane == STRIP // 2, ninth, spread(strip, r))
 
+    def strip(group, k):
+        return packs[group, pl.ds(SUBS * k, SUBS), :]
+
     def unpack(group):
         def body(y):
             r = y - group * SUBS
             for z in range(2):
                 for c in range(6):
                     v[y, c, 2 * z] = bulk[group, c, depth_rows(r, z), :]
-                    v[y, c, 2 * z + 1] = spread(packs[group, 2 * c + z], r)
-                mat[y, 2 * z] = packs[group, 16 + 2 * r + z]
-                mat[y, 2 * z + 1] = cell_halo(packs[group, 12 + z], packs[group, 14 + z], r)
+                    v[y, c, 2 * z + 1] = spread(strip(group, 2 * c + z), r)
+                mat[y, 2 * z] = packs[group, depth_rows(r, 2 + z), :]
+                mat[y, 2 * z + 1] = cell_halo(strip(group, 12 + z), strip(group, 14 + z), r)
 
         return (body, group * SUBS, group * SUBS + SUBS, 0)
 
@@ -582,7 +583,7 @@
 def strip_call():
     return call(
         strip_kernel,
-        [((16,) + TILE, VMEM), ((16,) + TILE, VMEM), ((6,) + TILE, VMEM), (BLOCK, ANY)],
+        [((16,) + TILE, VMEM), ((6,) + TILE, VMEM), (BLOCK, ANY)],
         [ANY] * 4,
         floats(BLOCK) + [((LANES, LANES), jnp.int32)] + floats((3, SUBS), (3, SUBS)),
         (5,),
@@ -599,7 +600,7 @@
         + [((ROWS + 1, 4) + TILE, jnp.int32)]
         + floats(rows(6, 1), rows(6), rows(8), *[rows(6)] * 3, rows(8, 1), rows(4, 1))
         + floats((ROWS, 6, 2) + TILE, (ROWS, 6, 2) + TILE)
-        + floats((3,) + BLOCK, (3, PACK) + TILE, (6,) + TILE, (6,) + TILE),
+        + floats((3,) + BLOCK, (3, SUBS * PACK, LANES), (6,) + TILE, (6,) + TILE),
         (8, 2),
     )
 
@@ -625,16 +626,19 @@
 def on_device(right_side, materials, sigma_diag, sigma_off):
     rhs = right_side.reshape(BLOCK)
     bulk = swapped(rhs, "gy")
-    strips, cells, table, own = strip_call()(
+    strips, table, own = strip_call()(
         rhs, materials.reshape(LANES, LANES), sigma_diag, sigma_off
     )
     first, second = swapped(strips, "gx")
     odd = lax.axis_index("gx") % 2 == 1
     lane = lax.broadcasted_iota(jnp.int32, (14,) + TILE, 2)
     mixed = jnp.where((lane % STRIP < STRIP // 2) == odd, first[:14], second[:14])
-    pack = jnp.concatenate([mixed, jnp.where(odd, second[14:], first[14:]), cells])
+    beyond = jnp.where(odd, second[14:], first[14:])
+    pack = jnp.concatenate([mixed, beyond, materials.astype(jnp.float32)])
+    pack = pack.reshape(SUBS * PACK, LANES)
     packs = swapped(pack, "gy")
-    last = moved(pack[12:18], "gy", -2)
+    first_row = materials[:, 0, :].astype(jnp.float32).reshape((2,) + TILE)
+    last = moved(jnp.concatenate([mixed[12:], beyond, first_row]), "gy", -2)
     a0, a1, sums = main_call()(
         lax.axis_index("gy").reshape(1) % 2, own, *bulk, pack, *packs, last, table
     )

time: 62.5 us -> 61.6 us (0.986)
  other arithmetic: 0.87 us -> 0.05 us
    concatenate x1, other arithmetic: 0.85 us -> 0.01 us  [on_device(): last = moved(jnp.concatenate([mixed[12:], beyond, first_row]), 'gy', -2)]
  transfers between devices with their start and end apart: 7 -> 7, of which waited for: 4 -> 4; matrix products, arithmetic and copies ran while one was open for 1% -> 0% of each run, Pallas kernels for 4% -> 4%
where the time goes in v9:
time: 61.6 us; the launch traced here: 61.4 us
  Pallas kernels  21.8 us (35%)
  blocking collectives  20.5 us (33%)
  starting transfers between devices  16.1 us (26%)
  waiting for transfers between devices  2.23 us (4%)
  between operations  0.74 us (1%)
    all_to_all x1, blocking collectives, on_device(): gathered = lax.all_to_all(sums, ('gx', 'gy'), 0, 0, tiled=True)  20.5 us
    pallas_call x1, Pallas kernels, on_device(): main_call()  17.3 us
    ppermute x3, starting transfers between devices, swapped(): second = lax.ppermute(value, axis, others)  9.28 us
    ppermute x1, starting transfers between devices, moved(): lax.ppermute(value, axis, [(i, (i + step) % size) for i in range(size)])  4.41 us
    pallas_call x1, Pallas kernels, on_device(): strip_call()(rhs, materials.reshape(LANES, LANES), sigma_diag, sigma_off)  2.5 us
    ppermute x3, starting transfers between devices, swapped(): return (lax.ppermute(value, axis, pairs), second)  2.43 us
    pallas_call x1, Pallas kernels, on_device(): result, hessenberg = final_call()(gathered, a0, a1)  2.07 us
  transfers between devices with their start and end apart: 7, of which 4 were waited for; matrix products, arithmetic and copies ran while one was open for 0% of the time, Pallas kernels for 4%

profile of v9, /device:TPU:1, one launch (start us, length us, event | category | flops | bytes accessed | tf_op | source)
XLA Modules:
  0.0 61.4 jit_solution(2346904722844538345)
XLA Ops:
  0.6 5.8 %collective-permute-start.1 = (f32[6,128,128]{2,1,0:T(8,128)}, f32[6,128,128]{2,1,0:T(8,128)S(1)}, u32[]{:S(2)}, u32[]{:S(2)}) collective-permute-start(f32[6,128,128]{2,1,0:T(8,128)} %bitcast.14), channel_id=1, source_target_pairs={{1,2},{2,1},{3,4},{4,3},{5,6},{6,5},{7,8},{8,7},{9,10},{10,9},{11,... | collective-permute-start | bytes 1179656 | tf_op jit(solution)/shard_map/ppermute | solution.py:622
  6.5 0.0 collective-permute-start
  6.5 0.0 copy-start.2
  6.5 2.5 %shard_map.59 = (f32[16,8,128]{2,1,0:T(8,128)}, f32[6,8,128]{2,1,0:T(8,128)}, f32[6,128,128]{2,1,0:T(8,128)}) custom-call(f32[6,128,128]{2,1,0:T(8,128)} %bitcast.16, s32[128,128]{1,0:T(8,128)} %bitcast.17, f32[3,8]{1,0:T(4,128)} %diag_in.1, f32[3,8]{1,0:T(4,128)} %off_in.1), custom_call_target="tpu_custom_call" | custom-call | tf_op jit(solution)/shard_map/pallas_call | solution.py:629
  9.0 0.0 copy-start
  9.0 2.6 %collective-permute-start.3 = (f32[16,8,128]{2,1,0:T(8,128)}, f32[16,8,128]{2,1,0:T(8,128)S(1)}, u32[]{:S(2)}, u32[]{:S(2)}) collective-permute-start(f32[16,8,128]{2,1,0:T(8,128)} %get-tuple-element.11), channel_id=1, source_target_pairs={{16,32},{32,16},{48,64},{64,48},{80,96},{96,80},{112,0},{0,112},{1... | collective-permute-start | bytes 196616 | tf_op jit(solution)/shard_map/ppermute | solution.py:622
  11.6 1.7 %collective-permute-start.2 = (f32[16,8,128]{2,1,0:T(8,128)}, f32[16,8,128]{2,1,0:T(8,128)S(1)}, u32[]{:S(2)}, u32[]{:S(2)}) collective-permute-start(f32[16,8,128]{2,1,0:T(8,128)} %get-tuple-element.11), channel_id=1, source_target_pairs={{0,16},{16,0},{32,48},{48,32},{64,80},{80,64},{96,112},{112,96},{1... | collective-permute-start | bytes 196616 | tf_op jit(solution)/shard_map/ppermute | solution.py:623
  13.2 0.0 copy-done.2
  13.3 0.7 %collective-permute-done.3 = f32[16,8,128]{2,1,0:T(8,128)S(1)} collective-permute-done((f32[16,8,128]{2,1,0:T(8,128)}, f32[16,8,128]{2,1,0:T(8,128)S(1)}, u32[]{:S(2)}, u32[]{:S(2)}) %collective-permute-start.3) | collective-permute-done | bytes 65568 | tf_op jit(solution)/shard_map/ppermute | solution.py:622
  14.0 0.3 collective-permute-done.2
  14.4 0.9 %collective-permute-start.5 = (f32[256,128]{1,0:T(8,128)S(1)}, f32[256,128]{1,0:T(8,128)S(1)}, u32[]{:S(2)}, u32[]{:S(2)}) collective-permute-start(f32[256,128]{1,0:T(8,128)S(1)} %maximum_bitcast_fusion.own_pack_ref), channel_id=1, source_target_pairs={{1,2},{2,1},{3,4},{4,3},{5,6},{6,5},{7,8},{8,7},{9,10},{10,9},{11,... | collective-permute-start | bytes 393224 | tf_op jit(solution)/shard_map/ppermute | solution.py:622
  15.3 0.8 %collective-permute-start.4 = (f32[256,128]{1,0:T(8,128)S(1)}, f32[256,128]{1,0:T(8,128)S(1)}, u32[]{:S(2)}, u32[]{:S(2)}) collective-permute-start(f32[256,128]{1,0:T(8,128)S(1)} %maximum_bitcast_fusion.own_pack_ref), channel_id=1, source_target_pairs={{0,1},{1,0},{2,3},{3,2},{4,5},{5,4},{6,7},{7,6},{8,9},{9,8},{10,11... | collective-permute-start | bytes 393224 | tf_op jit(solution)/shard_map/ppermute | solution.py:623
  16.0 0.0 copy-start.1
  16.0 4.4 %collective-permute-start.6 = (f32[6,8,128]{2,1,0:T(8,128)S(1)}, f32[6,8,128]{2,1,0:T(8,128)S(1)}, u32[]{:S(2)}, u32[]{:S(2)}) collective-permute-start(f32[6,8,128]{2,1,0:T(8,128)S(1)} %pad_maximum_fusion), channel_id=1, source_target_pairs={{0,14},{1,15},{2,0},{3,1},{4,2},{5,3},{6,4},{7,5},{8,6},{9,7},{10,... | collective-permute-start | bytes 73736 | tf_op jit(solution)/shard_map/ppermute | solution.py:567
  20.4 0.9 %collective-permute-done.6.last_ref = f32[6,8,128]{2,1,0:T(8,128)S(1)} collective-permute-done((f32[6,8,128]{2,1,0:T(8,128)S(1)}, f32[6,8,128]{2,1,0:T(8,128)S(1)}, u32[]{:S(2)}, u32[]{:S(2)}) %collective-permute-start.6) | collective-permute-done | bytes 24608 | tf_op jit(solution)/shard_map/ppermute | solution.py:567
  21.4 0.2 collective-permute-done.5.second_pack_ref
  21.6 0.0 collective-permute-done.4.first_pack_ref
  21.6 0.0 collective-permute-done.1.second_ref
  21.6 0.0 collective-permute-done.first_ref
  21.6 0.0 copy-done
  21.6 0.0 copy-done.1
  21.6 17.3 %shard_map.60 = (f32[8,6,2,8,128]{4,3,2,1,0:T(8,128)S(1)}, f32[8,6,2,8,128]{4,3,2,1,0:T(8,128)S(1)}, f32[128,128]{1,0:T(8,128)S(1)}) custom-call(s32[1]{0:T(128)S(6)} %select_n.31.odd_ref, f32[6,128,128]{2,1,0:T(8,128)S(1)} %copy-done, f32[6,128,128]{2,1,0:T(8,128)S(1)} %collective-permute-done.first_ref, ...), custom_call_target="tpu_custom_call" | custom-call | tf_op jit(solution)/shard_map/pallas_call | solution.py:642
  38.9 20.5 %all_to_all.11 = f32[128,1,128]{2,1,0:T(1,128)S(1)} all-to-all(f32[128,1,128]{2,1,0:T(1,128)S(1)} %bitcast.13), channel_id=1, replica_groups=mesh['gx'=8,'gy'=16] {'gx','gy'}, dimensions={0} | all-to-all | bytes 131072 | tf_op jit(solution)/shard_map/all_to_all | solution.py:645
  59.4 2.1 %shard_map.61 = (f32[6,128,128]{2,1,0:T(8,128)}, f32[2,3]{1,0:T(2,128)}) custom-call(f32[128,128]{1,0:T(8,128)S(1)} %bitcast.12, f32[8,6,2,8,128]{4,3,2,1,0:T(8,128)S(1)} %get-tuple-element.14.a0_ref, f32[8,6,2,8,128]{4,3,2,1,0:T(8,128)S(1)} %get-tuple-element.15.a1_ref), custom_call_target="tpu_custom_call" | custom-call | tf_op jit(solution)/shard_map/pallas_call | solution.py:646
  (9 shorter events, 0.1 us)
Async XLA Ops:
  0.6 21.0 %collective-permute-start.1 = (f32[6,128,128]{2,1,0:T(8,128)}, f32[6,128,128]{2,1,0:T(8,128)S(1)}, u32[]{:S(2)}, u32[]{:S(2)}) collective-permute-start(f32[6,128,128]{2,1,0:T(8,128)} %bitcast.14), channel_id=1, source_target_pairs={{1,2},{2,1},{3,4},{4,3},{5,6},{6,5},{7,8},{8,7},{9,10},{10,9},{11,... | collective-permute-start | bytes 1179656 | tf_op jit(solution)/shard_map/ppermute | solution.py:622
  6.5 15.2 %collective-permute-start = (f32[6,128,128]{2,1,0:T(8,128)}, f32[6,128,128]{2,1,0:T(8,128)S(1)}, u32[]{:S(2)}, u32[]{:S(2)}) collective-permute-start(f32[6,128,128]{2,1,0:T(8,128)} %bitcast.15), channel_id=1, source_target_pairs={{0,1},{1,0},{2,3},{3,2},{4,5},{5,4},{6,7},{7,6},{8,9},{9,8},{10,11... | collective-permute-start | bytes 1179656 | tf_op jit(solution)/shard_map/ppermute | solution.py:623
  6.5 6.8 %copy-start.2 = (s32[16,8,128]{2,1,0:T(8,128)S(1)}, s32[16,8,128]{2,1,0:T(8,128)}, u32[]{:S(2)}) copy-start(s32[16,8,128]{2,1,0:T(8,128)} %param.5) | copy-start | bytes 196612
  9.0 12.6 %copy-start = (f32[6,128,128]{2,1,0:T(8,128)S(1)}, f32[6,128,128]{2,1,0:T(8,128)}, u32[]{:S(2)}) copy-start(f32[6,128,128]{2,1,0:T(8,128)} %get-tuple-element.10.own_ref) | copy-start | bytes 1179652
  9.0 5.0 %collective-permute-start.3 = (f32[16,8,128]{2,1,0:T(8,128)}, f32[16,8,128]{2,1,0:T(8,128)S(1)}, u32[]{:S(2)}, u32[]{:S(2)}) collective-permute-start(f32[16,8,128]{2,1,0:T(8,128)} %get-tuple-element.11), channel_id=1, source_target_pairs={{16,32},{32,16},{48,64},{64,48},{80,96},{96,80},{112,0},{0,112},{1... | collective-permute-start | bytes 196616 | tf_op jit(solution)/shard_map/ppermute | solution.py:622
  11.6 2.8 %collective-permute-start.2 = (f32[16,8,128]{2,1,0:T(8,128)}, f32[16,8,128]{2,1,0:T(8,128)S(1)}, u32[]{:S(2)}, u32[]{:S(2)}) collective-permute-start(f32[16,8,128]{2,1,0:T(8,128)} %get-tuple-element.11), channel_id=1, source_target_pairs={{0,16},{16,0},{32,48},{48,32},{64,80},{80,64},{96,112},{112,96},{1... | collective-permute-start | bytes 196616 | tf_op jit(solution)/shard_map/ppermute | solution.py:623
  14.4 7.2 %collective-permute-start.5 = (f32[256,128]{1,0:T(8,128)S(1)}, f32[256,128]{1,0:T(8,128)S(1)}, u32[]{:S(2)}, u32[]{:S(2)}) collective-permute-start(f32[256,128]{1,0:T(8,128)S(1)} %maximum_bitcast_fusion.own_pack_ref), channel_id=1, source_target_pairs={{1,2},{2,1},{3,4},{4,3},{5,6},{6,5},{7,8},{8,7},{9,10},{10,9},{11,... | collective-permute-start | bytes 393224 | tf_op jit(solution)/shard_map/ppermute | solution.py:622
  15.3 6.3 %collective-permute-start.4 = (f32[256,128]{1,0:T(8,128)S(1)}, f32[256,128]{1,0:T(8,128)S(1)}, u32[]{:S(2)}, u32[]{:S(2)}) collective-permute-start(f32[256,128]{1,0:T(8,128)S(1)} %maximum_bitcast_fusion.own_pack_ref), channel_id=1, source_target_pairs={{0,1},{1,0},{2,3},{3,2},{4,5},{5,4},{6,7},{7,6},{8,9},{9,8},{10,11... | collective-permute-start | bytes 393224 | tf_op jit(solution)/shard_map/ppermute | solution.py:623
  16.0 5.6 %copy-start.1 = (f32[6,8,128]{2,1,0:T(8,128)S(1)}, f32[6,8,128]{2,1,0:T(8,128)}, u32[]{:S(2)}) copy-start(f32[6,8,128]{2,1,0:T(8,128)} %get-tuple-element.12.table_ref) | copy-start | bytes 73732
  16.0 5.4 %collective-permute-start.6 = (f32[6,8,128]{2,1,0:T(8,128)S(1)}, f32[6,8,128]{2,1,0:T(8,128)S(1)}, u32[]{:S(2)}, u32[]{:S(2)}) collective-permute-start(f32[6,8,128]{2,1,0:T(8,128)S(1)} %pad_maximum_fusion), channel_id=1, source_target_pairs={{0,14},{1,15},{2,0},{3,1},{4,2},{5,3},{6,4},{7,5},{8,6},{9,7},{10,... | collective-permute-start | bytes 73736 | tf_op jit(solution)/shard_map/ppermute | solution.py:567

commit v10 on v9

--- a/solution.py
+++ b/solution.py
@@ -91,12 +91,11 @@
 ):
     pairs = ((mat_in, mat_ref), (rhs_in, rhs_ref), (diag_in, diag_ref), (off_in, off_ref))
     copies = [pltpu.make_async_copy(f, t, arrived.at[k]) for k, (f, t) in enumerate(pairs)]
-    for copy in copies:
+    own_copy = pltpu.make_async_copy(rhs_in, own_ref, arrived.at[4])
+    for copy in copies + [own_copy]:
         copy.start()
     for copy in copies:
         copy.wait()
-    own_copy = pltpu.make_async_copy(rhs_ref, own_ref, arrived.at[4])
-    own_copy.start()
     lane = lax.broadcasted_iota(jnp.int32, (SUBS, LANES), 1)
     half = STRIP // 2
 

time: 61.6 us -> 72.8 us (1.18)
  Pallas kernels: 21.8 us -> 33 us
    pallas_call x1, Pallas kernels: 2.5 us -> 13.7 us  [on_device(): strip_call()(rhs, materials.reshape(LANES, LANES), sigma_diag, sigma_off)]
  transfers between devices with their start and end apart: 7 -> 7, of which waited for: 4 -> 4; matrix products, arithmetic and copies ran while one was open for 0% -> 0% of each run, Pallas kernels for 4% -> 19%
where the time goes in v10:
time: 72.8 us; the launch traced here: 72.6 us
  Pallas kernels  33 us (45%)
  blocking collectives  20.5 us (28%)
  starting transfers between devices  16.1 us (22%)
  waiting for transfers between devices  2.23 us (3%)
  between operations  0.74 us (1%)
    all_to_all x1, blocking collectives, on_device(): gathered = lax.all_to_all(sums, ('gx', 'gy'), 0, 0, tiled=True)  20.5 us
    pallas_call x1, Pallas kernels, on_device(): main_call()  17.3 us
    pallas_call x1, Pallas kernels, on_device(): strip_call()(rhs, materials.reshape(LANES, LANES), sigma_diag, sigma_off)  13.7 us
    ppermute x3, starting transfers between devices, swapped(): second = lax.ppermute(value, axis, others)  9.27 us
    ppermute x1, starting transfers between devices, moved(): lax.ppermute(value, axis, [(i, (i + step) % size) for i in range(size)])  4.41 us
    ppermute x3, starting transfers between devices, swapped(): return (lax.ppermute(value, axis, pairs), second)  2.43 us
    pallas_call x1, Pallas kernels, on_device(): result, hessenberg = final_call()(gathered, a0, a1)  2.07 us
  transfers between devices with their start and end apart: 7, of which 4 were waited for; matrix products, arithmetic and copies ran while one was open for 0% of the time, Pallas kernels for 19%

profile of v10, /device:TPU:1, one launch (start us, length us, event | category | flops | bytes accessed | tf_op | source)
XLA Modules:
  0.0 72.6 jit_solution(4030984973820713525)
XLA Ops:
  0.6 5.8 %collective-permute-start.1 = (f32[6,128,128]{2,1,0:T(8,128)}, f32[6,128,128]{2,1,0:T(8,128)S(1)}, u32[]{:S(2)}, u32[]{:S(2)}) collective-permute-start(f32[6,128,128]{2,1,0:T(8,128)} %bitcast.14), channel_id=1, source_target_pairs={{1,2},{2,1},{3,4},{4,3},{5,6},{6,5},{7,8},{8,7},{9,10},{10,9},{11,... | collective-permute-start | bytes 1179656 | tf_op jit(solution)/shard_map/ppermute | solution.py:621
  6.5 0.0 collective-permute-start
  6.5 0.0 copy-start.2
  6.5 13.7 %shard_map.59 = (f32[16,8,128]{2,1,0:T(8,128)}, f32[6,8,128]{2,1,0:T(8,128)}, f32[6,128,128]{2,1,0:T(8,128)}) custom-call(f32[6,128,128]{2,1,0:T(8,128)} %bitcast.16, s32[128,128]{1,0:T(8,128)} %bitcast.17, f32[3,8]{1,0:T(4,128)} %diag_in.1, f32[3,8]{1,0:T(4,128)} %off_in.1), custom_call_target="tpu_custom_call" | custom-call | tf_op jit(solution)/shard_map/pallas_call | solution.py:628
  20.2 0.0 copy-start
  20.2 2.6 %collective-permute-start.3 = (f32[16,8,128]{2,1,0:T(8,128)}, f32[16,8,128]{2,1,0:T(8,128)S(1)}, u32[]{:S(2)}, u32[]{:S(2)}) collective-permute-start(f32[16,8,128]{2,1,0:T(8,128)} %get-tuple-element.11), channel_id=1, source_target_pairs={{16,32},{32,16},{48,64},{64,48},{80,96},{96,80},{112,0},{0,112},{1... | collective-permute-start | bytes 196616 | tf_op jit(solution)/shard_map/ppermute | solution.py:621
  22.7 1.7 %collective-permute-start.2 = (f32[16,8,128]{2,1,0:T(8,128)}, f32[16,8,128]{2,1,0:T(8,128)S(1)}, u32[]{:S(2)}, u32[]{:S(2)}) collective-permute-start(f32[16,8,128]{2,1,0:T(8,128)} %get-tuple-element.11), channel_id=1, source_target_pairs={{0,16},{16,0},{32,48},{48,32},{64,80},{80,64},{96,112},{112,96},{1... | collective-permute-start | bytes 196616 | tf_op jit(solution)/shard_map/ppermute | solution.py:622
  24.4 0.0 copy-done.2
  24.5 0.4 collective-permute-done.3
  24.9 0.6 collective-permute-done.2
  25.6 0.9 %collective-permute-start.5 = (f32[256,128]{1,0:T(8,128)S(1)}, f32[256,128]{1,0:T(8,128)S(1)}, u32[]{:S(2)}, u32[]{:S(2)}) collective-permute-start(f32[256,128]{1,0:T(8,128)S(1)} %maximum_bitcast_fusion.own_pack_ref), channel_id=1, source_target_pairs={{1,2},{2,1},{3,4},{4,3},{5,6},{6,5},{7,8},{8,7},{9,10},{10,9},{11,... | collective-permute-start | bytes 393224 | tf_op jit(solution)/shard_map/ppermute | solution.py:621
  26.5 0.8 %collective-permute-start.4 = (f32[256,128]{1,0:T(8,128)S(1)}, f32[256,128]{1,0:T(8,128)S(1)}, u32[]{:S(2)}, u32[]{:S(2)}) collective-permute-start(f32[256,128]{1,0:T(8,128)S(1)} %maximum_bitcast_fusion.own_pack_ref), channel_id=1, source_target_pairs={{0,1},{1,0},{2,3},{3,2},{4,5},{5,4},{6,7},{7,6},{8,9},{9,8},{10,11... | collective-permute-start | bytes 393224 | tf_op jit(solution)/shard_map/ppermute | solution.py:622
  27.2 0.0 copy-start.1
  27.2 4.4 %collective-permute-start.6 = (f32[6,8,128]{2,1,0:T(8,128)S(1)}, f32[6,8,128]{2,1,0:T(8,128)S(1)}, u32[]{:S(2)}, u32[]{:S(2)}) collective-permute-start(f32[6,8,128]{2,1,0:T(8,128)S(1)} %pad_maximum_fusion), channel_id=1, source_target_pairs={{0,14},{1,15},{2,0},{3,1},{4,2},{5,3},{6,4},{7,5},{8,6},{9,7},{10,... | collective-permute-start | bytes 73736 | tf_op jit(solution)/shard_map/ppermute | solution.py:566
  31.6 0.9 %collective-permute-done.6.last_ref = f32[6,8,128]{2,1,0:T(8,128)S(1)} collective-permute-done((f32[6,8,128]{2,1,0:T(8,128)S(1)}, f32[6,8,128]{2,1,0:T(8,128)S(1)}, u32[]{:S(2)}, u32[]{:S(2)}) %collective-permute-start.6) | collective-permute-done | bytes 24608 | tf_op jit(solution)/shard_map/ppermute | solution.py:566
  32.6 0.2 collective-permute-done.5.second_pack_ref
  32.8 0.0 collective-permute-done.4.first_pack_ref
  32.8 0.0 collective-permute-done.1.second_ref
  32.8 0.0 collective-permute-done.first_ref
  32.8 0.0 copy-done
  32.8 0.0 copy-done.1
  32.8 17.3 %shard_map.60 = (f32[8,6,2,8,128]{4,3,2,1,0:T(8,128)S(1)}, f32[8,6,2,8,128]{4,3,2,1,0:T(8,128)S(1)}, f32[128,128]{1,0:T(8,128)S(1)}) custom-call(s32[1]{0:T(128)S(6)} %select_n.31.odd_ref, f32[6,128,128]{2,1,0:T(8,128)S(1)} %copy-done, f32[6,128,128]{2,1,0:T(8,128)S(1)} %collective-permute-done.first_ref, ...), custom_call_target="tpu_custom_call" | custom-call | tf_op jit(solution)/shard_map/pallas_call | solution.py:641
  50.1 20.5 %all_to_all.11 = f32[128,1,128]{2,1,0:T(1,128)S(1)} all-to-all(f32[128,1,128]{2,1,0:T(1,128)S(1)} %bitcast.13), channel_id=1, replica_groups=mesh['gx'=8,'gy'=16] {'gx','gy'}, dimensions={0} | all-to-all | bytes 131072 | tf_op jit(solution)/shard_map/all_to_all | solution.py:644
  70.5 2.1 %shard_map.61 = (f32[6,128,128]{2,1,0:T(8,128)}, f32[2,3]{1,0:T(2,128)}) custom-call(f32[128,128]{1,0:T(8,128)S(1)} %bitcast.12, f32[8,6,2,8,128]{4,3,2,1,0:T(8,128)S(1)} %get-tuple-element.14.a0_ref, f32[8,6,2,8,128]{4,3,2,1,0:T(8,128)S(1)} %get-tuple-element.15.a1_ref), custom_call_target="tpu_custom_call" | custom-call | tf_op jit(solution)/shard_map/pallas_call | solution.py:645
  (9 shorter events, 0.1 us)
Async XLA Ops:
  0.6 32.2 %collective-permute-start.1 = (f32[6,128,128]{2,1,0:T(8,128)}, f32[6,128,128]{2,1,0:T(8,128)S(1)}, u32[]{:S(2)}, u32[]{:S(2)}) collective-permute-start(f32[6,128,128]{2,1,0:T(8,128)} %bitcast.14), channel_id=1, source_target_pairs={{1,2},{2,1},{3,4},{4,3},{5,6},{6,5},{7,8},{8,7},{9,10},{10,9},{11,... | collective-permute-start | bytes 1179656 | tf_op jit(solution)/shard_map/ppermute | solution.py:621
  6.5 26.3 %collective-permute-start = (f32[6,128,128]{2,1,0:T(8,128)}, f32[6,128,128]{2,1,0:T(8,128)S(1)}, u32[]{:S(2)}, u32[]{:S(2)}) collective-permute-start(f32[6,128,128]{2,1,0:T(8,128)} %bitcast.15), channel_id=1, source_target_pairs={{0,1},{1,0},{2,3},{3,2},{4,5},{5,4},{6,7},{7,6},{8,9},{9,8},{10,11... | collective-permute-start | bytes 1179656 | tf_op jit(solution)/shard_map/ppermute | solution.py:622
  6.5 17.9 %copy-start.2 = (s32[16,8,128]{2,1,0:T(8,128)S(1)}, s32[16,8,128]{2,1,0:T(8,128)}, u32[]{:S(2)}) copy-start(s32[16,8,128]{2,1,0:T(8,128)} %param.5) | copy-start | bytes 196612
  20.2 12.6 %copy-start = (f32[6,128,128]{2,1,0:T(8,128)S(1)}, f32[6,128,128]{2,1,0:T(8,128)}, u32[]{:S(2)}) copy-start(f32[6,128,128]{2,1,0:T(8,128)} %get-tuple-element.10.own_ref) | copy-start | bytes 1179652
  20.2 4.7 %collective-permute-start.3 = (f32[16,8,128]{2,1,0:T(8,128)}, f32[16,8,128]{2,1,0:T(8,128)S(1)}, u32[]{:S(2)}, u32[]{:S(2)}) collective-permute-start(f32[16,8,128]{2,1,0:T(8,128)} %get-tuple-element.11), channel_id=1, source_target_pairs={{16,32},{32,16},{48,64},{64,48},{80,96},{96,80},{112,0},{0,112},{1... | collective-permute-start | bytes 196616 | tf_op jit(solution)/shard_map/ppermute | solution.py:621
  22.7 2.8 %collective-permute-start.2 = (f32[16,8,128]{2,1,0:T(8,128)}, f32[16,8,128]{2,1,0:T(8,128)S(1)}, u32[]{:S(2)}, u32[]{:S(2)}) collective-permute-start(f32[16,8,128]{2,1,0:T(8,128)} %get-tuple-element.11), channel_id=1, source_target_pairs={{0,16},{16,0},{32,48},{48,32},{64,80},{80,64},{96,112},{112,96},{1... | collective-permute-start | bytes 196616 | tf_op jit(solution)/shard_map/ppermute | solution.py:622
  25.6 7.2 %collective-permute-start.5 = (f32[256,128]{1,0:T(8,128)S(1)}, f32[256,128]{1,0:T(8,128)S(1)}, u32[]{:S(2)}, u32[]{:S(2)}) collective-permute-start(f32[256,128]{1,0:T(8,128)S(1)} %maximum_bitcast_fusion.own_pack_ref), channel_id=1, source_target_pairs={{1,2},{2,1},{3,4},{4,3},{5,6},{6,5},{7,8},{8,7},{9,10},{10,9},{11,... | collective-permute-start | bytes 393224 | tf_op jit(solution)/shard_map/ppermute | solution.py:621
  26.5 6.3 %collective-permute-start.4 = (f32[256,128]{1,0:T(8,128)S(1)}, f32[256,128]{1,0:T(8,128)S(1)}, u32[]{:S(2)}, u32[]{:S(2)}) collective-permute-start(f32[256,128]{1,0:T(8,128)S(1)} %maximum_bitcast_fusion.own_pack_ref), channel_id=1, source_target_pairs={{0,1},{1,0},{2,3},{3,2},{4,5},{5,4},{6,7},{7,6},{8,9},{9,8},{10,11... | collective-permute-start | bytes 393224 | tf_op jit(solution)/shard_map/ppermute | solution.py:622
  27.2 5.6 %copy-start.1 = (f32[6,8,128]{2,1,0:T(8,128)S(1)}, f32[6,8,128]{2,1,0:T(8,128)}, u32[]{:S(2)}) copy-start(f32[6,8,128]{2,1,0:T(8,128)} %get-tuple-element.12.table_ref) | copy-start | bytes 73732
  27.2 5.4 %collective-permute-start.6 = (f32[6,8,128]{2,1,0:T(8,128)S(1)}, f32[6,8,128]{2,1,0:T(8,128)S(1)}, u32[]{:S(2)}, u32[]{:S(2)}) collective-permute-start(f32[6,8,128]{2,1,0:T(8,128)S(1)} %pad_maximum_fusion), channel_id=1, source_target_pairs={{0,14},{1,15},{2,0},{3,1},{4,2},{5,3},{6,4},{7,5},{8,6},{9,7},{10,... | collective-permute-start | bytes 73736 | tf_op jit(solution)/shard_map/ppermute | solution.py:566
